TPU v7x, 32 devices: a whole 2x2x4 slice. The times are simulated.
32 devices in a mesh: req: 8 (over z, y), grp: 4 (over x, core).
Axes of the slice: x: 2, y: 2, z: 4, core: 2. Of those that a mesh axis runs over, the one named last changes fastest.
Arguments:
- hidden_in: bfloat16 [4096, 2048], P('req'), may hold values from -6 to 6
- attn_gain: float32 [2048], replicated, may hold values from 0.1 to 1.9
- mlp_gain: float32 [2048], replicated, may hold values from 0.1 to 1.9
- w_query: bfloat16 [2048, 2048], P(None, 'grp'), may hold values from -0.75 to 0.75
- w_key: bfloat16 [2048, 512], P(None, 'grp'), may hold values from -0.125 to 0.125
- w_value: bfloat16 [2048, 512], P(None, 'grp'), may hold values from -0.125 to 0.125
- w_out: bfloat16 [2048, 2048], P('grp'), may hold values from -0.125 to 0.125
- w_gate: bfloat16 [2048, 8192], P(None, 'req'), may hold values from -0.125 to 0.125
- w_up: bfloat16 [2048, 8192], P(None, 'req'), may hold values from -0.125 to 0.125
- w_down: bfloat16 [8192, 2048], P('req'), may hold values from -0.0625 to 0.0625
- cache_k: bfloat16 [1024, 16, 512], P('req', None, 'grp'), may hold values from -4000 to 4000
- cache_v: bfloat16 [1024, 16, 512], P('req', None, 'grp'), may hold values from -6 to 6
- owner_of_row: int32 [4096], P('req'), may hold values from 0 to 7, as said below
- new_len: int32 [8, 8], P('req'), may hold values from 0 to 128, as said below
- prior_len: int32 [8, 8], P('req'), may hold values from 0 to 256, as said below
- page_table: int32 [8, 128], P('req'), may hold values from 0 to 127, each once within a row
Outputs:
- layer_out: bfloat16 [4096, 2048], P(('req', 'grp'))
- new_cache_k: bfloat16 [1024, 16, 512], P('req', None, 'grp')
- new_cache_v: bfloat16 [1024, 16, 512], P('req', None, 'grp')
Inputs may be any that keep to these rules, and one draw needn't show every extreme that they name: `owner_of_row`: rows of one block of 512 that name the same owner are consecutive; each block holds at most one request for each owner, of at most 128 rows; in every draw one owner receives a request of exactly 128 rows from every block. new_len[o, s] is the number of rows of block s of owner_of_row that name o. prior_len[o, s] + new_len[o, s] <= 256.
All inputs are finite; a program needn't handle non-finite values.
Results may differ from a plain program's by a relative error of at most 0.0063.
Values may be sent and summed in bfloat16 or wider, within the bound.
No kernel may reach another device: no remote copies, remote signals or barrier semaphores. Data moves between devices by JAX's collectives and lax.ppermute only.
A program may use at most 128 MiB of HBM per device.

v0:
```python
import jax
import jax.numpy as jnp
from jax import lax
from jax.sharding import PartitionSpec as P

HD = 64
PAGE = 16
MAXP = 16
CONTEXT = 256


EPSILON = 1e-05
RESIDUAL_MULT = 0.22
SCORE_MULT = 0.015625
ROPE_BASE = 10000000.0


def normalize(values, gain):
    mean_square = jnp.mean(values * values, axis=-1, keepdims=True)
    return values * lax.rsqrt(mean_square + EPSILON) * gain


def rotary(values, positions):
    dim = values.shape[-1]
    half = dim // 2
    freq = jnp.power(ROPE_BASE, -2.0 * jnp.arange(half, dtype=jnp.int32).astype(jnp.float32) / dim)
    angle = positions.astype(jnp.float32)[:, :, None] * freq
    cosine = jnp.cos(angle)[:, :, None, :]
    sine = jnp.sin(angle)[:, :, None, :]
    first = values[..., :half].astype(jnp.float32)
    second = values[..., half:].astype(jnp.float32)
    return jnp.concatenate(
        [first * cosine - second * sine, second * cosine + first * sine], axis=-1
    )


def source_layout(owner_block, peers, pair_rows):
    row_count = owner_block.shape[0]
    owners = jnp.arange(peers, dtype=jnp.int32)
    member = owner_block[None, :] == owners[:, None]
    counts = jnp.sum(member.astype(jnp.int32), axis=1)
    row_ids = jnp.arange(row_count, dtype=jnp.int32)
    starts = jnp.min(jnp.where(member, row_ids[None, :], row_count), axis=1)
    slots = jnp.arange(pair_rows, dtype=jnp.int32)
    gather_rows = jnp.where(
        slots[None, :] < counts[:, None], starts[:, None] + slots[None, :], row_count
    )
    row_start = jnp.sum(jnp.where(member, starts[:, None], 0), axis=0)
    back_rows = owner_block * pair_rows + (row_ids - row_start)
    return (gather_rows.reshape(-1), back_rows)


def owner_attention(query_in, key_in, value_in, cache_keys, cache_values, lengths, priors, table):
    sources, pair_rows, qcols = query_in.shape
    kcols = key_in.shape[-1]
    kv_heads = kcols // HD
    group = qcols // kcols
    pool_pages = cache_keys.shape[0]
    slots = jnp.arange(pair_rows, dtype=jnp.int32)
    positions = priors[:, None] + slots[None, :]
    live = slots[None, :] < lengths[:, None]
    query_rot = rotary(query_in.reshape(sources, pair_rows, qcols // HD, HD), positions).astype(
        jnp.bfloat16
    )
    key_rot = rotary(key_in.reshape(sources, pair_rows, kv_heads, HD), positions).astype(
        jnp.bfloat16
    )
    key_rot = key_rot.reshape(sources, pair_rows, kcols)
    pages = table.reshape(sources, MAXP)
    page_index = jnp.minimum(positions // PAGE, MAXP - 1)
    target = jnp.take_along_axis(pages, page_index, axis=1)
    target = jnp.where(live, target, pool_pages).reshape(-1)
    offset = (positions % PAGE).reshape(-1)
    keys_out = cache_keys.at[target, offset].set(key_rot.reshape(-1, kcols), mode="drop")
    values_out = cache_values.at[target, offset].set(value_in.reshape(-1, kcols), mode="drop")
    key_block = jnp.take(keys_out, pages.reshape(-1), axis=0).reshape(
        sources, CONTEXT, kv_heads, HD
    )
    value_block = jnp.take(values_out, pages.reshape(-1), axis=0).reshape(
        sources, CONTEXT, kv_heads, HD
    )
    grouped = query_rot.reshape(sources, pair_rows, kv_heads, group, HD)
    scores = (
        jnp.einsum("stkgd,sjkd->skgtj", grouped, key_block, preferred_element_type=jnp.float32)
        * SCORE_MULT
    )
    allowed = (
        jnp.arange(CONTEXT, dtype=jnp.int32)[None, None, None, None, :]
        <= positions[:, None, None, :, None]
    )
    scores = jnp.where(allowed, scores, -jnp.inf)
    top = jnp.max(scores, axis=-1, keepdims=True)
    weights = jnp.exp(scores - top)
    probs = (weights / jnp.sum(weights, axis=-1, keepdims=True)).astype(jnp.bfloat16)
    mixed = jnp.einsum("skgtj,sjkd->stkgd", probs, value_block, preferred_element_type=jnp.float32)
    return (mixed.astype(jnp.bfloat16).reshape(sources, pair_rows, qcols), keys_out, values_out)


def body(
    hidden_in,
    attn_gain,
    mlp_gain,
    w_query,
    w_key,
    w_value,
    w_out,
    w_gate,
    w_up,
    w_down,
    cache_k,
    cache_v,
    owner_of_row,
    new_len,
    prior_len,
    page_table,
):
    peers = lax.axis_size("req")
    groups = lax.axis_size("grp")
    row_count = hidden_in.shape[0]
    pair_rows = 2 * row_count // peers
    quarter = row_count // groups
    group_index = lax.axis_index("grp")
    normed = normalize(hidden_in.astype(jnp.float32), attn_gain).astype(jnp.bfloat16)
    query_rows = jnp.dot(normed, w_query, preferred_element_type=jnp.float32).astype(jnp.bfloat16)
    key_rows = jnp.dot(normed, w_key, preferred_element_type=jnp.float32).astype(jnp.bfloat16)
    value_rows = jnp.dot(normed, w_value, preferred_element_type=jnp.float32).astype(jnp.bfloat16)
    gather_rows, back_rows = source_layout(owner_of_row, peers, pair_rows)
    send_query = jnp.take(query_rows, gather_rows, axis=0, mode="fill", fill_value=0).reshape(
        peers, pair_rows, -1
    )
    send_key = jnp.take(key_rows, gather_rows, axis=0, mode="fill", fill_value=0).reshape(
        peers, pair_rows, -1
    )
    send_value = jnp.take(value_rows, gather_rows, axis=0, mode="fill", fill_value=0).reshape(
        peers, pair_rows, -1
    )
    recv_query, recv_key, recv_value = (
        lax.all_to_all(send_query, "req", split_axis=0, concat_axis=0, tiled=True),
        lax.all_to_all(send_key, "req", split_axis=0, concat_axis=0, tiled=True),
        lax.all_to_all(send_value, "req", split_axis=0, concat_axis=0, tiled=True),
    )
    mixed, keys_out, values_out = owner_attention(
        recv_query, recv_key, recv_value, cache_k, cache_v, new_len[0], prior_len[0], page_table[0]
    )
    returned = lax.all_to_all(mixed, "req", split_axis=0, concat_axis=0, tiled=True)
    attn_rows = jnp.take(returned.reshape(peers * pair_rows, -1), back_rows, axis=0)
    picked = attn_rows
    attn_part = lax.psum_scatter(
        jnp.dot(picked, w_out, preferred_element_type=jnp.float32).astype(jnp.bfloat16),
        "grp",
        scatter_dimension=0,
        tiled=True,
    ).astype(jnp.float32)
    own_rows = lax.dynamic_slice_in_dim(hidden_in, group_index * quarter, quarter, 0).astype(
        jnp.float32
    )
    residual = own_rows + RESIDUAL_MULT * attn_part
    mlp_in = normalize(residual, mlp_gain).astype(jnp.bfloat16)
    piece = lax.all_gather(mlp_in, "req", axis=0, tiled=True)
    gate = jnp.dot(piece, w_gate, preferred_element_type=jnp.float32)
    upper = jnp.dot(piece, w_up, preferred_element_type=jnp.float32)
    hidden = (jax.nn.silu(gate) * upper).astype(jnp.bfloat16)
    picked = hidden
    down = lax.psum_scatter(
        jnp.dot(picked, w_down, preferred_element_type=jnp.float32).astype(jnp.bfloat16),
        "req",
        scatter_dimension=0,
        tiled=True,
    ).astype(jnp.float32)
    layer_out = (residual + RESIDUAL_MULT * down).astype(jnp.bfloat16)
    return (layer_out, keys_out, values_out)


def solution(mesh):
    in_specs = (
        P("req", None),
        P(),
        P(),
        P(None, "grp"),
        P(None, "grp"),
        P(None, "grp"),
        P("grp", None),
        P(None, "req"),
        P(None, "req"),
        P("req", None),
        P("req", None, "grp"),
        P("req", None, "grp"),
        P("req"),
        P("req", None),
        P("req", None),
        P("req", None),
    )
    out_specs = (P(("req", "grp"), None), P("req", None, "grp"), P("req", None, "grp"))
    return jax.shard_map(body, mesh=mesh, in_specs=in_specs, out_specs=out_specs, check_vma=False)
```

profile of v0, /device:TPU:0, one launch (start us, length us, event | category | flops | bytes accessed | tf_op | source)
XLA Modules:
  0.0 372.2 jit_solution(14132992227413498554)
XLA Ops:
  13.0 3.2 gather_fusion.3
  16.3 3.2 gather_fusion.5
  21.2 7.3 %all-to-all-start.1 = ((bf16[8,128,128]{1,2,0:T(8,128)(2,1)}), bf16[8,128,128]{1,2,0:T(8,128)(2,1)S(1)}, u32[]{:S(2)}, u32[]{:S(2)}) async-start(bf16[8,128,128]{1,2,0:T(8,128)(2,1)} %copy.41), calls=%async_computation.1 | async-start | bytes 524288 | tf_op jit(solution)/shard_map/all_to_all | solution.py:139
  29.9 4.8 %gather_fusion.2 = s32[1024]{0:T(1024)S(1)} fusion(s32[8,16]{1,0:T(8,128)S(1)} %reshape_squeeze.3, s32[1024]{0:T(1024)S(1)} %fusion.32), kind=kCustom, calls=%fused_computation.6 | custom fusion | bytes 16384 | tf_op jit(solution)/shard_map/jit(take_along_axis)/gather | solution.py:71
  35.1 3.5 convolution_convert_fusion.2
  38.6 5.1 %gather_fusion = bf16[1024,512]{1,0:T(8,128)(2,1)} fusion(bf16[512,512]{1,0:T(8,128)(2,1)S(1)} %convolution_convert_fusion.2, s32[1024]{0:T(1024)S(1)} %broadcast_clamp_fusion), kind=kCustom, calls=%fused_computation.4 | custom fusion | bytes 2101248 | tf_op jit(solution)/shard_map/jit(_take)/gather | solution.py:128
  43.9 6.0 %all-to-all-start = ((bf16[8,128,128]{2,1,0:T(8,128)(2,1)}), bf16[8,128,128]{2,1,0:T(8,128)(2,1)S(1)}, u32[]{:S(2)}, u32[]{:S(2)}) async-start(bf16[8,128,128]{2,1,0:T(8,128)(2,1)} %bitcast.79), calls=%async_computation | async-start | bytes 524288 | tf_op jit(solution)/shard_map/all_to_all | solution.py:140
  52.5 6.0 %all-to-all-done = bf16[8,128,128]{2,1,0:T(8,128)(2,1)S(1)} async-done(((bf16[8,128,128]{2,1,0:T(8,128)(2,1)}), bf16[8,128,128]{2,1,0:T(8,128)(2,1)S(1)}, u32[]{:S(2)}, u32[]{:S(2)}) %all-to-all-start) | async-done | bytes 262176 | tf_op jit(solution)/shard_map/all_to_all | solution.py:140
  58.4 4.2 %all-to-all-start.2 = ((bf16[8,128,512]{2,1,0:T(8,128)(2,1)}), bf16[8,128,512]{2,1,0:T(8,128)(2,1)}, u32[]{:S(2)}, u32[]{:S(2)}) async-start(bf16[8,128,512]{2,1,0:T(8,128)(2,1)} %broadcast_select_fusion), calls=%async_computation.2 | async-start | bytes 2097152 | tf_op jit(solution)/shard_map/all_to_all | solution.py:138
  70.0 3.8 %scatter_fusion.1 = bf16[2048,128]{1,0:T(8,128)(2,1)S(1)} fusion(bf16[2048,128]{1,0:T(8,128)(2,1)S(1)} %bitcast.72, s32[1024]{0:T(1024)S(1)} %broadcast_select_fusion.5, bf16[1024,128]{1,0:T(8,128)(2,1)} %reshape.607), kind=kCustom, calls=%fused_computation.8 | custom fusion | bytes 790528
  75.4 4.0 %scatter_fusion = bf16[2048,128]{1,0:T(8,128)(2,1)S(1)} fusion(bf16[2048,128]{1,0:T(8,128)(2,1)S(1)} %bitcast.69, s32[1024]{0:T(1024)S(1)} %broadcast_select_fusion.5, bf16[1024,128]{1,0:T(8,128)(2,1)} %bitcast.80), kind=kCustom, calls=%fused_computation.7 | custom fusion | bytes 790528
  83.2 3.2 reshape.513
  86.4 3.2 reshape.510
  96.0 4.4 %fusion.52 = (f32[8,2,4,128]{3,2,1,0:T(4,128)S(1)}, f32[8,2,4,128,256]{3,4,2,1,0:T(8,128)}) fusion(f32[8,2,256,128,4]{3,2,4,1,0:T(8,128)S(1)} %fusion.14, pred[8,128,256]{1,2,0:T(8,128)(4,1)S(1)} %copy-done.11), kind=kOutput, calls=%fused_computation.134 | output fusion | flops 12583167 | bytes 17072128 | tf_op jit(solution)/shard_map/sub | solution.py:93
  100.4 5.4 %fusion.9 = bf16[8,2,64,4,128]{4,2,3,1,0:T(8,128)(2,1)} fusion(f32[8,2,4,128,256]{3,4,2,1,0:T(8,128)} %get-tuple-element.25, f32[8,2,4,128]{3,2,1,0:T(4,128)S(1)} %get-tuple-element.24, bf16[8,256,2,64,1]{3,2,1,0,4:T(2,128)(2,1)S(1)} %bitcast.82), kind=kOutput, calls=%fused_computation.26 | convolution fusion | flops 273154048 | bytes 9994240 | tf_op jit(solution)/shard_map/skgtj,sjkd->stkgd/dot_general | solution.py:95
  105.8 5.9 %all-to-all-start.3 = ((bf16[8,128,512]{1,2,0:T(8,128)(2,1)}), bf16[8,128,512]{1,2,0:T(8,128)(2,1)}, u32[]{:S(2)}, u32[]{:S(2)}) async-start(bf16[8,128,512]{1,2,0:T(8,128)(2,1)} %bitcast.29), calls=%async_computation.3 | async-start | bytes 2097152 | tf_op jit(solution)/shard_map/all_to_all | solution.py:145
  111.8 24.2 %all-to-all-done.3 = bf16[8,128,512]{1,2,0:T(8,128)(2,1)} async-done(((bf16[8,128,512]{1,2,0:T(8,128)(2,1)}), bf16[8,128,512]{1,2,0:T(8,128)(2,1)}, u32[]{:S(2)}, u32[]{:S(2)}) %all-to-all-start.3) | async-done | bytes 1048608 | tf_op jit(solution)/shard_map/all_to_all | solution.py:145
  137.6 2.6 gather_fusion.1
  140.2 3.7 convolution_convert_fusion.1
  144.0 30.3 %reduce-scatter.3.cloned.1.call-done = bf16[128,2048]{1,0:T(8,128)(2,1)} async-done(((bf16[512,2048]{1,0:T(8,128)(2,1)}), bf16[128,2048]{1,0:T(8,128)(2,1)}) %reduce-scatter.3.cloned.1.call-update) | async-done | bytes 524304 | tf_op jit(solution)/shard_map/reduce_scatter | solution.py:148
  178.4 73.3 %all-gather.2.cloned.1.call-done = bf16[1024,2048]{1,0:T(8,128)(2,1)} async-done(((bf16[128,2048]{1,0:T(8,128)(2,1)}), bf16[1024,2048]{1,0:T(8,128)(2,1)}) %all-gather.2.cloned.1.call-update) | async-done | bytes 4194320 | tf_op jit(solution)/shard_map/all_gather | solution.py:159
  251.7 9.9 %fusion.53 = f32[1024,1024]{1,0:T(8,128)} fusion(bf16[1024,2048]{1,0:T(8,128)(2,1)} %all-gather.2.cloned.1.call-done, bf16[2048,1024]{1,0:T(8,128)(2,1)} %param.27), kind=kOutput, calls=%fused_computation.135 | convolution fusion | flops 4294967296 | bytes 12582912 | tf_op jit(solution)/shard_map/dot_general | solution.py:160
  261.6 15.3 %convolution_convert_fusion = bf16[1024,2048]{1,0:T(8,128)(2,1)} fusion(bf16[1024,2048]{1,0:T(8,128)(2,1)} %param.29, f32[1024,1024]{1,0:T(8,128)} %fusion.53, bf16[1024,2048]{1,0:T(8,128)(2,1)} %all-gather.2.cloned.1.call-done, bf16[2048,1024]{1,0:T(8,128)(2,1)} %param.28), kind=kOutput, calls=%fused_computation.24 | convolution fusion | flops 8598323200 | bytes 20971520 | tf_op jit(solution)/shard_map/dot_general | solution.py:165
  276.9 86.5 %reduce-scatter.5.cloned.1.call-done = bf16[128,2048]{1,0:T(8,128)(2,1)} async-done(((bf16[1024,2048]{1,0:T(8,128)(2,1)}), bf16[128,2048]{1,0:T(8,128)(2,1)}) %reduce-scatter.5.cloned.1.call-update) | async-done | bytes 524304 | tf_op jit(solution)/shard_map/reduce_scatter | solution.py:164
  (103 shorter events, 38.9 us)
Async XLA Ops:
  7.2 133.0 %copy-start = (bf16[512,2048]{1,0:T(8,128)(2,1)S(1)}, bf16[512,2048]{1,0:T(8,128)(2,1)}, u32[]{:S(2)}) copy-start(bf16[512,2048]{1,0:T(8,128)(2,1)} %param.26) | copy-start | bytes 6291460
  7.2 5.0 %copy-start.19 = (bf16[2048,128]{1,0:T(8,128)(2,1)S(1)}, bf16[2048,128]{1,0:T(8,128)(2,1)}, u32[]{:S(2)}) copy-start(bf16[2048,128]{1,0:T(8,128)(2,1)} %param.24) | copy-start | bytes 1572868
  13.0 15.5 %copy-start.14 = (s32[1,8]{1,0:T(1,128)S(1)}, s32[1,8]{1,0:T(1,128)}, u32[]{:S(2)}) copy-start(s32[1,8]{1,0:T(1,128)} %param.34) | copy-start | bytes 100
  13.0 16.1 %copy-start.21 = (s32[1,128]{1,0:T(1,128)S(1)}, s32[1,128]{1,0:T(1,128)}, u32[]{:S(2)}) copy-start(s32[1,128]{1,0:T(1,128)} %param.35) | copy-start | bytes 1540
  16.2 18.7 %copy-start.15 = (s32[1,8]{1,0:T(1,128)S(1)}, s32[1,8]{1,0:T(1,128)}, u32[]{:S(2)}) copy-start(s32[1,8]{1,0:T(1,128)} %param.33) | copy-start | bytes 100
  21.2 22.7 %all-to-all-start.1 = ((bf16[8,128,128]{1,2,0:T(8,128)(2,1)}), bf16[8,128,128]{1,2,0:T(8,128)(2,1)S(1)}, u32[]{:S(2)}, u32[]{:S(2)}) async-start(bf16[8,128,128]{1,2,0:T(8,128)(2,1)} %copy.41), calls=%async_computation.1 | async-start | bytes 524288 | tf_op jit(solution)/shard_map/all_to_all | solution.py:139
  38.6 5.1 %copy-start.17 = (s32[2]{0:T(128)S(1)}, s32[2]{0:T(128)}, u32[]{:S(2)}) copy-start(s32[2]{0:T(128)} %constant.135) | copy-start | bytes 28
  38.6 5.2 %copy-start.16 = (s32[2]{0:T(128)S(1)}, s32[2]{0:T(128)}, u32[]{:S(2)}) copy-start(s32[2]{0:T(128)} %constant.138) | copy-start | bytes 28
  43.7 26.4 %copy-start.5 = (bf16[128,16,128]{2,1,0:T(8,128)(2,1)S(1)}, bf16[128,16,128]{2,1,0:T(8,128)(2,1)}, u32[]{:S(2)}) copy-start(bf16[128,16,128]{2,1,0:T(8,128)(2,1)} %param.30) | copy-start | bytes 1572868
  43.9 19.7 %copy-start.8 = (bf16[8,128,128]{1,2,0:T(8,128)(2,1)}, bf16[8,128,128]{1,2,0:T(8,128)(2,1)S(1)}, u32[]{:S(2)}) copy-start(bf16[8,128,128]{1,2,0:T(8,128)(2,1)S(1)} %all-to-all-done.1) | copy-start | bytes 786436
  43.9 14.5 %all-to-all-start = ((bf16[8,128,128]{2,1,0:T(8,128)(2,1)}), bf16[8,128,128]{2,1,0:T(8,128)(2,1)S(1)}, u32[]{:S(2)}, u32[]{:S(2)}) async-start(bf16[8,128,128]{2,1,0:T(8,128)(2,1)} %bitcast.79), calls=%async_computation | async-start | bytes 524288 | tf_op jit(solution)/shard_map/all_to_all | solution.py:140
  58.4 5.8 %copy-start.9 = (bf16[8,128,128]{2,1,0:T(8,128)(2,1)}, bf16[8,128,128]{2,1,0:T(8,128)(2,1)S(1)}, u32[]{:S(2)}) copy-start(bf16[8,128,128]{2,1,0:T(8,128)(2,1)S(1)} %all-to-all-done) | copy-start | bytes 786436
  58.4 31.2 %all-to-all-start.2 = ((bf16[8,128,512]{2,1,0:T(8,128)(2,1)}), bf16[8,128,512]{2,1,0:T(8,128)(2,1)}, u32[]{:S(2)}, u32[]{:S(2)}) async-start(bf16[8,128,512]{2,1,0:T(8,128)(2,1)} %broadcast_select_fusion), calls=%async_computation.2 | async-start | bytes 2097152 | tf_op jit(solution)/shard_map/all_to_all | solution.py:138
  64.2 11.2 %copy-start.3 = (bf16[128,16,128]{2,1,0:T(8,128)(2,1)S(1)}, bf16[128,16,128]{2,1,0:T(8,128)(2,1)}, u32[]{:S(2)}) copy-start(bf16[128,16,128]{2,1,0:T(8,128)(2,1)} %param.31) | copy-start | bytes 1572868
  73.9 9.4 %copy-start.4 = (bf16[2048,128]{1,0:T(8,128)(2,1)}, bf16[2048,128]{1,0:T(8,128)(2,1)S(1)}, u32[]{:S(2)}) copy-start(bf16[2048,128]{1,0:T(8,128)(2,1)S(1)} %scatter_fusion.1) | copy-start | bytes 1572868
  79.3 12.5 %copy-start.2 = (bf16[2048,128]{1,0:T(8,128)(2,1)}, bf16[2048,128]{1,0:T(8,128)(2,1)S(1)}, u32[]{:S(2)}) copy-start(bf16[2048,128]{1,0:T(8,128)(2,1)S(1)} %scatter_fusion) | copy-start | bytes 1572868
  100.4 11.4 %copy-start.12 = (s32[512]{0:T(512)S(1)}, s32[512]{0:T(512)}, u32[]{:S(2)}) copy-start(s32[512]{0:T(512)} %param.32) | copy-start | bytes 6148
  105.8 30.2 %all-to-all-start.3 = ((bf16[8,128,512]{1,2,0:T(8,128)(2,1)}), bf16[8,128,512]{1,2,0:T(8,128)(2,1)}, u32[]{:S(2)}, u32[]{:S(2)}) async-start(bf16[8,128,512]{1,2,0:T(8,128)(2,1)} %bitcast.29), calls=%async_computation.3 | async-start | bytes 2097152 | tf_op jit(solution)/shard_map/all_to_all | solution.py:145
  111.8 62.6 %reduce-scatter.3.cloned.1.call-start = ((), (), s32[]{:S(2)}) async-start(), calls=%async_computation.6 | async-start | bytes 2621440 | tf_op jit(solution)/shard_map/reduce_scatter | solution.py:148
  140.2 35.6 %copy-start.13 = (f32[2048]{0:T(1024)S(1)}, f32[2048]{0:T(1024)}, u32[]{:S(2)}) copy-start(f32[2048]{0:T(1024)} %param.22) | copy-start | bytes 24580
  143.9 107.7 %all-gather.2.cloned.1.call-start = ((), (), s32[]{:S(2)}) async-start(), calls=%async_computation.7 | async-start | bytes 4718592 | tf_op jit(solution)/shard_map/all_gather | solution.py:159
  178.1 185.3 %reduce-scatter.5.cloned.1.call-start = ((), (), s32[]{:S(2)}) async-start(), calls=%async_computation.8 | async-start | bytes 4718592 | tf_op jit(solution)/shard_map/reduce_scatter | solution.py:164
  261.6 104.1 %copy-start.1 = (bf16[512,2048]{1,0:T(8,128)(2,1)S(1)}, bf16[512,2048]{1,0:T(8,128)(2,1)}, u32[]{:S(2)}) copy-start(bf16[512,2048]{1,0:T(8,128)(2,1)} %param.26) | copy-start | bytes 6291460
  276.8 86.5 %copy-start.7 = (bf16[128,2048]{1,0:T(8,128)(2,1)S(1)}, bf16[128,2048]{1,0:T(8,128)(2,1)}, u32[]{:S(2)}) copy-start(bf16[128,2048]{1,0:T(8,128)(2,1)} %reduce-scatter.3.cloned.1.call-done) | copy-start | bytes 1572868
  (5 other events, 19.7 us)
Sparse Core Ops, SparseCore 0:
  144.1 30.2 reduce-scatter.2
  178.2 73.3 all-gather.1
  277.0 86.3 reduce-scatter.4
where the time goes:
time: 373 us; the launch traced here: 372 us
  waiting for transfers between devices  220 us (59%)
  local copies, waits for them, and re-layouts  45.6 us (12%)
  matrix products  41.9 us (11%)
  other arithmetic  26.3 us (7%)
  starting transfers between devices  23.8 us (6%)
  between operations  14.1 us (4%)
    reduce_scatter x1, waiting for transfers between devices, body(): lax.psum_scatter(jnp.dot(picked, w_down, preferred_element_type=jnp.float...  86.5 us
    all_gather x1, waiting for transfers between devices, body(): piece = lax.all_gather(mlp_in, 'req', axis=0, tiled=True)  73.3 us
    reduce_scatter x1, waiting for transfers between devices, body(): lax.psum_scatter(jnp.dot(picked, w_out, preferred_element_type=jnp.float3...  30.3 us
    all_to_all x1, waiting for transfers between devices, body(): lax.all_to_all(mixed, 'req', split_axis=0, concat_axis=0, tiled=True)  24.2 us
    dot_general x1, matrix products, body(): jnp.dot(picked, w_down, preferred_element_type=jnp.float32)  15.3 us
    dot_general x1, matrix products, body(): gate = jnp.dot(piece, w_gate, preferred_element_type=jnp.float32)  9.92 us
    unnamed x47, local copies, waits for them, and re-layouts  8.42 us
  transfers between devices with their start and end apart: 7, of which 5 were waited for; matrix products, arithmetic and copies ran while one was open for 12% of the time, Pallas kernels for 0%

commit v1 on v0

v1 whole, which is shorter than its diff:
```python
import functools

import jax
import jax.numpy as jnp
from jax import lax
from jax.experimental import pallas as pl
from jax.experimental.pallas import tpu as pltpu
from jax.sharding import PartitionSpec as P

HD = 64
PAGE = 16
MAXP = 16
CONTEXT = 256
LANES = 128
INFO = 16


EPSILON = 1e-05
RESIDUAL_MULT = 0.22
SCORE_MULT = 0.015625
ROPE_BASE = 10000000.0
BF = jnp.bfloat16
F32 = jnp.float32
SMEM = pl.BlockSpec(memory_space=pltpu.SMEM)
VMEM = pl.BlockSpec(memory_space=pltpu.VMEM)


def normalize(values, gain):
    mean_square = jnp.mean(values * values, axis=-1, keepdims=True)
    return values * lax.rsqrt(mean_square + EPSILON) * gain


def rope_tables(length):
    lane = jnp.arange(LANES, dtype=jnp.int32)
    half = HD // 2
    freq = jnp.power(ROPE_BASE, -2.0 * (lane % half).astype(F32) / HD)
    angle = jnp.arange(length, dtype=jnp.int32).astype(F32)[:, None] * freq
    sign = jnp.where(lane % HD < half, -1.0, 1.0).astype(F32)
    return jnp.cos(angle), jnp.sin(angle) * sign


def rotate(values, cosine, sine):
    lane = lax.broadcasted_iota(jnp.int32, values.shape, 1)
    swapped = jnp.where(
        lane % HD < HD // 2,
        pltpu.roll(values, LANES - HD // 2, 1),
        pltpu.roll(values, HD // 2, 1),
    )
    return values * cosine + swapped * sine


def dot(a, b):
    return jnp.dot(a, b, preferred_element_type=F32)


def pack_kernel(order, table, prior, cache_k, cache_v, *outs):
    for step, out in enumerate(outs):
        source = order[step]
        for page in range(MAXP):
            at = table[source * MAXP + page]
            out[page * PAGE : (page + 1) * PAGE, :] = cache_k[at]
            out[CONTEXT + page * PAGE : CONTEXT + (page + 1) * PAGE, :] = cache_v[at]
        out[2 * CONTEXT :, :] = jnp.full((INFO, LANES), prior[source].astype(F32), F32).astype(BF)


def pack_pages(order, table, prior, cache_k, cache_v):
    peers = order.shape[0]
    block = jax.ShapeDtypeStruct((2 * CONTEXT + INFO, LANES), BF)
    return pl.pallas_call(
        pack_kernel,
        out_shape=[block] * peers,
        in_specs=[SMEM, SMEM, SMEM, VMEM, VMEM],
        out_specs=[VMEM] * peers,
        name="pack_pages",
    )(order, table, prior, cache_k, cache_v)


def attention_kernel(
    order, starts, counts, priors, group, query, key, value, pages, cosines, sines, mixed, sent, total
):
    step = pl.program_id(0)
    owner = order[step]
    start, count, prior = starts[owner], counts[owner], priors[step]
    rows, qcols = query.shape
    pair = sent.shape[1]

    @pl.when(step == 0)
    def _():
        total[...] = jnp.zeros_like(total)

    @pl.when(count == 0)
    def _():
        sent[...] = jnp.zeros_like(sent)

    @pl.when(count > 0)
    def _():
        slot = lax.broadcasted_iota(jnp.int32, (pair, rows), 0)
        row = lax.broadcasted_iota(jnp.int32, (pair, rows), 1)
        pick = jnp.where((row == slot + start) & (slot < count), 1.0, 0.0).astype(BF)
        cosine = cosines[pl.ds(prior, pair), :]
        sine = sines[pl.ds(prior, pair), :]
        new_key = rotate(dot(pick, key[...]), cosine, sine).astype(BF)
        new_value = dot(pick, value[...]).astype(BF)
        sent[0, :, :LANES] = new_key
        sent[0, :, LANES:] = new_value

        place = lax.broadcasted_iota(jnp.int32, (CONTEXT, pair), 0)
        new_slot = lax.broadcasted_iota(jnp.int32, (CONTEXT, pair), 1)
        put = jnp.where((place == new_slot + prior) & (new_slot < count), 1.0, 0.0).astype(BF)
        position = lax.broadcasted_iota(jnp.int32, (CONTEXT, LANES), 0)
        lane = lax.broadcasted_iota(jnp.int32, (CONTEXT, LANES), 1)
        low = lane < HD

        def merged(new, old):
            whole = jnp.where(position < prior, old.astype(F32), dot(put, new))
            turned = pltpu.roll(whole, HD, 1)
            return (
                jnp.where(low, whole, turned).astype(BF),
                jnp.where(low, turned, whole).astype(BF),
            )

        keys = merged(new_key, pages[0, :CONTEXT, :])
        values = merged(new_value, pages[0, CONTEXT : 2 * CONTEXT, :])

        queries = dot(pick, query[...])
        query_slot = lax.broadcasted_iota(jnp.int32, (2 * pair, CONTEXT), 0)
        query_slot = jnp.where(query_slot >= pair, query_slot - pair, query_slot)
        at = lax.broadcasted_iota(jnp.int32, (2 * pair, CONTEXT), 1)
        allowed = at <= query_slot + prior
        left = lax.broadcasted_iota(jnp.int32, (pair, LANES), 1) < HD
        tiles = qcols // LANES
        outs = []
        for tile in range(tiles):
            kv = tile * 2 // tiles
            turned = rotate(queries[:, tile * LANES : (tile + 1) * LANES], cosine, sine)
            both = jnp.concatenate([jnp.where(left, turned, 0.0), jnp.where(left, 0.0, turned)], 0)
            score = lax.dot_general(
                both.astype(BF), keys[kv], (((1,), (1,)), ((), ())), preferred_element_type=F32
            )
            score = jnp.where(allowed, score * SCORE_MULT, -1e30)
            weight = jnp.exp(score - jnp.max(score, axis=-1, keepdims=True))
            probs = (weight / jnp.sum(weight, axis=-1, keepdims=True)).astype(BF)
            out = dot(probs, values[kv])
            outs.append(jnp.where(left, out[:pair], out[pair:]).astype(BF))
        block = jnp.concatenate(outs, axis=1)
        home = lax.broadcasted_iota(jnp.int32, (rows, pair), 0)
        slot_back = lax.broadcasted_iota(jnp.int32, (rows, pair), 1)
        back = jnp.where((home == slot_back + start) & (slot_back < count), 1.0, 0.0).astype(BF)
        total[...] += dot(back, block)

    @pl.when(step == pl.num_programs(0) - 1)
    def _():
        parts = mixed.shape[0]
        quarter = rows // parts
        for part in range(parts):
            first = pl.multiple_of((group[0] ^ part) * quarter, quarter)
            mixed[part] = total[pl.ds(first, quarter), :].astype(BF)


def attend(order, starts, counts, priors, group, query, key, value, pages, cosines, sines, pair, parts):
    peers = order.shape[0]
    rows, qcols = query.shape
    whole = lambda step, *_: (0, 0)
    here = lambda step, *_: (step, 0, 0)
    return pl.pallas_call(
        attention_kernel,
        out_shape=[
            jax.ShapeDtypeStruct((parts, rows // parts, qcols), BF),
            jax.ShapeDtypeStruct((peers, pair, 2 * LANES), BF),
        ],
        grid_spec=pltpu.PrefetchScalarGridSpec(
            num_scalar_prefetch=5,
            grid=(peers,),
            in_specs=[
                pl.BlockSpec((rows, qcols), whole),
                pl.BlockSpec((rows, LANES), whole),
                pl.BlockSpec((rows, LANES), whole),
                pl.BlockSpec((1,) + pages.shape[1:], here),
                pl.BlockSpec(cosines.shape, whole),
                pl.BlockSpec(sines.shape, whole),
            ],
            out_specs=[
                pl.BlockSpec((parts, rows // parts, qcols), lambda step, *_: (0, 0, 0)),
                pl.BlockSpec((1, pair, 2 * LANES), lambda step, order, *_: (order[step], 0, 0)),
            ],
            scratch_shapes=[pltpu.VMEM((rows, qcols), F32)],
        ),
        compiler_params=pltpu.CompilerParams(
            vmem_limit_bytes=32 * 1024 * 1024, dimension_semantics=("arbitrary",)
        ),
        name="attend",
    )(order, starts, counts, priors, group, query, key, value, pages, cosines, sines)


def store_kernel(table, priors, counts, new, cache_k, cache_v, keys_out, values_out):
    peers, pair, _ = new.shape
    keys_out[...] = cache_k[...]
    values_out[...] = cache_v[...]

    def request(source, carry):
        prior, count = priors[source], counts[source]
        place = lax.broadcasted_iota(jnp.int32, (CONTEXT, pair), 0)
        slot = lax.broadcasted_iota(jnp.int32, (CONTEXT, pair), 1)
        put = jnp.where((place == slot + prior) & (slot < count), 1.0, 0.0).astype(BF)
        moved = dot(put, new[source])
        position = lax.broadcasted_iota(jnp.int32, (PAGE, LANES), 0)
        for page in range(MAXP):
            at = table[source * MAXP + page]
            here = position + page * PAGE
            fresh = (here >= prior) & (here < prior + count)
            rows = moved[page * PAGE : (page + 1) * PAGE]
            keys_out[at] = jnp.where(fresh, rows[:, :LANES], cache_k[at].astype(F32)).astype(BF)
            values_out[at] = jnp.where(fresh, rows[:, LANES:], cache_v[at].astype(F32)).astype(BF)
        return carry

    lax.fori_loop(0, peers, request, 0)


def store_new(table, priors, counts, new, cache_k, cache_v):
    return pl.pallas_call(
        store_kernel,
        out_shape=[jax.ShapeDtypeStruct(cache_k.shape, BF)] * 2,
        in_specs=[SMEM, SMEM, SMEM, VMEM, VMEM, VMEM],
        out_specs=[VMEM] * 2,
        compiler_params=pltpu.CompilerParams(vmem_limit_bytes=32 * 1024 * 1024),
        name="store_new",
    )(table, priors, counts, new, cache_k, cache_v)


def swap(values, axis, size, bit):
    return lax.ppermute(values, axis, [(at, at ^ bit) for at in range(size)])


def feed_forward(rows, w_gate, w_up, w_down):
    gate = dot(rows, w_gate)
    upper = dot(rows, w_up)
    hidden = (jax.nn.silu(gate) * upper).astype(BF)
    return dot(hidden, w_down).astype(BF)


def exchange_mlp(own, peers, w_gate, w_up, w_down):
    send = functools.partial(swap, axis="req", size=peers)
    unit = own.shape[0]
    if peers != 8:
        piece = lax.all_gather(own, "req", axis=0, tiled=True)
        part = feed_forward(piece, w_gate, w_up, w_down)
        return lax.psum_scatter(part, "req", scatter_dimension=0, tiled=True).astype(F32)
    far = send(own, bit=4)
    near = send(own, bit=2)
    side = send(own, bit=1)
    both = send(far, bit=2)
    mine = [own, near, far, both]
    theirs = [side] + [send(rows, bit=1) for rows in mine[1:]]
    sums = []
    for a, b in zip(mine, theirs):
        part = feed_forward(jnp.concatenate([a, b], 0), w_gate, w_up, w_down)
        back = send(part[unit:], bit=1)
        sums.append(part[:unit].astype(F32) + back.astype(F32))
    from_both = send(sums[3].astype(BF), bit=2)
    from_far = send((sums[2] + from_both.astype(F32)).astype(BF), bit=4)
    from_near = send(sums[1].astype(BF), bit=2)
    return sums[0] + from_near.astype(F32) + from_far.astype(F32)


def body(
    hidden_in,
    attn_gain,
    mlp_gain,
    w_query,
    w_key,
    w_value,
    w_out,
    w_gate,
    w_up,
    w_down,
    cache_k,
    cache_v,
    owner_of_row,
    new_len,
    prior_len,
    page_table,
):
    peers = lax.axis_size("req")
    groups = lax.axis_size("grp")
    row_count = hidden_in.shape[0]
    pair = 2 * row_count // peers
    quarter = row_count // groups
    me = lax.axis_index("req")
    group_index = lax.axis_index("grp")
    owners = jnp.arange(peers, dtype=jnp.int32)
    order = owners ^ me if peers == 8 else owners

    packed = pack_pages(order, page_table[0], prior_len[0], cache_k, cache_v)
    if peers == 8:
        pages = [packed[0]] + [swap(packed[bit], "req", peers, bit) for bit in range(1, peers)]
        pages = jnp.stack(pages)
    else:
        pages = lax.all_to_all(jnp.stack(packed), "req", split_axis=0, concat_axis=0, tiled=True)
    priors = pages[:, 2 * CONTEXT, 0].astype(jnp.int32)

    member = owner_of_row[None, :] == owners[:, None]
    counts = jnp.sum(member.astype(jnp.int32), axis=1)
    row_ids = jnp.arange(row_count, dtype=jnp.int32)
    starts = jnp.min(jnp.where(member, row_ids[None, :], row_count), axis=1)
    cosines, sines = rope_tables(CONTEXT + pair)

    normed = normalize(hidden_in.astype(F32), attn_gain).astype(BF)
    query = dot(normed, w_query).astype(BF)
    key = dot(normed, w_key).astype(BF)
    value = dot(normed, w_value).astype(BF)
    mixed, sent = attend(
        order,
        starts,
        counts,
        priors,
        group_index.reshape(1),
        query,
        key,
        value,
        pages,
        cosines,
        sines,
        pair,
        groups,
    )
    new = lax.all_to_all(sent, "req", split_axis=0, concat_axis=0, tiled=True)
    keys_out, values_out = store_new(page_table[0], prior_len[0], new_len[0], new, cache_k, cache_v)

    out_of = lambda part: dot(mixed[part], w_out).astype(BF)
    cross = swap(out_of(3), "grp", groups, 1)
    beside = swap(out_of(1), "grp", groups, 1)
    over = swap((out_of(2).astype(F32) + cross.astype(F32)).astype(BF), "grp", groups, 2)
    attn_sum = out_of(0).astype(F32) + beside.astype(F32) + over.astype(F32)

    own_rows = lax.dynamic_slice_in_dim(hidden_in, group_index * quarter, quarter, 0).astype(F32)
    residual = own_rows + RESIDUAL_MULT * attn_sum
    mlp_in = normalize(residual, mlp_gain).astype(BF)
    down = exchange_mlp(mlp_in, peers, w_gate, w_up, w_down)
    layer_out = (residual + RESIDUAL_MULT * down).astype(BF)
    return (layer_out, keys_out, values_out)


def solution(mesh):
    in_specs = (
        P("req", None),
        P(),
        P(),
        P(None, "grp"),
        P(None, "grp"),
        P(None, "grp"),
        P("grp", None),
        P(None, "req"),
        P(None, "req"),
        P("req", None),
        P("req", None, "grp"),
        P("req", None, "grp"),
        P("req"),
        P("req", None),
        P("req", None),
        P("req", None),
    )
    out_specs = (P(("req", "grp"), None), P("req", None, "grp"), P("req", None, "grp"))
    return jax.shard_map(body, mesh=mesh, in_specs=in_specs, out_specs=out_specs, check_vma=False)
```

time: 373 us -> 215 us (0.58)
  waiting for transfers between devices: 220 us -> 73.4 us
  local copies, waits for them, and re-layouts: 45.6 us -> 19.8 us
  Pallas kernels: 0 us -> 19.5 us
  between operations: 14.1 us -> 1.17 us
  starting transfers between devices: 23.8 us -> 34.9 us
  other arithmetic: 26.3 us -> 15.5 us
  matrix products: 41.9 us -> 49.5 us
    reduce_scatter x2 -> x0, waiting for transfers between devices: 117 us -> none  [the longest x1 86.5 us: body(): lax.psum_scatter(jnp.dot(picked, w_down, preferred_element_type=jnp.float...]
    ppermute x0 -> x24, waiting for transfers between devices: none -> 73.3 us  [swap(): return lax.ppermute(values, axis, [(at, at ^ bit) for at in range(size)])]
    all_gather x1 -> x0, waiting for transfers between devices: 73.3 us -> none  [body(): piece = lax.all_gather(mlp_in, 'req', axis=0, tiled=True)]
    ppermute x0 -> x24, starting transfers between devices: none -> 30.5 us  [swap(): return lax.ppermute(values, axis, [(at, at ^ bit) for at in range(size)])]
    all_to_all x4 -> x1, waiting for transfers between devices: 30.2 us -> 0.01 us  [body(): new = lax.all_to_all(sent, 'req', split_axis=0, concat_axis=0, tiled=True)]
    gather x7 -> x0, local copies, waits for them, and re-layouts: 21.9 us -> none  [the longest x1 5.05 us: body(): jnp.take(query_rows, gather_rows, axis=0, mode='fill', fill_value=0)]
    pallas_call x0 -> x3, Pallas kernels: none -> 19.5 us  [the longest x1 13.5 us: attend(): pl.pallas_call(attention_kernel, out_shape=[jax.ShapeDtypeStruct((parts,...]
    all_to_all x4 -> x1, starting transfers between devices: 23.4 us -> 4.32 us  [body(): new = lax.all_to_all(sent, 'req', split_axis=0, concat_axis=0, tiled=True)]
  transfers between devices with their start and end apart: 7 -> 25, of which waited for: 5 -> 11; matrix products, arithmetic and copies ran while one was open for 12% -> 34% of each run, Pallas kernels for 0% -> 2%
where the time goes in v1:
time: 215 us; the launch traced here: 214 us
  waiting for transfers between devices  73.4 us (34%)
  matrix products  49.5 us (23%)
  starting transfers between devices  34.9 us (16%)
  local copies, waits for them, and re-layouts  19.8 us (9%)
  Pallas kernels  19.5 us (9%)
  other arithmetic  15.5 us (7%)
    ppermute x24, waiting for transfers between devices, swap(): return lax.ppermute(values, axis, [(at, at ^ bit) for at in range(size)])  73.3 us
    dot_general x15, matrix products, dot(): return jnp.dot(a, b, preferred_element_type=F32)  49.5 us
    ppermute x24, starting transfers between devices, swap(): return lax.ppermute(values, axis, [(at, at ^ bit) for at in range(size)])  30.5 us
    unnamed x76, local copies, waits for them, and re-layouts  15.1 us
    pallas_call x1, Pallas kernels, attend(): pl.pallas_call(attention_kernel, out_shape=[jax.ShapeDtypeStruct((parts,...  13.5 us
    all_to_all x1, starting transfers between devices, body(): new = lax.all_to_all(sent, 'req', split_axis=0, concat_axis=0, tiled=True)  4.32 us
  transfers between devices with their start and end apart: 25, of which 11 were waited for; matrix products, arithmetic and copies ran while one was open for 34% of the time, Pallas kernels for 2%

profile of v1, /device:TPU:0, one launch (start us, length us, event | category | flops | bytes accessed | tf_op | source)
XLA Modules:
  0.0 213.7 jit_solution(17926592632955658239)
XLA Ops:
  3.6 3.0 %collective-permute-start = (bf16[528,128]{1,0:T(8,128)(2,1)}, bf16[528,128]{1,0:T(8,128)(2,1)}, u32[]{:S(2)}, u32[]{:S(2)}) collective-permute-start(bf16[528,128]{1,0:T(8,128)(2,1)} %get-tuple-element.16), channel_id=1, source_target_pairs={{0,4},{4,0},{8,12},{12,8},{16,20},{20,16},{24,28},{28,24},{1,5},{5... | collective-permute-start | bytes 405512 | tf_op jit(solution)/shard_map/ppermute | solution.py:231
  8.2 3.0 %collective-permute-start.3 = (bf16[528,128]{1,0:T(8,128)(2,1)}, bf16[528,128]{1,0:T(8,128)(2,1)}, u32[]{:S(2)}, u32[]{:S(2)}) collective-permute-start(bf16[528,128]{1,0:T(8,128)(2,1)} %get-tuple-element.19), channel_id=1, source_target_pairs={{0,16},{4,20},{8,24},{12,28},{16,0},{20,4},{24,8},{28,12},{1,17},{... | collective-permute-start | bytes 405512 | tf_op jit(solution)/shard_map/ppermute | solution.py:231
  14.6 3.8 %convolution_convert_fusion.8.query = bf16[512,512]{1,0:T(8,128)(2,1)} fusion(bf16[2048,512]{1,0:T(8,128)(2,1)} %param.19, bf16[512,2048]{1,0:T(8,128)(2,1)S(1)} %copy-done.13, f32[2048]{0:T(1024)S(1)} %copy-done.32, f32[512]{0:T(512)S(1)} %add_rsqrt_fusion), kind=kOutput, calls=%fused_computation.15 | convolution fusion | flops 1078198272 | bytes 4728832 | tf_op jit(solution)/shard_map/dot_general | solution.py:53
  22.5 3.7 %collective-permute-start.5 = (bf16[528,128]{1,0:T(8,128)(2,1)}, bf16[528,128]{1,0:T(8,128)(2,1)S(1)}, u32[]{:S(2)}, u32[]{:S(2)}) collective-permute-start(bf16[528,128]{1,0:T(8,128)(2,1)} %get-tuple-element.21), channel_id=1, source_target_pairs={{0,24},{4,28},{8,16},{12,20},{16,8},{20,12},{24,0},{28,4},{1,25},{... | collective-permute-start | bytes 405512 | tf_op jit(solution)/shard_map/ppermute | solution.py:231
  30.9 4.2 %collective-permute-done.6 = bf16[528,128]{1,0:T(8,128)(2,1)S(1)} collective-permute-done((bf16[528,128]{1,0:T(8,128)(2,1)}, bf16[528,128]{1,0:T(8,128)(2,1)S(1)}, u32[]{:S(2)}, u32[]{:S(2)}) %collective-permute-start.6) | collective-permute-done | bytes 135200 | tf_op jit(solution)/shard_map/ppermute | solution.py:231
  37.3 13.5 %attend.1 = (bf16[4,128,512]{2,1,0:T(8,128)(2,1)S(1)}, bf16[8,128,256]{2,1,0:T(8,128)(2,1)}) custom-call(s32[8]{0:T(128)S(1)} %copy-done.9, s32[8]{0:T(128)S(1)} %get-tuple-element.28.starts, s32[8]{0:T(128)S(1)} %get-tuple-element.27.counts, s32[8]{0:T(128)S(1)} %fusion.22.priors, s32[1]{0:T(128)} %bitcast.10.group, bf16[512,512]{1,0:T(8,128)(2,1)S(1)} %copy-done.4, ...), custom_call_target="tpu_custom_call" | custom-call | tf_op jit(solution)/shard_map/attend/pallas_call | solution.py:165
  56.6 11.2 %collective-permute-done.9 = bf16[128,2048]{1,0:T(8,128)(2,1)} collective-permute-done((bf16[128,2048]{1,0:T(8,128)(2,1)S(1)}, bf16[128,2048]{1,0:T(8,128)(2,1)}, u32[]{:S(2)}, u32[]{:S(2)}) %collective-permute-start.9) | collective-permute-done | bytes 524320 | tf_op jit(solution)/shard_map/ppermute | solution.py:231
  70.6 3.8 %collective-permute-start.16 = (bf16[128,2048]{1,0:T(8,128)(2,1)S(1)}, bf16[128,2048]{1,0:T(8,128)(2,1)}, u32[]{:S(2)}, u32[]{:S(2)}) collective-permute-start(bf16[128,2048]{1,0:T(8,128)(2,1)S(1)} %multiply_convert_fusion.4), channel_id=1, source_target_pairs={{0,16},{4,20},{8,24},{12,28},{16,0},{20,4},{24,8},{28,12},{1,17},{... | collective-permute-start | bytes 1572872 | tf_op jit(solution)/shard_map/ppermute | solution.py:231
  75.5 4.3 %all-to-all-start = ((bf16[8,128,256]{2,1,0:T(8,128)(2,1)}), bf16[8,128,256]{2,1,0:T(8,128)(2,1)}, u32[]{:S(2)}, u32[]{:S(2)}) async-start(bf16[8,128,256]{2,1,0:T(8,128)(2,1)} %get-tuple-element.24), calls=%async_computation | async-start | bytes 1048576 | tf_op jit(solution)/shard_map/all_to_all | solution.py:326
  79.8 18.6 %collective-permute-done.16 = bf16[128,2048]{1,0:T(8,128)(2,1)} collective-permute-done((bf16[128,2048]{1,0:T(8,128)(2,1)S(1)}, bf16[128,2048]{1,0:T(8,128)(2,1)}, u32[]{:S(2)}, u32[]{:S(2)}) %collective-permute-start.16) | collective-permute-done | bytes 524320 | tf_op jit(solution)/shard_map/ppermute | solution.py:231
  104.0 4.6 %fusion.6 = f32[256,1024]{1,0:T(8,128)} fusion(bf16[2048,1024]{1,0:T(8,128)(2,1)} %param.23, bf16[128,2048]{1,0:T(8,128)(2,1)S(1)} %collective-permute-done.10, bf16[128,2048]{1,0:T(8,128)(2,1)S(1)} %multiply_convert_fusion.4), kind=kOutput, calls=%fused_computation.32 | convolution fusion | flops 1075838976 | bytes 6291456 | tf_op jit(solution)/shard_map/dot_general | solution.py:53
  108.6 7.0 %collective-permute-done.17 = bf16[128,2048]{1,0:T(8,128)(2,1)S(1)} collective-permute-done((bf16[128,2048]{1,0:T(8,128)(2,1)}, bf16[128,2048]{1,0:T(8,128)(2,1)S(1)}, u32[]{:S(2)}, u32[]{:S(2)}) %collective-permute-start.17) | collective-permute-done | bytes 524320 | tf_op jit(solution)/shard_map/ppermute | solution.py:231
  118.9 6.5 %convolution_convert_fusion.1 = bf16[256,2048]{1,0:T(8,128)(2,1)S(1)} fusion(bf16[1024,2048]{1,0:T(8,128)(2,1)} %param.25, f32[256,1024]{1,0:T(8,128)} %fusion.43, bf16[256,2048]{1,0:T(8,128)(2,1)} %copy-done.22, bf16[2048,1024]{1,0:T(8,128)(2,1)} %param.24), kind=kOutput, calls=%fused_computation.6 | convolution fusion | flops 2149580800 | bytes 11534336 | tf_op jit(solution)/shard_map/dot_general | solution.py:53
  130.6 4.9 %fusion.42 = f32[256,1024]{1,0:T(8,128)} fusion(bf16[256,2048]{1,0:T(8,128)(2,1)S(1)} %constant_dynamic-update-slice_fusion, bf16[2048,1024]{1,0:T(8,128)(2,1)} %param.23), kind=kOutput, calls=%fused_computation.86 | convolution fusion | flops 1073741824 | bytes 6291456 | tf_op jit(solution)/shard_map/dot_general | solution.py:53
  135.5 11.8 %collective-permute-done.20 = bf16[128,2048]{1,0:T(8,128)(2,1)S(1)} collective-permute-done((bf16[128,2048]{1,0:T(8,128)(2,1)}, bf16[128,2048]{1,0:T(8,128)(2,1)S(1)}, u32[]{:S(2)}, u32[]{:S(2)}) %collective-permute-start.20) | collective-permute-done | bytes 524320 | tf_op jit(solution)/shard_map/ppermute | solution.py:231
  150.6 6.5 %convolution_convert_fusion = bf16[256,2048]{1,0:T(8,128)(2,1)S(1)} fusion(bf16[1024,2048]{1,0:T(8,128)(2,1)} %param.25, f32[256,1024]{1,0:T(8,128)} %fusion.44, bf16[256,2048]{1,0:T(8,128)(2,1)} %copy-done.23, bf16[2048,1024]{1,0:T(8,128)(2,1)} %param.24), kind=kOutput, calls=%fused_computation.5 | convolution fusion | flops 2149580800 | bytes 11534336 | tf_op jit(solution)/shard_map/dot_general | solution.py:53
  158.8 6.5 %convolution_convert_fusion.2 = bf16[256,2048]{1,0:T(8,128)(2,1)S(1)} fusion(bf16[1024,2048]{1,0:T(8,128)(2,1)} %param.25, f32[256,1024]{1,0:T(8,128)} %fusion.42, bf16[256,2048]{1,0:T(8,128)(2,1)} %copy-done.21, bf16[2048,1024]{1,0:T(8,128)(2,1)} %param.24), kind=kOutput, calls=%fused_computation.7 | convolution fusion | flops 2149580800 | bytes 11534336 | tf_op jit(solution)/shard_map/dot_general | solution.py:53
  167.7 4.4 %collective-permute-done.21 = bf16[128,2048]{1,0:T(8,128)(2,1)} collective-permute-done((bf16[128,2048]{1,0:T(8,128)(2,1)}, bf16[128,2048]{1,0:T(8,128)(2,1)}, u32[]{:S(2)}, u32[]{:S(2)}) %collective-permute-start.21) | collective-permute-done | bytes 524320 | tf_op jit(solution)/shard_map/ppermute | solution.py:231
  174.3 3.4 %collective-permute-start.22 = (bf16[128,2048]{1,0:T(8,128)(2,1)}, bf16[128,2048]{1,0:T(8,128)(2,1)}, u32[]{:S(2)}, u32[]{:S(2)}) collective-permute-start(bf16[128,2048]{1,0:T(8,128)(2,1)} %add_convert_fusion.2), channel_id=1, source_target_pairs={{0,8},{4,12},{8,0},{12,4},{16,24},{20,28},{24,16},{28,20},{1,9},{5... | collective-permute-start | bytes 1572872 | tf_op jit(solution)/shard_map/ppermute | solution.py:231
  177.7 6.5 %convolution_convert_fusion.3 = bf16[256,2048]{1,0:T(8,128)(2,1)S(1)} fusion(bf16[1024,2048]{1,0:T(8,128)(2,1)} %param.25, f32[256,1024]{1,0:T(8,128)} %fusion.6, bf16[2048,1024]{1,0:T(8,128)(2,1)} %param.24, bf16[128,2048]{1,0:T(8,128)(2,1)} %copy-done.31, bf16[128,2048]{1,0:T(8,128)(2,1)} %copy-done.19), kind=kOutput, calls=%fused_computation.8 | convolution fusion | flops 2151677952 | bytes 11534336 | tf_op jit(solution)/shard_map/dot_general | solution.py:53
  194.7 3.6 %store_new.1 = (bf16[128,16,128]{2,1,0:T(8,128)(2,1)}, bf16[128,16,128]{2,1,0:T(8,128)(2,1)}) custom-call(s32[128]{0:T(128)S(1)} %bitcast.60, s32[8]{0:T(128)S(1)} %bitcast.62, s32[8]{0:T(128)S(1)} %bitcast.63, bf16[8,128,256]{2,1,0:T(8,128)(2,1)} %all-to-all-done.new, bf16[128,16,128]{2,1,0:T(8,128)(2,1)S(1)} %copy-done.1, bf16[128,16,128]{2,1,0:T(8,128)(2,1)S(1)} %copy-done.2), custom_call_target="tpu_custom_call" | custom-call | tf_op jit(solution)/shard_map/store_new/pallas_call | solution.py:220
  198.3 5.5 %collective-permute-done.15 = bf16[128,2048]{1,0:T(8,128)(2,1)} collective-permute-done((bf16[128,2048]{1,0:T(8,128)(2,1)}, bf16[128,2048]{1,0:T(8,128)(2,1)}, u32[]{:S(2)}, u32[]{:S(2)}) %collective-permute-start.15) | collective-permute-done | bytes 524320 | tf_op jit(solution)/shard_map/ppermute | solution.py:231
  203.7 7.2 %collective-permute-done.23 = bf16[128,2048]{1,0:T(8,128)(2,1)} collective-permute-done((bf16[128,2048]{1,0:T(8,128)(2,1)}, bf16[128,2048]{1,0:T(8,128)(2,1)}, u32[]{:S(2)}, u32[]{:S(2)}) %collective-permute-start.23) | collective-permute-done | bytes 524320 | tf_op jit(solution)/shard_map/ppermute | solution.py:231
  211.0 2.7 %add_convert_fusion = bf16[128,2048]{1,0:T(8,128)(2,1)} fusion(f32[128,2048]{1,0:T(8,128)S(1)} %copy-done.12, bf16[128,2048]{1,0:T(8,128)(2,1)} %collective-permute-done.23, bf16[128,2048]{1,0:T(8,128)(2,1)} %collective-permute-done.15, bf16[128,2048]{1,0:T(8,128)(2,1)} %collective-permute-done.11, bf16[256,2048]{1,0:T(8,128)(2,1)} %copy-done.14), kind=kLoop, calls=%fused_computation.19 | loop fusion | flops 2621440 | bytes 3670016 | tf_op jit(solution)/shard_map/convert_element_type | solution.py:339
  (143 shorter events, 62.3 us)
Async XLA Ops:
  3.6 18.8 %collective-permute-start = (bf16[528,128]{1,0:T(8,128)(2,1)}, bf16[528,128]{1,0:T(8,128)(2,1)}, u32[]{:S(2)}, u32[]{:S(2)}) collective-permute-start(bf16[528,128]{1,0:T(8,128)(2,1)} %get-tuple-element.16), channel_id=1, source_target_pairs={{0,4},{4,0},{8,12},{12,8},{16,20},{20,16},{24,28},{28,24},{1,5},{5... | collective-permute-start | bytes 405512 | tf_op jit(solution)/shard_map/ppermute | solution.py:231
  6.6 20.4 %collective-permute-start.1 = (bf16[528,128]{1,0:T(8,128)(2,1)}, bf16[528,128]{1,0:T(8,128)(2,1)}, u32[]{:S(2)}, u32[]{:S(2)}) collective-permute-start(bf16[528,128]{1,0:T(8,128)(2,1)} %get-tuple-element.17), channel_id=1, source_target_pairs={{0,8},{4,12},{8,0},{12,4},{16,24},{20,28},{24,16},{28,20},{1,9},{5... | collective-permute-start | bytes 405512 | tf_op jit(solution)/shard_map/ppermute | solution.py:231
  8.2 19.9 %collective-permute-start.2 = (bf16[528,128]{1,0:T(8,128)(2,1)}, bf16[528,128]{1,0:T(8,128)(2,1)}, u32[]{:S(2)}, u32[]{:S(2)}) collective-permute-start(bf16[528,128]{1,0:T(8,128)(2,1)} %get-tuple-element.18), channel_id=1, source_target_pairs={{0,12},{4,8},{8,4},{12,0},{16,28},{20,24},{24,20},{28,16},{1,13},{... | collective-permute-start | bytes 405512 | tf_op jit(solution)/shard_map/ppermute | solution.py:231
  8.2 20.8 %collective-permute-start.3 = (bf16[528,128]{1,0:T(8,128)(2,1)}, bf16[528,128]{1,0:T(8,128)(2,1)}, u32[]{:S(2)}, u32[]{:S(2)}) collective-permute-start(bf16[528,128]{1,0:T(8,128)(2,1)} %get-tuple-element.19), channel_id=1, source_target_pairs={{0,16},{4,20},{8,24},{12,28},{16,0},{20,4},{24,8},{28,12},{1,17},{... | collective-permute-start | bytes 405512 | tf_op jit(solution)/shard_map/ppermute | solution.py:231
  11.2 18.8 %collective-permute-start.4 = (bf16[528,128]{1,0:T(8,128)(2,1)}, bf16[528,128]{1,0:T(8,128)(2,1)}, u32[]{:S(2)}, u32[]{:S(2)}) collective-permute-start(bf16[528,128]{1,0:T(8,128)(2,1)} %get-tuple-element.20), channel_id=1, source_target_pairs={{0,20},{4,16},{8,28},{12,24},{16,4},{20,0},{24,12},{28,8},{1,21},{... | collective-permute-start | bytes 405512 | tf_op jit(solution)/shard_map/ppermute | solution.py:231
  22.5 8.4 %collective-permute-start.5 = (bf16[528,128]{1,0:T(8,128)(2,1)}, bf16[528,128]{1,0:T(8,128)(2,1)S(1)}, u32[]{:S(2)}, u32[]{:S(2)}) collective-permute-start(bf16[528,128]{1,0:T(8,128)(2,1)} %get-tuple-element.21), channel_id=1, source_target_pairs={{0,24},{4,28},{8,16},{12,20},{16,8},{20,12},{24,0},{28,4},{1,25},{... | collective-permute-start | bytes 405512 | tf_op jit(solution)/shard_map/ppermute | solution.py:231
  27.1 8.1 %collective-permute-start.6 = (bf16[528,128]{1,0:T(8,128)(2,1)}, bf16[528,128]{1,0:T(8,128)(2,1)S(1)}, u32[]{:S(2)}, u32[]{:S(2)}) collective-permute-start(bf16[528,128]{1,0:T(8,128)(2,1)} %get-tuple-element.22), channel_id=1, source_target_pairs={{0,28},{4,24},{8,20},{12,16},{16,12},{20,8},{24,4},{28,0},{1,29},{... | collective-permute-start | bytes 405512 | tf_op jit(solution)/shard_map/ppermute | solution.py:231
  52.5 4.0 %collective-permute-start.7 = (bf16[128,2048]{1,0:T(8,128)(2,1)}, bf16[128,2048]{1,0:T(8,128)(2,1)S(1)}, u32[]{:S(2)}, u32[]{:S(2)}) collective-permute-start(bf16[128,2048]{1,0:T(8,128)(2,1)} %convolution_convert_fusion.6), channel_id=1, source_target_pairs={{0,1},{1,0},{2,3},{3,2},{4,5},{5,4},{6,7},{7,6},{8,9},{9,8},{10,11... | collective-permute-start | bytes 1572872 | tf_op jit(solution)/shard_map/ppermute | solution.py:231
  53.7 14.1 %collective-permute-start.9 = (bf16[128,2048]{1,0:T(8,128)(2,1)S(1)}, bf16[128,2048]{1,0:T(8,128)(2,1)}, u32[]{:S(2)}, u32[]{:S(2)}) collective-permute-start(bf16[128,2048]{1,0:T(8,128)(2,1)S(1)} %add_convert_fusion.4), channel_id=1, source_target_pairs={{0,2},{1,3},{2,0},{3,1},{4,6},{5,7},{6,4},{7,5},{8,10},{9,11},{10,... | collective-permute-start | bytes 1572872 | tf_op jit(solution)/shard_map/ppermute | solution.py:231
  70.6 27.8 %collective-permute-start.16 = (bf16[128,2048]{1,0:T(8,128)(2,1)S(1)}, bf16[128,2048]{1,0:T(8,128)(2,1)}, u32[]{:S(2)}, u32[]{:S(2)}) collective-permute-start(bf16[128,2048]{1,0:T(8,128)(2,1)S(1)} %multiply_convert_fusion.4), channel_id=1, source_target_pairs={{0,16},{4,20},{8,24},{12,28},{16,0},{20,4},{24,8},{28,12},{1,17},{... | collective-permute-start | bytes 1572872 | tf_op jit(solution)/shard_map/ppermute | solution.py:231
  74.4 27.7 %collective-permute-start.12 = (bf16[128,2048]{1,0:T(8,128)(2,1)S(1)}, bf16[128,2048]{1,0:T(8,128)(2,1)}, u32[]{:S(2)}, u32[]{:S(2)}) collective-permute-start(bf16[128,2048]{1,0:T(8,128)(2,1)S(1)} %multiply_convert_fusion.4), channel_id=1, source_target_pairs={{0,8},{4,12},{8,0},{12,4},{16,24},{20,28},{24,16},{28,20},{1,9},{5... | collective-permute-start | bytes 1572872 | tf_op jit(solution)/shard_map/ppermute | solution.py:231
  74.4 29.6 %collective-permute-start.10 = (bf16[128,2048]{1,0:T(8,128)(2,1)S(1)}, bf16[128,2048]{1,0:T(8,128)(2,1)S(1)}, u32[]{:S(2)}, u32[]{:S(2)}) collective-permute-start(bf16[128,2048]{1,0:T(8,128)(2,1)S(1)} %multiply_convert_fusion.4), channel_id=1, source_target_pairs={{0,4},{4,0},{8,12},{12,8},{16,20},{20,16},{24,28},{28,24},{1,5},{5... | collective-permute-start | bytes 1572872 | tf_op jit(solution)/shard_map/ppermute | solution.py:231
  75.5 119.2 %all-to-all-start = ((bf16[8,128,256]{2,1,0:T(8,128)(2,1)}), bf16[8,128,256]{2,1,0:T(8,128)(2,1)}, u32[]{:S(2)}, u32[]{:S(2)}) async-start(bf16[8,128,256]{2,1,0:T(8,128)(2,1)} %get-tuple-element.24), calls=%async_computation | async-start | bytes 1048576 | tf_op jit(solution)/shard_map/all_to_all | solution.py:326
  98.3 29.1 %collective-permute-start.19 = (bf16[128,2048]{1,0:T(8,128)(2,1)}, bf16[128,2048]{1,0:T(8,128)(2,1)}, u32[]{:S(2)}, u32[]{:S(2)}) collective-permute-start(bf16[128,2048]{1,0:T(8,128)(2,1)} %collective-permute-done.16), channel_id=1, source_target_pairs={{0,8},{4,12},{8,0},{12,4},{16,24},{20,28},{24,16},{28,20},{1,9},{5... | collective-permute-start | bytes 1572872 | tf_op jit(solution)/shard_map/ppermute | solution.py:231
  98.3 17.3 %collective-permute-start.17 = (bf16[128,2048]{1,0:T(8,128)(2,1)}, bf16[128,2048]{1,0:T(8,128)(2,1)S(1)}, u32[]{:S(2)}, u32[]{:S(2)}) collective-permute-start(bf16[128,2048]{1,0:T(8,128)(2,1)} %collective-permute-done.16), channel_id=1, source_target_pairs={{0,4},{4,0},{8,12},{12,8},{16,20},{20,16},{24,28},{28,24},{1,5},{5... | collective-permute-start | bytes 1572872 | tf_op jit(solution)/shard_map/ppermute | solution.py:231
  104.0 25.5 %collective-permute-start.13 = (bf16[128,2048]{1,0:T(8,128)(2,1)}, bf16[128,2048]{1,0:T(8,128)(2,1)}, u32[]{:S(2)}, u32[]{:S(2)}) collective-permute-start(bf16[128,2048]{1,0:T(8,128)(2,1)} %collective-permute-done.12), channel_id=1, source_target_pairs={{0,4},{4,0},{8,12},{12,8},{16,20},{20,16},{24,28},{28,24},{1,5},{5... | collective-permute-start | bytes 1572872 | tf_op jit(solution)/shard_map/ppermute | solution.py:231
  126.3 62.0 %collective-permute-start.18 = (bf16[128,2048]{1,0:T(8,128)(2,1)}, bf16[128,2048]{1,0:T(8,128)(2,1)}, u32[]{:S(2)}, u32[]{:S(2)}) collective-permute-start(bf16[128,2048]{1,0:T(8,128)(2,1)} %slice.58), channel_id=1, source_target_pairs={{0,4},{4,0},{8,12},{12,8},{16,20},{20,16},{24,28},{28,24},{1,5},{5... | collective-permute-start | bytes 1572872 | tf_op jit(solution)/shard_map/ppermute | solution.py:231
  127.5 19.8 %collective-permute-start.20 = (bf16[128,2048]{1,0:T(8,128)(2,1)}, bf16[128,2048]{1,0:T(8,128)(2,1)S(1)}, u32[]{:S(2)}, u32[]{:S(2)}) collective-permute-start(bf16[128,2048]{1,0:T(8,128)(2,1)} %collective-permute-done.19), channel_id=1, source_target_pairs={{0,4},{4,0},{8,12},{12,8},{16,20},{20,16},{24,28},{28,24},{1,5},{5... | collective-permute-start | bytes 1572872 | tf_op jit(solution)/shard_map/ppermute | solution.py:231
  158.3 13.8 %collective-permute-start.21 = (bf16[128,2048]{1,0:T(8,128)(2,1)}, bf16[128,2048]{1,0:T(8,128)(2,1)}, u32[]{:S(2)}, u32[]{:S(2)}) collective-permute-start(bf16[128,2048]{1,0:T(8,128)(2,1)} %slice.60), channel_id=1, source_target_pairs={{0,4},{4,0},{8,12},{12,8},{16,20},{20,16},{24,28},{28,24},{1,5},{5... | collective-permute-start | bytes 1572872 | tf_op jit(solution)/shard_map/ppermute | solution.py:231
  166.3 19.8 %collective-permute-start.14 = (bf16[128,2048]{1,0:T(8,128)(2,1)}, bf16[128,2048]{1,0:T(8,128)(2,1)}, u32[]{:S(2)}, u32[]{:S(2)}) collective-permute-start(bf16[128,2048]{1,0:T(8,128)(2,1)} %slice.56), channel_id=1, source_target_pairs={{0,4},{4,0},{8,12},{12,8},{16,20},{20,16},{24,28},{28,24},{1,5},{5... | collective-permute-start | bytes 1572872 | tf_op jit(solution)/shard_map/ppermute | solution.py:231
  174.3 16.5 %collective-permute-start.22 = (bf16[128,2048]{1,0:T(8,128)(2,1)}, bf16[128,2048]{1,0:T(8,128)(2,1)}, u32[]{:S(2)}, u32[]{:S(2)}) collective-permute-start(bf16[128,2048]{1,0:T(8,128)(2,1)} %add_convert_fusion.2), channel_id=1, source_target_pairs={{0,8},{4,12},{8,0},{12,4},{16,24},{20,28},{24,16},{28,20},{1,9},{5... | collective-permute-start | bytes 1572872 | tf_op jit(solution)/shard_map/ppermute | solution.py:231
  186.0 12.3 %collective-permute-start.11 = (bf16[128,2048]{1,0:T(8,128)(2,1)}, bf16[128,2048]{1,0:T(8,128)(2,1)}, u32[]{:S(2)}, u32[]{:S(2)}) collective-permute-start(bf16[128,2048]{1,0:T(8,128)(2,1)} %slice.54), channel_id=1, source_target_pairs={{0,4},{4,0},{8,12},{12,8},{16,20},{20,16},{24,28},{28,24},{1,5},{5... | collective-permute-start | bytes 1572872 | tf_op jit(solution)/shard_map/ppermute | solution.py:231
  188.3 15.4 %collective-permute-start.15 = (bf16[128,2048]{1,0:T(8,128)(2,1)}, bf16[128,2048]{1,0:T(8,128)(2,1)}, u32[]{:S(2)}, u32[]{:S(2)}) collective-permute-start(bf16[128,2048]{1,0:T(8,128)(2,1)} %add_convert_fusion.3), channel_id=1, source_target_pairs={{0,8},{4,12},{8,0},{12,4},{16,24},{20,28},{24,16},{28,20},{1,9},{5... | collective-permute-start | bytes 1572872 | tf_op jit(solution)/shard_map/ppermute | solution.py:231
  193.0 18.0 %collective-permute-start.23 = (bf16[128,2048]{1,0:T(8,128)(2,1)}, bf16[128,2048]{1,0:T(8,128)(2,1)}, u32[]{:S(2)}, u32[]{:S(2)}) collective-permute-start(bf16[128,2048]{1,0:T(8,128)(2,1)} %add_convert_fusion.1), channel_id=1, source_target_pairs={{0,16},{4,20},{8,24},{12,28},{16,0},{20,4},{24,8},{28,12},{1,17},{... | collective-permute-start | bytes 1572872 | tf_op jit(solution)/shard_map/ppermute | solution.py:231
  (34 other events, 304.7 us)

commit v2 on v1

v2 whole, which is shorter than its diff:
```python
import functools

import jax
import jax.numpy as jnp
from jax import lax
from jax.experimental import pallas as pl
from jax.experimental.pallas import tpu as pltpu
from jax.sharding import PartitionSpec as P

HD = 64
PAGE = 16
MAXP = 16
CONTEXT = 256
LANES = 128
INFO = 16


EPSILON = 1e-05
RESIDUAL_MULT = 0.22
SCORE_MULT = 0.015625
ROPE_BASE = 10000000.0
LOG2E = 1.4426950408889634
BF = jnp.bfloat16
F32 = jnp.float32
SMEM = pl.BlockSpec(memory_space=pltpu.SMEM)
VMEM = pl.BlockSpec(memory_space=pltpu.VMEM)
SMALL = pl.CostEstimate(flops=0, bytes_accessed=0, transcendentals=0)


def normalize(values, gain):
    mean_square = jnp.mean(values * values, axis=-1, keepdims=True)
    return values * lax.rsqrt(mean_square + EPSILON) * gain


def rope_tables(length):
    lane = jnp.arange(LANES, dtype=jnp.int32)
    half = HD // 2
    freq = jnp.power(ROPE_BASE, -2.0 * (lane % half).astype(F32) / HD)
    angle = jnp.arange(length, dtype=jnp.int32).astype(F32)[:, None] * freq
    sign = jnp.where(lane % HD < half, -1.0, 1.0).astype(F32)
    return jnp.cos(angle), jnp.sin(angle) * sign


def rotate(values, cosine, sine):
    lane = lax.broadcasted_iota(jnp.int32, values.shape, 1)
    swapped = jnp.where(
        lane % HD < HD // 2,
        pltpu.roll(values, LANES - HD // 2, 1),
        pltpu.roll(values, HD // 2, 1),
    )
    return values * cosine + swapped * sine


def dot(a, b):
    return jnp.dot(a, b, preferred_element_type=F32)


def pack_kernel(table, prior, cache_k, cache_v, out):
    for source in range(out.shape[0]):
        for page in range(MAXP):
            at = table[source * MAXP + page]
            out[source, page * PAGE : (page + 1) * PAGE, :] = cache_k[at]
            out[source, CONTEXT + page * PAGE : CONTEXT + (page + 1) * PAGE, :] = cache_v[at]
        info = jnp.full((INFO, LANES), prior[source].astype(F32), F32)
        out[source, 2 * CONTEXT :, :] = info.astype(BF)


def pack_pages(table, prior, cache_k, cache_v):
    peers = prior.shape[0]
    return pl.pallas_call(
        pack_kernel,
        out_shape=jax.ShapeDtypeStruct((peers, 2 * CONTEXT + INFO, LANES), BF),
        in_specs=[SMEM, SMEM, VMEM, VMEM],
        out_specs=VMEM,
        compiler_params=pltpu.CompilerParams(vmem_limit_bytes=60 * 1024 * 1024),
        name="pack_pages",
        cost_estimate=SMALL,
    )(table, prior, cache_k, cache_v)


def one_hot(shape, start, count, slot_axis):
    slot = lax.broadcasted_iota(jnp.int32, shape, slot_axis)
    row = lax.broadcasted_iota(jnp.int32, shape, 1 - slot_axis)
    return jnp.where((row == slot + start) & (slot < count), 1.0, 0.0).astype(BF)


def project_kernel(starts, counts, hidden, gain, w_query, w_key, w_value, queries, news, whole):
    step = pl.program_id(0)
    rows = hidden.shape[0]
    qcols = w_query.shape[1]
    peers, pair, _ = queries.shape
    normed = normalize(hidden[...].astype(F32), gain[...]).astype(BF)
    here = pl.ds(pl.multiple_of(step * rows, rows), rows)
    whole[here, :qcols] = dot(normed, w_query[...]).astype(BF)
    whole[here, qcols : qcols + LANES] = dot(normed, w_key[...]).astype(BF)
    whole[here, qcols + LANES :] = dot(normed, w_value[...]).astype(BF)

    @pl.when(step == pl.num_programs(0) - 1)
    def _():
        def request(owner, carry):
            pick = one_hot((pair, whole.shape[0]), starts[owner], counts[owner], 0)
            slots = dot(pick, whole[...]).astype(BF)
            queries[owner] = slots[:, :qcols]
            news[owner] = slots[:, qcols:]
            return carry

        lax.fori_loop(0, peers, request, 0)


def project(starts, counts, hidden, gain, w_query, w_key, w_value, pair):
    rows, width = hidden.shape
    peers = starts.shape[0]
    qcols = w_query.shape[1]
    steps = 2
    whole = lambda step, *_: (0, 0)
    every = lambda step, *_: (0, 0, 0)
    return pl.pallas_call(
        project_kernel,
        out_shape=[
            jax.ShapeDtypeStruct((peers, pair, qcols), BF),
            jax.ShapeDtypeStruct((peers, pair, 2 * LANES), BF),
        ],
        grid_spec=pltpu.PrefetchScalarGridSpec(
            num_scalar_prefetch=2,
            grid=(steps,),
            in_specs=[
                pl.BlockSpec((rows // steps, width), lambda step, *_: (step, 0)),
                pl.BlockSpec((1, width), whole),
                pl.BlockSpec(w_query.shape, whole),
                pl.BlockSpec(w_key.shape, whole),
                pl.BlockSpec(w_value.shape, whole),
            ],
            out_specs=[
                pl.BlockSpec((peers, pair, qcols), every),
                pl.BlockSpec((peers, pair, 2 * LANES), every),
            ],
            scratch_shapes=[pltpu.VMEM((rows, qcols + 2 * LANES), BF)],
        ),
        compiler_params=pltpu.CompilerParams(
            vmem_limit_bytes=32 * 1024 * 1024, dimension_semantics=("arbitrary",)
        ),
        name="project",
        cost_estimate=SMALL,
    )(starts, counts, hidden, gain.reshape(1, width), w_query, w_key, w_value)


def attention_kernel(
    starts, counts, group, query, new, pages, cosines, sines, mixed, total
):
    step = pl.program_id(0)
    start, count = starts[step], counts[step]
    _, pair, qcols = query.shape
    rows = total.shape[0]
    parts = mixed.shape[0]
    quarter = rows // parts

    def span(part):
        return pl.ds(pl.multiple_of((group[0] ^ part) * quarter, quarter), quarter)

    @pl.when(step == 0)
    def _():
        total[...] = jnp.zeros_like(total)

    @pl.when(count > 0)
    def _():
        info = pages[0, 2 * CONTEXT :, :].astype(F32)
        prior = jnp.max(info).astype(jnp.int32)
        cosine = cosines[pl.ds(prior, pair), :]
        sine = sines[pl.ds(prior, pair), :]
        new_key = rotate(new[0, :, :LANES].astype(F32), cosine, sine).astype(BF)
        new_value = new[0, :, LANES:]

        place = lax.broadcasted_iota(jnp.int32, (CONTEXT, pair), 0)
        new_slot = lax.broadcasted_iota(jnp.int32, (CONTEXT, pair), 1)
        put = jnp.where((place == new_slot + prior) & (new_slot < count), 1.0, 0.0).astype(BF)
        position = lax.broadcasted_iota(jnp.int32, (CONTEXT, LANES), 0)
        lane = lax.broadcasted_iota(jnp.int32, (CONTEXT, LANES), 1)
        low = lane < HD

        def merged(fresh, old):
            whole = jnp.where(position < prior, old.astype(F32), dot(put, fresh))
            turned = pltpu.roll(whole, HD, 1)
            return (
                jnp.where(low, whole, turned).astype(BF),
                jnp.where(low, turned, whole).astype(BF),
            )

        keys = merged(new_key, pages[0, :CONTEXT, :])
        values = merged(new_value, pages[0, CONTEXT : 2 * CONTEXT, :])

        query_slot = lax.broadcasted_iota(jnp.int32, (2 * pair, CONTEXT), 0)
        query_slot = jnp.where(query_slot >= pair, query_slot - pair, query_slot)
        at = lax.broadcasted_iota(jnp.int32, (2 * pair, CONTEXT), 1)
        allowed = at <= query_slot + prior
        left = lax.broadcasted_iota(jnp.int32, (pair, LANES), 1) < HD
        tiles = qcols // LANES
        outs = []
        for tile in range(tiles):
            kv = tile * 2 // tiles
            turned = rotate(query[0, :, tile * LANES : (tile + 1) * LANES].astype(F32), cosine, sine)
            both = jnp.concatenate([jnp.where(left, turned, 0.0), jnp.where(left, 0.0, turned)], 0)
            score = lax.dot_general(
                both.astype(BF), keys[kv], (((1,), (1,)), ((), ())), preferred_element_type=F32
            )
            score = jnp.where(allowed, score, -1e30)
            score = score - jnp.max(score, axis=-1, keepdims=True)
            weight = jnp.exp2(score * (SCORE_MULT * LOG2E))
            share = 1.0 / jnp.sum(weight, axis=-1, keepdims=True)
            probs = (weight * share).astype(BF)
            out = dot(probs, values[kv])
            outs.append(jnp.where(left, out[:pair], out[pair:]).astype(BF))
        block = jnp.concatenate(outs, axis=1)
        total[...] += dot(one_hot((rows, pair), start, count, 1), block)

    @pl.when(step == pl.num_programs(0) - 1)
    def _():
        for part in range(parts):
            mixed[part] = total[span(part), :].astype(BF)


def attend(starts, counts, group, query, new, pages, cosines, sines, rows, parts):
    peers, pair, qcols = query.shape
    whole = lambda step, *_: (0, 0)
    here = lambda step, *_: (step, 0, 0)
    result = (parts, rows // parts, qcols)
    return pl.pallas_call(
        attention_kernel,
        out_shape=jax.ShapeDtypeStruct(result, BF),
        grid_spec=pltpu.PrefetchScalarGridSpec(
            num_scalar_prefetch=3,
            grid=(peers,),
            in_specs=[
                pl.BlockSpec((1, pair, qcols), here),
                pl.BlockSpec((1, pair, 2 * LANES), here),
                pl.BlockSpec((1,) + pages.shape[1:], here),
                pl.BlockSpec(cosines.shape, whole),
                pl.BlockSpec(sines.shape, whole),
            ],
            out_specs=pl.BlockSpec(result, lambda step, *_: (0, 0, 0)),
            scratch_shapes=[pltpu.VMEM((rows, qcols), F32)],
        ),
        compiler_params=pltpu.CompilerParams(
            vmem_limit_bytes=32 * 1024 * 1024, dimension_semantics=("arbitrary",)
        ),
        name="attend",
        cost_estimate=SMALL,
    )(starts, counts, group, query, new, pages, cosines, sines)


def store_kernel(
    table, priors, counts, new, cosines, sines, cache_k, cache_v, keys_out, values_out
):
    peers, pair, _ = new.shape
    keys_out[...] = cache_k[...]
    values_out[...] = cache_v[...]

    def request(source, carry):
        prior, count = priors[source], counts[source]
        place = lax.broadcasted_iota(jnp.int32, (CONTEXT, pair), 0)
        slot = lax.broadcasted_iota(jnp.int32, (CONTEXT, pair), 1)
        put = jnp.where((place == slot + prior) & (slot < count), 1.0, 0.0).astype(BF)
        cosine = cosines[pl.ds(prior, pair), :]
        sine = sines[pl.ds(prior, pair), :]
        new_key = rotate(new[source, :, :LANES].astype(F32), cosine, sine).astype(BF)
        moved = dot(put, jnp.concatenate([new_key, new[source, :, LANES:]], axis=1))
        position = lax.broadcasted_iota(jnp.int32, (PAGE, LANES), 0)
        for page in range(MAXP):
            at = table[source * MAXP + page]
            here = position + page * PAGE
            fresh = (here >= prior) & (here < prior + count)
            rows = moved[page * PAGE : (page + 1) * PAGE]
            keys_out[at] = jnp.where(fresh, rows[:, :LANES], cache_k[at].astype(F32)).astype(BF)
            values_out[at] = jnp.where(fresh, rows[:, LANES:], cache_v[at].astype(F32)).astype(BF)
        return carry

    lax.fori_loop(0, peers, request, 0)


def store_new(table, priors, counts, new, cosines, sines, cache_k, cache_v):
    return pl.pallas_call(
        store_kernel,
        out_shape=[jax.ShapeDtypeStruct(cache_k.shape, BF)] * 2,
        in_specs=[SMEM] * 3 + [VMEM] * 5,
        out_specs=[VMEM] * 2,
        compiler_params=pltpu.CompilerParams(vmem_limit_bytes=32 * 1024 * 1024),
        name="store_new",
        cost_estimate=SMALL,
    )(table, priors, counts, new, cosines, sines, cache_k, cache_v)


def swap(values, axis, size, bit):
    return lax.ppermute(values, axis, [(at, at ^ bit) for at in range(size)])


def feed_forward(rows, w_gate, w_up, w_down):
    gate = dot(rows, w_gate)
    upper = dot(rows, w_up)
    hidden = (jax.nn.silu(gate) * upper).astype(BF)
    return dot(hidden, w_down).astype(BF)


UNIT_TILE = 256
COLUMN_TILE = 512
HBM = pl.BlockSpec(memory_space=pltpu.HBM)
ROOM = pltpu.CompilerParams(vmem_limit_bytes=16 * 1024 * 1024)


def up_kernel(mine, theirs, gate, upper, mine_out, theirs_out, stack, sems):
    unit = mine.shape[0]
    copies = [
        pltpu.make_async_copy(ref, stack.at[pl.ds(at * unit, unit)], sems.at[at])
        for at, ref in enumerate((mine, theirs))
    ]
    for copy in copies:
        copy.start()
    for copy in copies:
        copy.wait()

    def work(tile, carry):
        span = pl.ds(pl.multiple_of(tile * UNIT_TILE, UNIT_TILE), UNIT_TILE)
        both = dot(stack[...], jnp.concatenate([gate[:, span], upper[:, span]], axis=1))
        hidden = (jax.nn.silu(both[:, :UNIT_TILE]) * both[:, UNIT_TILE:]).astype(BF)
        mine_out[:, span] = hidden[:unit]
        theirs_out[:, span] = hidden[unit:]
        return carry

    lax.fori_loop(0, gate.shape[1] // UNIT_TILE, work, 0)


def mlp_up(mine, theirs, gate, upper):
    unit, width = mine.shape
    return pl.pallas_call(
        up_kernel,
        out_shape=[jax.ShapeDtypeStruct((unit, gate.shape[1]), BF)] * 2,
        in_specs=[HBM, HBM, VMEM, VMEM],
        out_specs=[VMEM] * 2,
        scratch_shapes=[pltpu.VMEM((2 * unit, width), BF), pltpu.SemaphoreType.DMA((2,))],
        compiler_params=ROOM,
        cost_estimate=SMALL,
        name="mlp_up",
    )(mine, theirs, gate, upper)


def down_kernel(count, group, *refs):
    hidden, side, down = refs[:3]
    pieces, outs, stack = refs[3 : 3 + count], refs[3 + count : -1], refs[-1]
    units = hidden.shape[1]
    size = units // count
    stack[:, :units] = hidden[...]
    for at in range(count):
        start = pl.multiple_of((group[0] ^ at) * size, size)
        stack[:, units + at * size : units + (at + 1) * size] = side[:, pl.ds(start, size)]

    def work(tile, carry):
        span = pl.ds(pl.multiple_of(tile * COLUMN_TILE, COLUMN_TILE), COLUMN_TILE)
        weights = jnp.concatenate([down[:, span]] + [ref[:, span] for ref in pieces], axis=0)
        total = dot(stack[...], weights).astype(BF)
        at = 0
        for ref in outs:
            ref[:, span] = total[at : at + ref.shape[0]]
            at += ref.shape[0]
        return carry

    lax.fori_loop(0, down.shape[1] // COLUMN_TILE, work, 0)


def mlp_down(group, hidden, side, down, pieces, sizes):
    many, units = hidden.shape
    width = down.shape[1]
    return pl.pallas_call(
        functools.partial(down_kernel, len(pieces)),
        out_shape=[jax.ShapeDtypeStruct((size, width), BF) for size in sizes],
        in_specs=[SMEM] + [VMEM] * (3 + len(pieces)),
        out_specs=[VMEM] * len(sizes),
        scratch_shapes=[pltpu.VMEM((many, 2 * units), BF)],
        compiler_params=ROOM,
        cost_estimate=SMALL,
        name="mlp_down",
    )(group, hidden, side, down, *pieces)


def after(value, *others):
    return lax.optimization_barrier((value,) + others)[0]


def rows_of(w, index, count):
    size = w.shape[0] // count
    return lax.dynamic_slice_in_dim(w, index * size, size, 0)


def sync(*values):
    return lax.optimization_barrier(values)


def exchange_mlp(own, new, peers, groups, group, held, side_down):
    send = functools.partial(swap, axis="req", size=peers)
    cross = functools.partial(swap, axis="grp", size=groups, bit=1)
    over = functools.partial(swap, axis="grp", size=groups, bit=2)
    add = lambda *terms: sum(term.astype(F32) for term in terms)
    join = lambda *blocks: jnp.concatenate(blocks, axis=0)
    up = lambda mine, theirs: mlp_up(mine, theirs, held[0], held[1])
    unit = own.shape[0]
    half = unit // 2
    own_a, own_b = own[:half], own[half:]

    far_a = send(own_a, bit=4)
    near = send(own, bit=2)
    side_own = send(own, bit=1)
    far_a, near, side_own = sync(far_a, near, side_own)
    far_b = send(after(own_b, far_a), bit=4)
    both_a = send(far_a, bit=2)
    side_near = send(near, bit=1)
    over_down = over(after(side_down, far_a))
    hidden_own, theirs_own = up(own, side_own)
    far_b, both_a, side_near, new, _ = sync(far_b, both_a, side_near, new, hidden_own)
    both_b = send(far_b, bit=2)
    rows_a = join(far_a, both_a)
    side_a = send(rows_a, bit=1)
    hidden_near, theirs_near = up(near, side_near)
    both_b, side_a, over_down, _ = sync(both_b, side_a, over_down, hidden_near)
    rows_b = join(far_b, both_b)
    side_b = send(rows_b, bit=1)
    pieces = [side_down, cross(side_down), over_down, cross(over_down)]
    down = lambda hidden, side, sizes: mlp_down(group, hidden, side, held[2], pieces, sizes)
    hidden_a, theirs_a = up(rows_a, side_a)
    side_b, hidden_a, theirs_a = sync(side_b, hidden_a, theirs_a)
    from_a = send(theirs_a, bit=1)
    hidden_b, theirs_b = up(rows_b, side_b)
    from_b = send(theirs_b, bit=1)
    from_a, _ = sync(from_a, hidden_b)
    sum_far_a, sum_both_a = down(hidden_a, from_a, [half, half])
    back_both_a = send(sum_both_a, bit=2)
    from_b, _ = sync(from_b, sum_far_a)
    from_near = send(after(theirs_near, from_b), bit=1)
    sum_far_b, sum_both_b = down(hidden_b, from_b, [half, half])
    back_both_b = send(sum_both_b, bit=2)
    back_both_a, _ = sync(back_both_a, sum_far_b)
    total_a = add(sum_far_a, back_both_a).astype(BF)
    back_far_a = send(total_a, bit=4)
    back_both_b, _ = sync(back_both_b, total_a)
    total_b = add(sum_far_b, back_both_b).astype(BF)
    back_far_b = send(total_b, bit=4)
    from_own = send(after(theirs_own, from_near), bit=1)
    (sum_near,) = down(after(hidden_near, total_a), from_near, [unit])
    back_near = send(sum_near, bit=2)
    (sum_own,) = down(hidden_own, from_own, [unit])
    return new, add(sum_own, back_near, join(back_far_a, back_far_b))


def body(
    hidden_in,
    attn_gain,
    mlp_gain,
    w_query,
    w_key,
    w_value,
    w_out,
    w_gate,
    w_up,
    w_down,
    cache_k,
    cache_v,
    owner_of_row,
    new_len,
    prior_len,
    page_table,
):
    peers = lax.axis_size("req")
    groups = lax.axis_size("grp")
    row_count = hidden_in.shape[0]
    pair = 2 * row_count // peers
    quarter = row_count // groups
    group_index = lax.axis_index("grp")
    owners = jnp.arange(peers, dtype=jnp.int32)

    member = owner_of_row[None, :] == owners[:, None]
    counts = jnp.sum(member.astype(jnp.int32), axis=1)
    row_ids = jnp.arange(row_count, dtype=jnp.int32)
    starts = jnp.min(jnp.where(member, row_ids[None, :], row_count), axis=1)
    cosines, sines = rope_tables(CONTEXT + pair)

    group = group_index.reshape(1)
    packed = pack_pages(page_table[0], prior_len[0], cache_k, cache_v)
    pages = lax.all_to_all(packed, "req", split_axis=0, concat_axis=0, tiled=True)
    query, fresh = project(starts, counts, hidden_in, attn_gain, w_query, w_key, w_value, pair)
    if peers == 8:
        side_down = swap(after(rows_of(w_down, group_index, groups), fresh), "req", peers, 1)
    mixed = attend(
        starts, counts, group, query, fresh, pages, cosines, sines, row_count, groups
    )
    if peers == 8:
        mixed, side_down = sync(mixed, side_down)

    out_of = lambda part: dot(mixed[part], w_out).astype(BF)
    to_home = functools.partial(swap, axis="grp", size=groups)
    cross = to_home(out_of(3), bit=1)
    beside = to_home(out_of(1), bit=1)
    over = (out_of(2).astype(F32) + cross.astype(F32)).astype(BF)
    new = lax.all_to_all(after(fresh, over), "req", split_axis=0, concat_axis=0, tiled=True)
    over = to_home(over, bit=2)
    attn_sum = out_of(0).astype(F32) + beside.astype(F32) + over.astype(F32)
    own_rows = lax.dynamic_slice_in_dim(hidden_in, group_index * quarter, quarter, 0).astype(F32)
    residual = own_rows + RESIDUAL_MULT * attn_sum
    own = normalize(residual, mlp_gain).astype(BF)
    if peers == 8:
        held = [w_gate, w_up, w_down]
        new, down = exchange_mlp(own, new, peers, groups, group, held, side_down)
    else:
        piece = lax.all_gather(own, "req", axis=0, tiled=True)
        part = feed_forward(piece, w_gate, w_up, w_down)
        down = lax.psum_scatter(part, "req", scatter_dimension=0, tiled=True).astype(F32)
    keys_out, values_out = store_new(page_table[0], prior_len[0], new_len[0], new, cosines, sines, cache_k, cache_v)
    layer_out = (residual + RESIDUAL_MULT * down).astype(BF)
    return (layer_out, keys_out, values_out)


def solution(mesh):
    in_specs = (
        P("req", None),
        P(),
        P(),
        P(None, "grp"),
        P(None, "grp"),
        P(None, "grp"),
        P("grp", None),
        P(None, "req"),
        P(None, "req"),
        P("req", None),
        P("req", None, "grp"),
        P("req", None, "grp"),
        P("req"),
        P("req", None),
        P("req", None),
        P("req", None),
    )
    out_specs = (P(("req", "grp"), None), P("req", None, "grp"), P("req", None, "grp"))
    return jax.shard_map(body, mesh=mesh, in_specs=in_specs, out_specs=out_specs, check_vma=False)
```

time: 215 us -> 192 us (0.89)
  matrix products: 49.5 us -> 5.32 us
  Pallas kernels: 19.5 us -> 51 us
  other arithmetic: 15.5 us -> 4.55 us
  local copies, waits for them, and re-layouts: 19.8 us -> 22.5 us
  waiting for transfers between devices: 73.4 us -> 71.1 us
    dot_general x15 -> x4, matrix products: 49.5 us -> 5.32 us  [dot(): return jnp.dot(a, b, preferred_element_type=F32)]
    pallas_call x2 -> x11, Pallas kernels: 15.9 us -> 46.9 us  [the longest x4 13.8 us: mlp_up(): pl.pallas_call(up_kernel, out_shape=[jax.ShapeDtypeStruct((unit, gate.sha...]
    ppermute x24 -> x25, waiting for transfers between devices: 73.3 us -> 60.3 us  [swap(): return lax.ppermute(values, axis, [(at, at ^ bit) for at in range(size)])]
    all_to_all x1 -> x2, waiting for transfers between devices: 0.01 us -> 10.7 us  [the longest x1 10.7 us: body(): lax.all_to_all(packed, 'req', split_axis=0, concat_axis=0, tiled=True)]
    all_to_all x1 -> x2, starting transfers between devices: 4.32 us -> 12.5 us  [the longest x1 7.28 us: body(): lax.all_to_all(packed, 'req', split_axis=0, concat_axis=0, tiled=True)]
    ppermute x24 -> x25, starting transfers between devices: 30.5 us -> 22.8 us  [swap(): return lax.ppermute(values, axis, [(at, at ^ bit) for at in range(size)])]
    convert_element_type x5 -> x3, other arithmetic: 6.94 us -> 0.29 us  [the longest x1 0.15 us: body(): own = normalize(residual, mlp_gain).astype(BF)]
    dynamic_slice x0 -> x1, local copies, waits for them, and re-layouts: none -> 2.88 us  [rows_of(): return lax.dynamic_slice_in_dim(w, index * size, size, 0)]
  transfers between devices with their start and end apart: 25 -> 27, of which waited for: 11 -> 14; matrix products, arithmetic and copies ran while one was open for 34% -> 9% of each run, Pallas kernels for 2% -> 25%
where the time goes in v2:
time: 192 us; the launch traced here: 191 us
  waiting for transfers between devices  71.1 us (37%)
  Pallas kernels  51 us (27%)
  starting transfers between devices  35.3 us (18%)
  local copies, waits for them, and re-layouts  22.5 us (12%)
  matrix products  5.32 us (3%)
  other arithmetic  4.55 us (2%)
    ppermute x25, waiting for transfers between devices, swap(): return lax.ppermute(values, axis, [(at, at ^ bit) for at in range(size)])  60.3 us
    ppermute x25, starting transfers between devices, swap(): return lax.ppermute(values, axis, [(at, at ^ bit) for at in range(size)])  22.8 us
    unnamed x66, local copies, waits for them, and re-layouts  17.2 us
    pallas_call x4, Pallas kernels, mlp_up(): pl.pallas_call(up_kernel, out_shape=[jax.ShapeDtypeStruct((unit, gate.sha...  13.8 us
    pallas_call x4, Pallas kernels, mlp_down(): pl.pallas_call(functools.partial(down_kernel, len(pieces)), out_shape=[ja...  12.5 us
    pallas_call x1, Pallas kernels, attend(): pl.pallas_call(attention_kernel, out_shape=jax.ShapeDtypeStruct(result, B...  12.3 us
    all_to_all x1, waiting for transfers between devices, body(): lax.all_to_all(packed, 'req', split_axis=0, concat_axis=0, tiled=True)  10.7 us
    all_to_all x1, starting transfers between devices, body(): lax.all_to_all(packed, 'req', split_axis=0, concat_axis=0, tiled=True)  7.28 us
  transfers between devices with their start and end apart: 27, of which 14 were waited for; matrix products, arithmetic and copies ran while one was open for 9% of the time, Pallas kernels for 25%

profile of v2, /device:TPU:0, one launch (start us, length us, event | category | flops | bytes accessed | tf_op | source)
XLA Modules:
  0.0 190.8 jit_solution(12208957609054707363)
XLA Ops:
  3.2 7.3 %all-to-all-start = ((bf16[8,528,128]{2,1,0:T(8,128)(2,1)}), bf16[8,528,128]{2,1,0:T(8,128)(2,1)}, u32[]{:S(2)}, u32[]{:S(2)}) async-start(bf16[8,528,128]{2,1,0:T(8,128)(2,1)} %pack_pages.1), calls=%async_computation | async-start | bytes 2162688 | tf_op jit(solution)/shard_map/all_to_all | solution.py:484
  14.9 5.7 %project.1 = (bf16[8,128,512]{2,1,0:T(8,128)(2,1)S(1)}, bf16[8,128,256]{2,1,0:T(8,128)(2,1)S(1)}) custom-call(s32[8]{0:T(128)S(1)} %get-tuple-element.88.starts, s32[8]{0:T(128)S(1)} %get-tuple-element.87.counts, bf16[512,2048]{1,0:T(8,128)(2,1)S(1)} %copy-done.8, f32[1,2048]{1,0:T(1,128)S(1)} %bitcast.23, bf16[2048,512]{1,0:T(8,128)(2,1)S(1)} %copy-done.9, ...), custom_call_target="tpu_custom_call" | custom-call | tf_op jit(solution)/shard_map/project/pallas_call | solution.py:117
  20.6 2.9 %constant_dynamic-slice_fusion = bf16[256,2048]{1,0:T(8,128)(2,1)} fusion(bf16[1024,2048]{1,0:T(8,128)(2,1)} %refs_2_.7, s32[]{:T(128)S(6)} %select_n.52), kind=kLoop, calls=%fused_computation.39 | loop fusion | bytes 2097156 | tf_op jit(solution)/shard_map/dynamic_slice | solution.py:388
  26.3 10.7 %all-to-all-done.pages = bf16[8,528,128]{2,1,0:T(8,128)(2,1)} async-done(((bf16[8,528,128]{2,1,0:T(8,128)(2,1)}), bf16[8,528,128]{2,1,0:T(8,128)(2,1)}, u32[]{:S(2)}, u32[]{:S(2)}) %all-to-all-start) | async-done | bytes 1081376 | tf_op jit(solution)/shard_map/all_to_all | solution.py:484
  39.3 12.3 %attend.1 = bf16[4,128,512]{2,1,0:T(8,128)(2,1)S(1)} custom-call(s32[8]{0:T(128)S(1)} %get-tuple-element.88.starts, s32[8]{0:T(128)S(1)} %get-tuple-element.87.counts, s32[1]{0:T(128)} %bitcast.group, bf16[8,128,512]{2,1,0:T(8,128)(2,1)S(1)} %copy-done.17, bf16[8,128,256]{2,1,0:T(8,128)(2,1)S(1)} %copy-done.11, bf16[8,528,128]{2,1,0:T(8,128)(2,1)} %all-to-all-done.pages, ...), custom_call_target="tpu_custom_call" | custom-call | tf_op jit(solution)/shard_map/attend/pallas_call | solution.py:226
  59.2 5.2 %all-to-all-start.1 = ((bf16[8,128,256]{2,1,0:T(8,128)(2,1)}), bf16[8,128,256]{2,1,0:T(8,128)(2,1)}, u32[]{:S(2)}, u32[]{:S(2)}) async-start(bf16[8,128,256]{2,1,0:T(8,128)(2,1)} %copy-done.10), calls=%async_computation.1 | async-start | bytes 1048576 | tf_op jit(solution)/shard_map/all_to_all | solution.py:499
  64.4 5.2 %collective-permute-done.3 = bf16[128,2048]{1,0:T(8,128)(2,1)} collective-permute-done((bf16[128,2048]{1,0:T(8,128)(2,1)}, bf16[128,2048]{1,0:T(8,128)(2,1)}, u32[]{:S(2)}, u32[]{:S(2)}) %collective-permute-start.3) | collective-permute-done | bytes 524320 | tf_op jit(solution)/shard_map/ppermute | solution.py:292
  75.2 2.7 %collective-permute-start.4 = (bf16[64,2048]{1,0:T(8,128)(2,1)S(1)}, bf16[64,2048]{1,0:T(8,128)(2,1)}, u32[]{:S(2)}, u32[]{:S(2)}) collective-permute-start(bf16[64,2048]{1,0:T(8,128)(2,1)S(1)} %get-tuple-element.92), channel_id=1, source_target_pairs={{0,16},{4,20},{8,24},{12,28},{16,0},{20,4},{24,8},{28,12},{1,17},{... | collective-permute-start | bytes 786440 | tf_op jit(solution)/shard_map/ppermute | solution.py:292
  77.9 12.5 %collective-permute-done.4 = bf16[64,2048]{1,0:T(8,128)(2,1)} collective-permute-done((bf16[64,2048]{1,0:T(8,128)(2,1)S(1)}, bf16[64,2048]{1,0:T(8,128)(2,1)}, u32[]{:S(2)}, u32[]{:S(2)}) %collective-permute-start.4) | collective-permute-done | bytes 262176 | tf_op jit(solution)/shard_map/ppermute | solution.py:292
  90.4 3.1 %collective-permute-done.5.mine = bf16[128,2048]{1,0:T(8,128)(2,1)} collective-permute-done((bf16[128,2048]{1,0:T(8,128)(2,1)S(1)}, bf16[128,2048]{1,0:T(8,128)(2,1)}, u32[]{:S(2)}, u32[]{:S(2)}) %collective-permute-start.5) | collective-permute-done | bytes 524320 | tf_op jit(solution)/shard_map/ppermute | solution.py:292
  101.1 3.1 %mlp_up.4 = (bf16[128,1024]{1,0:T(8,128)(2,1)S(1)}, bf16[128,1024]{1,0:T(8,128)(2,1)S(1)}) custom-call(bf16[128,2048]{1,0:T(8,128)(2,1)S(1)} %multiply_convert_fusion.mine, bf16[128,2048]{1,0:T(8,128)(2,1)S(1)} %collective-permute-done.6.theirs, bf16[2048,1024]{1,0:T(8,128)(2,1)S(1)} %copy-done.2, bf16[2048,1024]{1,0:T(8,128)(2,1)S(1)} %copy-done.5), custom_call_target="tpu_custom_call" | custom-call | tf_op jit(solution)/shard_map/mlp_up/pallas_call | solution.py:332
  116.7 4.4 %mlp_up.5 = (bf16[128,1024]{1,0:T(8,128)(2,1)S(1)}, bf16[128,1024]{1,0:T(8,128)(2,1)S(1)}) custom-call(bf16[128,2048]{1,0:T(8,128)(2,1)} %collective-permute-done.5.mine, bf16[128,2048]{1,0:T(8,128)(2,1)} %collective-permute-done.9.theirs, bf16[2048,1024]{1,0:T(8,128)(2,1)S(1)} %copy-done.3, bf16[2048,1024]{1,0:T(8,128)(2,1)S(1)} %copy-done.6), custom_call_target="tpu_custom_call" | custom-call | tf_op jit(solution)/shard_map/mlp_up/pallas_call | solution.py:332
  121.1 4.5 %collective-permute-done.11.theirs = bf16[128,2048]{1,0:T(8,128)(2,1)S(1)} collective-permute-done((bf16[128,2048]{1,0:T(8,128)(2,1)}, bf16[128,2048]{1,0:T(8,128)(2,1)S(1)}, u32[]{:S(2)}, u32[]{:S(2)}) %collective-permute-start.11) | collective-permute-done | bytes 524320 | tf_op jit(solution)/shard_map/ppermute | solution.py:292
  127.1 3.1 %mlp_up.6 = (bf16[128,1024]{1,0:T(8,128)(2,1)S(1)}, bf16[128,1024]{1,0:T(8,128)(2,1)S(1)}) custom-call(bf16[128,2048]{1,0:T(8,128)(2,1)S(1)} %copy-done.15, bf16[128,2048]{1,0:T(8,128)(2,1)S(1)} %collective-permute-done.11.theirs, bf16[2048,1024]{1,0:T(8,128)(2,1)S(1)} %copy-done.4, bf16[2048,1024]{1,0:T(8,128)(2,1)S(1)} %copy-done.7), custom_call_target="tpu_custom_call" | custom-call | tf_op jit(solution)/shard_map/mlp_up/pallas_call | solution.py:332
  130.2 10.8 %collective-permute-done.13.theirs = bf16[128,2048]{1,0:T(8,128)(2,1)S(1)} collective-permute-done((bf16[128,2048]{1,0:T(8,128)(2,1)S(1)}, bf16[128,2048]{1,0:T(8,128)(2,1)S(1)}, u32[]{:S(2)}, u32[]{:S(2)}) %collective-permute-start.13) | collective-permute-done | bytes 524320 | tf_op jit(solution)/shard_map/ppermute | solution.py:292
  141.4 3.1 %mlp_up.7 = (bf16[128,1024]{1,0:T(8,128)(2,1)S(1)}, bf16[128,1024]{1,0:T(8,128)(2,1)S(1)}) custom-call(bf16[128,2048]{1,0:T(8,128)(2,1)S(1)} %constant_dynamic-update-slice_fusion.2.mine, bf16[128,2048]{1,0:T(8,128)(2,1)S(1)} %collective-permute-done.13.theirs, bf16[2048,1024]{1,0:T(8,128)(2,1)S(1)} %copy-done.4, bf16[2048,1024]{1,0:T(8,128)(2,1)S(1)} %copy-done.7), custom_call_target="tpu_custom_call" | custom-call | tf_op jit(solution)/shard_map/mlp_up/pallas_call | solution.py:332
  146.3 4.0 %collective-permute-done.15.refs_1_ = bf16[128,1024]{1,0:T(8,128)(2,1)S(1)} collective-permute-done((bf16[128,1024]{1,0:T(8,128)(2,1)S(1)}, bf16[128,1024]{1,0:T(8,128)(2,1)S(1)}, u32[]{:S(2)}, u32[]{:S(2)}) %collective-permute-start.15) | collective-permute-done | bytes 262176 | tf_op jit(solution)/shard_map/ppermute | solution.py:292
  150.3 3.1 %mlp_down.4 = (bf16[64,2048]{1,0:T(8,128)(2,1)S(1)}, bf16[64,2048]{1,0:T(8,128)(2,1)S(1)}) custom-call(s32[1]{0:T(128)} %bitcast.group, bf16[128,1024]{1,0:T(8,128)(2,1)S(1)} %get-tuple-element.69.refs_0_, bf16[128,1024]{1,0:T(8,128)(2,1)S(1)} %collective-permute-done.15.refs_1_, bf16[1024,2048]{1,0:T(8,128)(2,1)S(1)} %copy-done.1, ...), custom_call_target="tpu_custom_call" | custom-call | tf_op jit(solution)/shard_map/mlp_down/pallas_call | solution.py:370
  155.0 3.1 %mlp_down.6 = (bf16[64,2048]{1,0:T(8,128)(2,1)S(1)}, bf16[64,2048]{1,0:T(8,128)(2,1)S(1)}) custom-call(s32[1]{0:T(128)} %bitcast.group, bf16[128,1024]{1,0:T(8,128)(2,1)S(1)} %get-tuple-element.71.refs_0_, bf16[128,1024]{1,0:T(8,128)(2,1)S(1)} %collective-permute-done.14.refs_1_, bf16[1024,2048]{1,0:T(8,128)(2,1)S(1)} %copy-done.1, ...), custom_call_target="tpu_custom_call" | custom-call | tf_op jit(solution)/shard_map/mlp_down/pallas_call | solution.py:370
  161.6 3.1 %mlp_down.7 = bf16[128,2048]{1,0:T(8,128)(2,1)S(1)} custom-call(s32[1]{0:T(128)} %bitcast.group, bf16[128,1024]{1,0:T(8,128)(2,1)S(1)} %get-tuple-element.81.refs_0_, bf16[128,1024]{1,0:T(8,128)(2,1)S(1)} %collective-permute-done.18.refs_1_, bf16[1024,2048]{1,0:T(8,128)(2,1)S(1)} %copy-done.1, bf16[256,2048]{1,0:T(8,128)(2,1)S(1)} %collective-permute-done.refs_3_, ...), custom_call_target="tpu_custom_call" | custom-call | tf_op jit(solution)/shard_map/mlp_down/pallas_call | solution.py:370
  168.7 4.1 %store_new.1 = (bf16[128,16,128]{2,1,0:T(8,128)(2,1)}, bf16[128,16,128]{2,1,0:T(8,128)(2,1)}) custom-call(s32[128]{0:T(128)S(1)} %bitcast.25, s32[8]{0:T(128)S(1)} %bitcast.27, s32[8]{0:T(128)S(1)} %bitcast.28, bf16[8,128,256]{2,1,0:T(8,128)(2,1)} %all-to-all-done.1.new, f32[384,128]{1,0:T(8,128)S(1)} %get-tuple-element.94.cosines, ...), custom_call_target="tpu_custom_call" | custom-call | tf_op jit(solution)/shard_map/store_new/pallas_call | solution.py:280
  172.8 3.2 %mlp_down.5 = bf16[128,2048]{1,0:T(8,128)(2,1)S(1)} custom-call(s32[1]{0:T(128)} %bitcast.group, bf16[128,1024]{1,0:T(8,128)(2,1)S(1)} %copy-done.21, bf16[128,1024]{1,0:T(8,128)(2,1)S(1)} %collective-permute-done.19.refs_1_, bf16[1024,2048]{1,0:T(8,128)(2,1)S(1)} %copy-done.1, bf16[256,2048]{1,0:T(8,128)(2,1)S(1)} %collective-permute-done.refs_3_, ...), custom_call_target="tpu_custom_call" | custom-call | tf_op jit(solution)/shard_map/mlp_down/pallas_call | solution.py:370
  176.0 6.8 %collective-permute-done.24 = bf16[64,2048]{1,0:T(8,128)(2,1)S(1)} collective-permute-done((bf16[64,2048]{1,0:T(8,128)(2,1)S(1)}, bf16[64,2048]{1,0:T(8,128)(2,1)S(1)}, u32[]{:S(2)}, u32[]{:S(2)}) %collective-permute-start.24) | collective-permute-done | bytes 262176 | tf_op jit(solution)/shard_map/ppermute | solution.py:292
  182.9 6.8 %collective-permute-done.22 = bf16[64,2048]{1,0:T(8,128)(2,1)S(1)} collective-permute-done((bf16[64,2048]{1,0:T(8,128)(2,1)S(1)}, bf16[64,2048]{1,0:T(8,128)(2,1)S(1)}, u32[]{:S(2)}, u32[]{:S(2)}) %collective-permute-start.22) | collective-permute-done | bytes 262176 | tf_op jit(solution)/shard_map/ppermute | solution.py:292
  (126 shorter events, 58.7 us)
Async XLA Ops:
  3.2 33.9 %all-to-all-start = ((bf16[8,528,128]{2,1,0:T(8,128)(2,1)}), bf16[8,528,128]{2,1,0:T(8,128)(2,1)}, u32[]{:S(2)}, u32[]{:S(2)}) async-start(bf16[8,528,128]{2,1,0:T(8,128)(2,1)} %pack_pages.1), calls=%async_computation | async-start | bytes 2162688 | tf_op jit(solution)/shard_map/all_to_all | solution.py:484
  23.5 28.1 %collective-permute-start = (bf16[256,2048]{1,0:T(8,128)(2,1)}, bf16[256,2048]{1,0:T(8,128)(2,1)S(1)}, u32[]{:S(2)}, u32[]{:S(2)}) collective-permute-start(bf16[256,2048]{1,0:T(8,128)(2,1)} %constant_dynamic-slice_fusion), channel_id=1, source_target_pairs={{0,4},{4,0},{8,12},{12,8},{16,20},{20,16},{24,28},{28,24},{1,5},{5... | collective-permute-start | bytes 3145736 | tf_op jit(solution)/shard_map/ppermute | solution.py:292
  53.4 11.0 %collective-permute-start.1 = (bf16[128,2048]{1,0:T(8,128)(2,1)}, bf16[128,2048]{1,0:T(8,128)(2,1)}, u32[]{:S(2)}, u32[]{:S(2)}) collective-permute-start(bf16[128,2048]{1,0:T(8,128)(2,1)} %convolution_convert_fusion.2), channel_id=1, source_target_pairs={{0,1},{1,0},{2,3},{3,2},{4,5},{5,4},{6,7},{7,6},{8,9},{9,8},{10,11... | collective-permute-start | bytes 1572872 | tf_op jit(solution)/shard_map/ppermute | solution.py:292
  55.3 14.3 %collective-permute-start.3 = (bf16[128,2048]{1,0:T(8,128)(2,1)}, bf16[128,2048]{1,0:T(8,128)(2,1)}, u32[]{:S(2)}, u32[]{:S(2)}) collective-permute-start(bf16[128,2048]{1,0:T(8,128)(2,1)} %add_convert_fusion.1), channel_id=1, source_target_pairs={{0,2},{1,3},{2,0},{3,1},{4,6},{5,7},{6,4},{7,5},{8,10},{9,11},{10,... | collective-permute-start | bytes 1572872 | tf_op jit(solution)/shard_map/ppermute | solution.py:292
  59.2 48.2 %all-to-all-start.1 = ((bf16[8,128,256]{2,1,0:T(8,128)(2,1)}), bf16[8,128,256]{2,1,0:T(8,128)(2,1)}, u32[]{:S(2)}, u32[]{:S(2)}) async-start(bf16[8,128,256]{2,1,0:T(8,128)(2,1)} %copy-done.10), calls=%async_computation.1 | async-start | bytes 1048576 | tf_op jit(solution)/shard_map/all_to_all | solution.py:499
  72.0 21.5 %collective-permute-start.5 = (bf16[128,2048]{1,0:T(8,128)(2,1)S(1)}, bf16[128,2048]{1,0:T(8,128)(2,1)}, u32[]{:S(2)}, u32[]{:S(2)}) collective-permute-start(bf16[128,2048]{1,0:T(8,128)(2,1)S(1)} %multiply_convert_fusion.mine), channel_id=1, source_target_pairs={{0,8},{4,12},{8,0},{12,4},{16,24},{20,28},{24,16},{28,20},{1,9},{5... | collective-permute-start | bytes 1572872 | tf_op jit(solution)/shard_map/ppermute | solution.py:292
  74.2 19.4 %collective-permute-start.6 = (bf16[128,2048]{1,0:T(8,128)(2,1)S(1)}, bf16[128,2048]{1,0:T(8,128)(2,1)S(1)}, u32[]{:S(2)}, u32[]{:S(2)}) collective-permute-start(bf16[128,2048]{1,0:T(8,128)(2,1)S(1)} %multiply_convert_fusion.mine), channel_id=1, source_target_pairs={{0,4},{4,0},{8,12},{12,8},{16,20},{20,16},{24,28},{28,24},{1,5},{5... | collective-permute-start | bytes 1572872 | tf_op jit(solution)/shard_map/ppermute | solution.py:292
  75.2 15.2 %collective-permute-start.4 = (bf16[64,2048]{1,0:T(8,128)(2,1)S(1)}, bf16[64,2048]{1,0:T(8,128)(2,1)}, u32[]{:S(2)}, u32[]{:S(2)}) collective-permute-start(bf16[64,2048]{1,0:T(8,128)(2,1)S(1)} %get-tuple-element.92), channel_id=1, source_target_pairs={{0,16},{4,20},{8,24},{12,28},{16,0},{20,4},{24,8},{28,12},{1,17},{... | collective-permute-start | bytes 786440 | tf_op jit(solution)/shard_map/ppermute | solution.py:292
  93.6 16.3 %collective-permute-start.9 = (bf16[128,2048]{1,0:T(8,128)(2,1)}, bf16[128,2048]{1,0:T(8,128)(2,1)}, u32[]{:S(2)}, u32[]{:S(2)}) collective-permute-start(bf16[128,2048]{1,0:T(8,128)(2,1)} %collective-permute-done.5.mine), channel_id=1, source_target_pairs={{0,4},{4,0},{8,12},{12,8},{16,20},{20,16},{24,28},{28,24},{1,5},{5... | collective-permute-start | bytes 1572872 | tf_op jit(solution)/shard_map/ppermute | solution.py:292
  95.2 30.4 %collective-permute-start.12 = (bf16[256,2048]{1,0:T(8,128)(2,1)S(1)}, bf16[256,2048]{1,0:T(8,128)(2,1)}, u32[]{:S(2)}, u32[]{:S(2)}) collective-permute-start(bf16[256,2048]{1,0:T(8,128)(2,1)S(1)} %collective-permute-done.refs_3_), channel_id=1, source_target_pairs={{0,2},{1,3},{2,0},{3,1},{4,6},{5,7},{6,4},{7,5},{8,10},{9,11},{10,... | collective-permute-start | bytes 3145736 | tf_op jit(solution)/shard_map/ppermute | solution.py:292
  96.4 13.5 %collective-permute-start.7 = (bf16[64,2048]{1,0:T(8,128)(2,1)}, bf16[64,2048]{1,0:T(8,128)(2,1)}, u32[]{:S(2)}, u32[]{:S(2)}) collective-permute-start(bf16[64,2048]{1,0:T(8,128)(2,1)} %get-tuple-element.54), channel_id=1, source_target_pairs={{0,16},{4,20},{8,24},{12,28},{16,0},{20,4},{24,8},{28,12},{1,17},{... | collective-permute-start | bytes 786440 | tf_op jit(solution)/shard_map/ppermute | solution.py:292
  96.4 13.5 %collective-permute-start.8 = (bf16[64,2048]{1,0:T(8,128)(2,1)}, bf16[64,2048]{1,0:T(8,128)(2,1)}, u32[]{:S(2)}, u32[]{:S(2)}) collective-permute-start(bf16[64,2048]{1,0:T(8,128)(2,1)} %collective-permute-done.4), channel_id=1, source_target_pairs={{0,8},{4,12},{8,0},{12,4},{16,24},{20,28},{24,16},{28,20},{1,9},{5... | collective-permute-start | bytes 786440 | tf_op jit(solution)/shard_map/ppermute | solution.py:292
  111.6 14.1 %collective-permute-start.11 = (bf16[128,2048]{1,0:T(8,128)(2,1)}, bf16[128,2048]{1,0:T(8,128)(2,1)S(1)}, u32[]{:S(2)}, u32[]{:S(2)}) collective-permute-start(bf16[128,2048]{1,0:T(8,128)(2,1)} %constant_dynamic-update-slice_fusion.mine), channel_id=1, source_target_pairs={{0,4},{4,0},{8,12},{12,8},{16,20},{20,16},{24,28},{28,24},{1,5},{5... | collective-permute-start | bytes 1572872 | tf_op jit(solution)/shard_map/ppermute | solution.py:292
  112.3 8.8 %collective-permute-start.10 = (bf16[64,2048]{1,0:T(8,128)(2,1)}, bf16[64,2048]{1,0:T(8,128)(2,1)S(1)}, u32[]{:S(2)}, u32[]{:S(2)}) collective-permute-start(bf16[64,2048]{1,0:T(8,128)(2,1)} %collective-permute-done.7), channel_id=1, source_target_pairs={{0,8},{4,12},{8,0},{12,4},{16,24},{20,28},{24,16},{28,20},{1,9},{5... | collective-permute-start | bytes 786440 | tf_op jit(solution)/shard_map/ppermute | solution.py:292
  112.3 38.0 %collective-permute-start.16 = (bf16[256,2048]{1,0:T(8,128)(2,1)S(1)}, bf16[256,2048]{1,0:T(8,128)(2,1)S(1)}, u32[]{:S(2)}, u32[]{:S(2)}) collective-permute-start(bf16[256,2048]{1,0:T(8,128)(2,1)S(1)} %collective-permute-done.refs_3_), channel_id=1, source_target_pairs={{0,1},{1,0},{2,3},{3,2},{4,5},{5,4},{6,7},{7,6},{8,9},{9,8},{10,11... | collective-permute-start | bytes 3145736 | tf_op jit(solution)/shard_map/ppermute | solution.py:292
  125.6 24.6 %collective-permute-start.17 = (bf16[256,2048]{1,0:T(8,128)(2,1)}, bf16[256,2048]{1,0:T(8,128)(2,1)S(1)}, u32[]{:S(2)}, u32[]{:S(2)}) collective-permute-start(bf16[256,2048]{1,0:T(8,128)(2,1)} %collective-permute-done.12.refs_5_), channel_id=1, source_target_pairs={{0,1},{1,0},{2,3},{3,2},{4,5},{5,4},{6,7},{7,6},{8,9},{9,8},{10,11... | collective-permute-start | bytes 3145736 | tf_op jit(solution)/shard_map/ppermute | solution.py:292
  126.6 14.4 %collective-permute-start.13 = (bf16[128,2048]{1,0:T(8,128)(2,1)S(1)}, bf16[128,2048]{1,0:T(8,128)(2,1)S(1)}, u32[]{:S(2)}, u32[]{:S(2)}) collective-permute-start(bf16[128,2048]{1,0:T(8,128)(2,1)S(1)} %constant_dynamic-update-slice_fusion.2.mine), channel_id=1, source_target_pairs={{0,4},{4,0},{8,12},{12,8},{16,20},{20,16},{24,28},{28,24},{1,5},{5... | collective-permute-start | bytes 1572872 | tf_op jit(solution)/shard_map/ppermute | solution.py:292
  141.0 9.2 %collective-permute-start.15 = (bf16[128,1024]{1,0:T(8,128)(2,1)S(1)}, bf16[128,1024]{1,0:T(8,128)(2,1)S(1)}, u32[]{:S(2)}, u32[]{:S(2)}) collective-permute-start(bf16[128,1024]{1,0:T(8,128)(2,1)S(1)} %get-tuple-element.70), channel_id=1, source_target_pairs={{0,4},{4,0},{8,12},{12,8},{16,20},{20,16},{24,28},{28,24},{1,5},{5... | collective-permute-start | bytes 786440 | tf_op jit(solution)/shard_map/ppermute | solution.py:292
  144.6 10.0 %collective-permute-start.14 = (bf16[128,1024]{1,0:T(8,128)(2,1)S(1)}, bf16[128,1024]{1,0:T(8,128)(2,1)S(1)}, u32[]{:S(2)}, u32[]{:S(2)}) collective-permute-start(bf16[128,1024]{1,0:T(8,128)(2,1)S(1)} %get-tuple-element.68), channel_id=1, source_target_pairs={{0,4},{4,0},{8,12},{12,8},{16,20},{20,16},{24,28},{28,24},{1,5},{5... | collective-permute-start | bytes 786440 | tf_op jit(solution)/shard_map/ppermute | solution.py:292
  158.1 7.5 %collective-permute-start.23 = (bf16[64,2048]{1,0:T(8,128)(2,1)S(1)}, bf16[64,2048]{1,0:T(8,128)(2,1)S(1)}, u32[]{:S(2)}, u32[]{:S(2)}) collective-permute-start(bf16[64,2048]{1,0:T(8,128)(2,1)S(1)} %get-tuple-element.82), channel_id=1, source_target_pairs={{0,8},{4,12},{8,0},{12,4},{16,24},{20,28},{24,16},{28,20},{1,9},{5... | collective-permute-start | bytes 786440 | tf_op jit(solution)/shard_map/ppermute | solution.py:292
  164.8 24.9 %collective-permute-start.21 = (bf16[128,2048]{1,0:T(8,128)(2,1)S(1)}, bf16[128,2048]{1,0:T(8,128)(2,1)S(1)}, u32[]{:S(2)}, u32[]{:S(2)}) collective-permute-start(bf16[128,2048]{1,0:T(8,128)(2,1)S(1)} %mlp_down.7), channel_id=1, source_target_pairs={{0,8},{4,12},{8,0},{12,4},{16,24},{20,28},{24,16},{28,20},{1,9},{5... | collective-permute-start | bytes 1572872 | tf_op jit(solution)/shard_map/ppermute | solution.py:292
  165.0 7.8 %collective-permute-start.19 = (bf16[128,1024]{1,0:T(8,128)(2,1)S(1)}, bf16[128,1024]{1,0:T(8,128)(2,1)S(1)}, u32[]{:S(2)}, u32[]{:S(2)}) collective-permute-start(bf16[128,1024]{1,0:T(8,128)(2,1)S(1)} %copy-done.27), channel_id=1, source_target_pairs={{0,4},{4,0},{8,12},{12,8},{16,20},{20,16},{24,28},{28,24},{1,5},{5... | collective-permute-start | bytes 786440 | tf_op jit(solution)/shard_map/ppermute | solution.py:292
  165.7 17.2 %collective-permute-start.24 = (bf16[64,2048]{1,0:T(8,128)(2,1)S(1)}, bf16[64,2048]{1,0:T(8,128)(2,1)S(1)}, u32[]{:S(2)}, u32[]{:S(2)}) collective-permute-start(bf16[64,2048]{1,0:T(8,128)(2,1)S(1)} %add_convert_fusion.2), channel_id=1, source_target_pairs={{0,16},{4,20},{8,24},{12,28},{16,0},{20,4},{24,8},{28,12},{1,17},{... | collective-permute-start | bytes 786440 | tf_op jit(solution)/shard_map/ppermute | solution.py:292
  167.8 21.9 %collective-permute-start.22 = (bf16[64,2048]{1,0:T(8,128)(2,1)S(1)}, bf16[64,2048]{1,0:T(8,128)(2,1)S(1)}, u32[]{:S(2)}, u32[]{:S(2)}) collective-permute-start(bf16[64,2048]{1,0:T(8,128)(2,1)S(1)} %add_convert_fusion.3), channel_id=1, source_target_pairs={{0,16},{4,20},{8,24},{12,28},{16,0},{20,4},{24,8},{28,12},{1,17},{... | collective-permute-start | bytes 786440 | tf_op jit(solution)/shard_map/ppermute | solution.py:292
  (35 other events, 295.7 us)

commit v3 on v2

--- a/solution.py
+++ b/solution.py
@@ -24,6 +24,7 @@
 F32 = jnp.float32
 SMEM = pl.BlockSpec(memory_space=pltpu.SMEM)
 VMEM = pl.BlockSpec(memory_space=pltpu.VMEM)
+HBM = pl.BlockSpec(memory_space=pltpu.HBM)
 SMALL = pl.CostEstimate(flops=0, bytes_accessed=0, transcendentals=0)
 
 
@@ -145,33 +146,40 @@
 
 
 def attention_kernel(
-    starts, counts, group, query, new, pages, cosines, sines, mixed, total
+    starts, counts, group, query, new, pages, cosines, sines, mixed, total, arrived, queries, news, sems
 ):
     step = pl.program_id(0)
     start, count = starts[step], counts[step]
     _, pair, qcols = query.shape
-    rows = total.shape[0]
+    rows = total.shape[1] - pair
     parts = mixed.shape[0]
     quarter = rows // parts
 
     def span(part):
         return pl.ds(pl.multiple_of((group[0] ^ part) * quarter, quarter), quarter)
 
+    moved = ((query, queries), (new, news), (pages, arrived))
+
     @pl.when(step == 0)
     def _():
+        for at in range(pages.shape[0]):
+            for kind, (source, target) in enumerate(moved):
+                pltpu.make_async_copy(source.at[at], target.at[at], sems.at[kind, at]).start()
         total[...] = jnp.zeros_like(total)
 
-    @pl.when(count > 0)
-    def _():
-        info = pages[0, 2 * CONTEXT :, :].astype(F32)
+    for kind, (_, target) in enumerate(moved):
+        pltpu.make_async_copy(target.at[step], target.at[step], sems.at[kind, step]).wait()
+
+    def request(size):
+        info = arrived[step, 2 * CONTEXT :, :].astype(F32)
         prior = jnp.max(info).astype(jnp.int32)
-        cosine = cosines[pl.ds(prior, pair), :]
-        sine = sines[pl.ds(prior, pair), :]
-        new_key = rotate(new[0, :, :LANES].astype(F32), cosine, sine).astype(BF)
-        new_value = new[0, :, LANES:]
-
-        place = lax.broadcasted_iota(jnp.int32, (CONTEXT, pair), 0)
-        new_slot = lax.broadcasted_iota(jnp.int32, (CONTEXT, pair), 1)
+        cosine = cosines[pl.ds(prior, size), :]
+        sine = sines[pl.ds(prior, size), :]
+        new_key = rotate(news[step, :size, :LANES].astype(F32), cosine, sine).astype(BF)
+        new_value = news[step, :size, LANES:]
+
+        place = lax.broadcasted_iota(jnp.int32, (CONTEXT, size), 0)
+        new_slot = lax.broadcasted_iota(jnp.int32, (CONTEXT, size), 1)
         put = jnp.where((place == new_slot + prior) & (new_slot < count), 1.0, 0.0).astype(BF)
         position = lax.broadcasted_iota(jnp.int32, (CONTEXT, LANES), 0)
         lane = lax.broadcasted_iota(jnp.int32, (CONTEXT, LANES), 1)
@@ -185,19 +193,20 @@
                 jnp.where(low, turned, whole).astype(BF),
             )
 
-        keys = merged(new_key, pages[0, :CONTEXT, :])
-        values = merged(new_value, pages[0, CONTEXT : 2 * CONTEXT, :])
-
-        query_slot = lax.broadcasted_iota(jnp.int32, (2 * pair, CONTEXT), 0)
-        query_slot = jnp.where(query_slot >= pair, query_slot - pair, query_slot)
-        at = lax.broadcasted_iota(jnp.int32, (2 * pair, CONTEXT), 1)
+        keys = merged(new_key, arrived[step, :CONTEXT, :])
+        values = merged(new_value, arrived[step, CONTEXT : 2 * CONTEXT, :])
+
+        query_slot = lax.broadcasted_iota(jnp.int32, (2 * size, CONTEXT), 0)
+        query_slot = jnp.where(query_slot >= size, query_slot - size, query_slot)
+        at = lax.broadcasted_iota(jnp.int32, (2 * size, CONTEXT), 1)
         allowed = at <= query_slot + prior
-        left = lax.broadcasted_iota(jnp.int32, (pair, LANES), 1) < HD
+        left = lax.broadcasted_iota(jnp.int32, (size, LANES), 1) < HD
+        slot = lax.broadcasted_iota(jnp.int32, (size, LANES), 0)
         tiles = qcols // LANES
-        outs = []
         for tile in range(tiles):
             kv = tile * 2 // tiles
-            turned = rotate(query[0, :, tile * LANES : (tile + 1) * LANES].astype(F32), cosine, sine)
+            span = slice(tile * LANES, (tile + 1) * LANES)
+            turned = rotate(queries[step, :size, span].astype(F32), cosine, sine)
             both = jnp.concatenate([jnp.where(left, turned, 0.0), jnp.where(left, 0.0, turned)], 0)
             score = lax.dot_general(
                 both.astype(BF), keys[kv], (((1,), (1,)), ((), ())), preferred_element_type=F32
@@ -208,20 +217,29 @@
             share = 1.0 / jnp.sum(weight, axis=-1, keepdims=True)
             probs = (weight * share).astype(BF)
             out = dot(probs, values[kv])
-            outs.append(jnp.where(left, out[:pair], out[pair:]).astype(BF))
-        block = jnp.concatenate(outs, axis=1)
-        total[...] += dot(one_hot((rows, pair), start, count, 1), block)
+            out = jnp.where(left, out[:size], out[size:])
+            rows_here = pl.ds(start, size)
+            total[tile, rows_here] = jnp.where(slot < count, out, total[tile, rows_here])
+
+    @pl.when(count > pair // 2)
+    def _():
+        request(pair)
+
+    @pl.when((count > 0) & (count <= pair // 2))
+    def _():
+        request(pair // 2)
 
     @pl.when(step == pl.num_programs(0) - 1)
     def _():
         for part in range(parts):
-            mixed[part] = total[span(part), :].astype(BF)
+            for tile in range(qcols // LANES):
+                here = slice(tile * LANES, (tile + 1) * LANES)
+                mixed[part, :, here] = total[tile, span(part), :].astype(BF)
 
 
 def attend(starts, counts, group, query, new, pages, cosines, sines, rows, parts):
     peers, pair, qcols = query.shape
     whole = lambda step, *_: (0, 0)
-    here = lambda step, *_: (step, 0, 0)
     result = (parts, rows // parts, qcols)
     return pl.pallas_call(
         attention_kernel,
@@ -230,17 +248,23 @@
             num_scalar_prefetch=3,
             grid=(peers,),
             in_specs=[
-                pl.BlockSpec((1, pair, qcols), here),
-                pl.BlockSpec((1, pair, 2 * LANES), here),
-                pl.BlockSpec((1,) + pages.shape[1:], here),
+                HBM,
+                HBM,
+                HBM,
                 pl.BlockSpec(cosines.shape, whole),
                 pl.BlockSpec(sines.shape, whole),
             ],
             out_specs=pl.BlockSpec(result, lambda step, *_: (0, 0, 0)),
-            scratch_shapes=[pltpu.VMEM((rows, qcols), F32)],
+            scratch_shapes=[
+                pltpu.VMEM((qcols // LANES, rows + pair, LANES), F32),
+                pltpu.VMEM(pages.shape, BF),
+                pltpu.VMEM(query.shape, BF),
+                pltpu.VMEM(new.shape, BF),
+                pltpu.SemaphoreType.DMA((3, peers)),
+            ],
         ),
         compiler_params=pltpu.CompilerParams(
-            vmem_limit_bytes=32 * 1024 * 1024, dimension_semantics=("arbitrary",)
+            vmem_limit_bytes=60 * 1024 * 1024, dimension_semantics=("arbitrary",)
         ),
         name="attend",
         cost_estimate=SMALL,
@@ -299,18 +323,51 @@
     return dot(hidden, w_down).astype(BF)
 
 
+def finish_kernel(base, over, gain, residual, own, own_a, own_b, arrived, sem):
+    copy = pltpu.make_async_copy(over, arrived, sem)
+    copy.start()
+    copy.wait()
+    half, block = own_a.shape[0], 16
+    for at in range(0, own.shape[0], block):
+        rows = slice(at, at + block)
+        values = base[rows] + RESIDUAL_MULT * arrived[rows].astype(F32)
+        residual[rows] = values
+        normed = normalize(values, gain[...]).astype(BF)
+        own[rows] = normed
+        if at < half:
+            own_a[rows] = normed
+        else:
+            own_b[at - half : at - half + block] = normed
+
+
+def finish(base, over, gain):
+    rows, width = base.shape
+    shape = lambda count, kind: jax.ShapeDtypeStruct((count, width), kind)
+    return pl.pallas_call(
+        finish_kernel,
+        out_shape=[shape(rows, F32), shape(rows, BF), shape(rows // 2, BF), shape(rows // 2, BF)],
+        in_specs=[VMEM, HBM, VMEM],
+        out_specs=[VMEM] * 4,
+        scratch_shapes=[pltpu.VMEM((rows, width), BF), pltpu.SemaphoreType.DMA],
+        compiler_params=pltpu.CompilerParams(vmem_limit_bytes=16 * 1024 * 1024),
+        cost_estimate=SMALL,
+        name="finish",
+    )(base, over, gain.reshape(1, width))
+
+
 UNIT_TILE = 256
 COLUMN_TILE = 512
-HBM = pl.BlockSpec(memory_space=pltpu.HBM)
 ROOM = pltpu.CompilerParams(vmem_limit_bytes=16 * 1024 * 1024)
 
 
-def up_kernel(mine, theirs, gate, upper, mine_out, theirs_out, stack, sems):
-    unit = mine.shape[0]
-    copies = [
-        pltpu.make_async_copy(ref, stack.at[pl.ds(at * unit, unit)], sems.at[at])
-        for at, ref in enumerate((mine, theirs))
-    ]
+def up_kernel(count, *refs):
+    rows, (gate, upper, mine_out, theirs_out, stack, sems) = refs[:count], refs[count:]
+    unit = mine_out.shape[0]
+    copies, start = [], 0
+    for at, ref in enumerate(rows):
+        target = stack.at[pl.ds(start, ref.shape[0])]
+        copies.append(pltpu.make_async_copy(ref, target, sems.at[at]))
+        start += ref.shape[0]
     for copy in copies:
         copy.start()
     for copy in copies:
@@ -328,17 +385,18 @@
 
 
 def mlp_up(mine, theirs, gate, upper):
-    unit, width = mine.shape
+    unit, width = sum(ref.shape[0] for ref in mine), gate.shape[0]
+    count = len(mine) + len(theirs)
     return pl.pallas_call(
-        up_kernel,
+        functools.partial(up_kernel, count),
         out_shape=[jax.ShapeDtypeStruct((unit, gate.shape[1]), BF)] * 2,
-        in_specs=[HBM, HBM, VMEM, VMEM],
+        in_specs=[HBM] * count + [VMEM, VMEM],
         out_specs=[VMEM] * 2,
-        scratch_shapes=[pltpu.VMEM((2 * unit, width), BF), pltpu.SemaphoreType.DMA((2,))],
+        scratch_shapes=[pltpu.VMEM((2 * unit, width), BF), pltpu.SemaphoreType.DMA((count,))],
         compiler_params=ROOM,
         cost_estimate=SMALL,
         name="mlp_up",
-    )(mine, theirs, gate, upper)
+    )(*mine, *theirs, gate, upper)
 
 
 def down_kernel(count, group, *refs):
@@ -392,7 +450,7 @@
     return lax.optimization_barrier(values)
 
 
-def exchange_mlp(own, new, peers, groups, group, held, side_down):
+def exchange_mlp(own, own_a, own_b, peers, groups, group, held, side_down):
     send = functools.partial(swap, axis="req", size=peers)
     cross = functools.partial(swap, axis="grp", size=groups, bit=1)
     over = functools.partial(swap, axis="grp", size=groups, bit=2)
@@ -401,50 +459,62 @@
     up = lambda mine, theirs: mlp_up(mine, theirs, held[0], held[1])
     unit = own.shape[0]
     half = unit // 2
-    own_a, own_b = own[:half], own[half:]
 
     far_a = send(own_a, bit=4)
-    near = send(own, bit=2)
-    side_own = send(own, bit=1)
-    far_a, near, side_own = sync(far_a, near, side_own)
+    near_a = send(own_a, bit=2)
+    side = send(own, bit=1)
+    far_a, near_a, side = sync(far_a, near_a, side)
     far_b = send(after(own_b, far_a), bit=4)
     both_a = send(far_a, bit=2)
-    side_near = send(near, bit=1)
-    over_down = over(after(side_down, far_a))
-    hidden_own, theirs_own = up(own, side_own)
-    far_b, both_a, side_near, new, _ = sync(far_b, both_a, side_near, new, hidden_own)
+    side_far_a = send(far_a, bit=1)
+    side_near_a = send(near_a, bit=1)
+    over_down = over(after(side_down, own))
+    hidden_own, theirs_own = up([own], [side])
+    far_b, both_a, side_far_a, side_near_a, _ = sync(
+        far_b, both_a, side_far_a, side_near_a, hidden_own
+    )
     both_b = send(far_b, bit=2)
-    rows_a = join(far_a, both_a)
-    side_a = send(rows_a, bit=1)
-    hidden_near, theirs_near = up(near, side_near)
-    both_b, side_a, over_down, _ = sync(both_b, side_a, over_down, hidden_near)
-    rows_b = join(far_b, both_b)
-    side_b = send(rows_b, bit=1)
+    near_b = send(after(own_b, far_b), bit=2)
+    side_far_b = send(far_b, bit=1)
+    side_both_a = send(both_a, bit=1)
+    hidden_a, theirs_a = up([far_a, near_a], [side_far_a, side_near_a])
+    both_b, near_b, side_far_b, side_both_a, over_down, _ = sync(
+        both_b, near_b, side_far_b, side_both_a, over_down, hidden_a
+    )
+    side_both_b = send(both_b, bit=1)
     pieces = [side_down, cross(side_down), over_down, cross(over_down)]
-    down = lambda hidden, side, sizes: mlp_down(group, hidden, side, held[2], pieces, sizes)
-    hidden_a, theirs_a = up(rows_a, side_a)
-    side_b, hidden_a, theirs_a = sync(side_b, hidden_a, theirs_a)
-    from_a = send(theirs_a, bit=1)
-    hidden_b, theirs_b = up(rows_b, side_b)
+    down = lambda hidden, other, sizes: mlp_down(group, hidden, other, held[2], pieces, sizes)
+    hidden_b, theirs_b = up([far_b, both_a], [side_far_b, side_both_a])
     from_b = send(theirs_b, bit=1)
-    from_a, _ = sync(from_a, hidden_b)
-    sum_far_a, sum_both_a = down(hidden_a, from_a, [half, half])
+    side_both_b, _ = sync(side_both_b, hidden_b)
+    side_near_b = send(after(near_b, side_both_b), bit=1)
+    hidden_c, theirs_c = up([both_b], [side_both_b])
+    from_c = send(theirs_c, bit=1)
+    from_b, _ = sync(from_b, hidden_c)
+    sum_far_b, sum_both_a = down(hidden_b, from_b, [half, half])
     back_both_a = send(sum_both_a, bit=2)
-    from_b, _ = sync(from_b, sum_far_a)
-    from_near = send(after(theirs_near, from_b), bit=1)
-    sum_far_b, sum_both_b = down(hidden_b, from_b, [half, half])
+    from_c, _ = sync(from_c, sum_both_a)
+    from_a = send(after(theirs_a, from_c), bit=1)
+    (sum_both_b,) = down(hidden_c, from_c, [half])
     back_both_b = send(sum_both_b, bit=2)
-    back_both_a, _ = sync(back_both_a, sum_far_b)
+    side_near_b, _ = sync(side_near_b, sum_both_b)
+    hidden_d, theirs_d = up([near_b], [side_near_b])
+    from_d = send(theirs_d, bit=1)
+    from_a, back_both_a, _ = sync(from_a, back_both_a, hidden_d)
+    sum_far_a, sum_near_a = down(hidden_a, from_a, [half, half])
     total_a = add(sum_far_a, back_both_a).astype(BF)
     back_far_a = send(total_a, bit=4)
+    back_near_a = send(sum_near_a, bit=2)
     back_both_b, _ = sync(back_both_b, total_a)
     total_b = add(sum_far_b, back_both_b).astype(BF)
     back_far_b = send(total_b, bit=4)
-    from_own = send(after(theirs_own, from_near), bit=1)
-    (sum_near,) = down(after(hidden_near, total_a), from_near, [unit])
-    back_near = send(sum_near, bit=2)
-    (sum_own,) = down(hidden_own, from_own, [unit])
-    return new, add(sum_own, back_near, join(back_far_a, back_far_b))
+    from_own = send(after(theirs_own, total_b), bit=1)
+    (sum_near_b,) = down(hidden_d, after(from_d, total_b), [half])
+    back_near_b = send(sum_near_b, bit=2)
+    (sum_own,) = down(hidden_own, after(from_own, sum_near_b), [unit])
+    return add(
+        sum_own, join(back_near_a, back_near_b), join(back_far_a, back_far_b)
+    )
 
 
 def body(
@@ -482,29 +552,30 @@
     group = group_index.reshape(1)
     packed = pack_pages(page_table[0], prior_len[0], cache_k, cache_v)
     pages = lax.all_to_all(packed, "req", split_axis=0, concat_axis=0, tiled=True)
-    query, fresh = project(starts, counts, hidden_in, attn_gain, w_query, w_key, w_value, pair)
+    query, fresh = project(starts, counts, after(hidden_in, cosines, sines), attn_gain, w_query, w_key, w_value, pair)
     if peers == 8:
-        side_down = swap(after(rows_of(w_down, group_index, groups), fresh), "req", peers, 1)
+        side_down = swap(rows_of(w_down, group_index, groups), "req", peers, 1)
     mixed = attend(
         starts, counts, group, query, fresh, pages, cosines, sines, row_count, groups
     )
+    new = lax.all_to_all(after(fresh, pages), "req", split_axis=0, concat_axis=0, tiled=True)
     if peers == 8:
-        mixed, side_down = sync(mixed, side_down)
-
-    out_of = lambda part: dot(mixed[part], w_out).astype(BF)
+        mixed, side_down, new = sync(mixed, side_down, new)
+
+    out_of = lambda part: dot(part, w_out).astype(BF)
     to_home = functools.partial(swap, axis="grp", size=groups)
-    cross = to_home(out_of(3), bit=1)
-    beside = to_home(out_of(1), bit=1)
-    over = (out_of(2).astype(F32) + cross.astype(F32)).astype(BF)
-    new = lax.all_to_all(after(fresh, over), "req", split_axis=0, concat_axis=0, tiled=True)
+    cross = out_of(mixed[3])
+    later = after(mixed, cross)
+    cross = to_home(cross, bit=1)
+    over = (out_of(mixed[2]).astype(F32) + cross.astype(F32)).astype(BF)
     over = to_home(over, bit=2)
-    attn_sum = out_of(0).astype(F32) + beside.astype(F32) + over.astype(F32)
+    beside = to_home(out_of(later[1]), bit=1)
     own_rows = lax.dynamic_slice_in_dim(hidden_in, group_index * quarter, quarter, 0).astype(F32)
-    residual = own_rows + RESIDUAL_MULT * attn_sum
-    own = normalize(residual, mlp_gain).astype(BF)
+    near_sum = out_of(later[0]).astype(F32) + beside.astype(F32)
+    residual, own, own_a, own_b = finish(own_rows + RESIDUAL_MULT * near_sum, over, mlp_gain)
     if peers == 8:
         held = [w_gate, w_up, w_down]
-        new, down = exchange_mlp(own, new, peers, groups, group, held, side_down)
+        down = exchange_mlp(own, own_a, own_b, peers, groups, group, held, side_down)
     else:
         piece = lax.all_gather(own, "req", axis=0, tiled=True)
         part = feed_forward(piece, w_gate, w_up, w_down)

time: 192 us -> 181 us (0.943)
  local copies, waits for them, and re-layouts: 22.5 us -> 10.2 us
  starting transfers between devices: 35.3 us -> 44 us
  waiting for transfers between devices: 71.1 us -> 68 us
  Pallas kernels: 51 us -> 49 us
    unnamed x66 -> x46, local copies, waits for them, and re-layouts: 17.2 us -> 7.7 us
    ppermute x25 -> x31, starting transfers between devices: 22.8 us -> 32.3 us  [swap(): return lax.ppermute(values, axis, [(at, at ^ bit) for at in range(size)])]
    ppermute x25 -> x31, waiting for transfers between devices: 60.3 us -> 56.8 us  [swap(): return lax.ppermute(values, axis, [(at, at ^ bit) for at in range(size)])]
    pallas_call x4 -> x5, Pallas kernels: 12.5 us -> 9.61 us  [mlp_down(): pl.pallas_call(functools.partial(down_kernel, len(pieces)), out_shape=[ja...]
    reduce_sum x1 -> x0, other arithmetic: 2.24 us -> none  [normalize(): mean_square = jnp.mean(values * values, axis=-1, keepdims=True)]
    all_to_all x1, waiting for transfers between devices: 0.01 us -> 1.99 us  [body(): lax.all_to_all(after(fresh, pages), 'req', split_axis=0, concat_axis=0, t...]
    pallas_call x4 -> x6, Pallas kernels: 13.8 us -> 14.9 us  [the longest x5 13.5 us: mlp_up(): pl.pallas_call(functools.partial(up_kernel, count), out_shape=[jax.ShapeD...]
  transfers between devices with their start and end apart: 27 -> 33, of which waited for: 14 -> 19; matrix products, arithmetic and copies ran while one was open for 9% -> 5% of each run, Pallas kernels for 25% -> 25%
where the time goes in v3:
time: 181 us
  waiting for transfers between devices  68 us (38%)
  Pallas kernels  49 us (27%)
  starting transfers between devices  44 us (24%)
  local copies, waits for them, and re-layouts  10.2 us (6%)
  matrix products  5.84 us (3%)
  other arithmetic  2.91 us (2%)
    ppermute x31, waiting for transfers between devices, swap(): return lax.ppermute(values, axis, [(at, at ^ bit) for at in range(size)])  56.8 us
    ppermute x31, starting transfers between devices, swap(): return lax.ppermute(values, axis, [(at, at ^ bit) for at in range(size)])  32.3 us
    pallas_call x5, Pallas kernels, mlp_up(): pl.pallas_call(functools.partial(up_kernel, count), out_shape=[jax.ShapeD...  13.5 us
    pallas_call x1, Pallas kernels, attend(): pl.pallas_call(attention_kernel, out_shape=jax.ShapeDtypeStruct(result, B...  12.1 us
    pallas_call x5, Pallas kernels, mlp_down(): pl.pallas_call(functools.partial(down_kernel, len(pieces)), out_shape=[ja...  9.61 us
    all_to_all x1, waiting for transfers between devices, body(): lax.all_to_all(packed, 'req', split_axis=0, concat_axis=0, tiled=True)  9.13 us
    unnamed x46, local copies, waits for them, and re-layouts  7.7 us
    all_to_all x1, starting transfers between devices, body(): lax.all_to_all(packed, 'req', split_axis=0, concat_axis=0, tiled=True)  7.41 us
  transfers between devices with their start and end apart: 33, of which 19 were waited for; matrix products, arithmetic and copies ran while one was open for 5% of the time, Pallas kernels for 25%

profile of v3, /device:TPU:0, one launch (start us, length us, event | category | flops | bytes accessed | tf_op | source)
XLA Modules:
  0.0 180.8 jit_solution(9572943554671581064)
XLA Ops:
  0.6 2.5 %pack_pages.1 = bf16[8,528,128]{2,1,0:T(8,128)(2,1)} custom-call(s32[128]{0:T(128)} %bitcast.28, s32[8]{0:T(128)} %bitcast.30, bf16[128,16,128]{2,1,0:T(8,128)(2,1)} %cache_k.3, bf16[128,16,128]{2,1,0:T(8,128)(2,1)} %cache_v.3), custom_call_target="tpu_custom_call" | custom-call | tf_op jit(solution)/shard_map/pack_pages/pallas_call | solution.py:71
  3.1 7.4 %all-to-all-start = ((bf16[8,528,128]{2,1,0:T(8,128)(2,1)}), bf16[8,528,128]{2,1,0:T(8,128)(2,1)}, u32[]{:S(2)}, u32[]{:S(2)}) async-start(bf16[8,528,128]{2,1,0:T(8,128)(2,1)} %pack_pages.1), calls=%async_computation | async-start | bytes 2162688 | tf_op jit(solution)/shard_map/all_to_all | solution.py:554
  10.6 2.5 %constant_dynamic-slice_fusion = bf16[256,2048]{1,0:T(8,128)(2,1)} fusion(bf16[1024,2048]{1,0:T(8,128)(2,1)} %refs_2_.15, s32[]{:T(128)S(6)} %select_n.60), kind=kLoop, calls=%fused_computation.32 | loop fusion | bytes 2097156 | tf_op jit(solution)/shard_map/dynamic_slice | solution.py:446
  13.0 2.0 %collective-permute-start = (bf16[256,2048]{1,0:T(8,128)(2,1)}, bf16[256,2048]{1,0:T(8,128)(2,1)S(1)}, u32[]{:S(2)}, u32[]{:S(2)}) collective-permute-start(bf16[256,2048]{1,0:T(8,128)(2,1)} %constant_dynamic-slice_fusion), channel_id=1, source_target_pairs={{0,4},{4,0},{8,12},{12,8},{16,20},{20,16},{24,28},{28,24},{1,5},{5... | collective-permute-start | bytes 3145736 | tf_op jit(solution)/shard_map/ppermute | solution.py:316
  20.5 5.7 %project.1 = (bf16[8,128,512]{2,1,0:T(8,128)(2,1)S(1)}, bf16[8,128,256]{2,1,0:T(8,128)(2,1)S(1)}) custom-call(s32[8]{0:T(128)S(1)} %get-tuple-element.114.starts, s32[8]{0:T(128)S(1)} %get-tuple-element.113.counts, bf16[512,2048]{1,0:T(8,128)(2,1)S(1)} %copy-done.4, f32[1,2048]{1,0:T(1,128)S(1)} %bitcast.26, bf16[2048,512]{1,0:T(8,128)(2,1)S(1)} %copy-done.5, ...), custom_call_target="tpu_custom_call" | custom-call | tf_op jit(solution)/shard_map/project/pallas_call | solution.py:118
  28.0 9.1 %all-to-all-done.pages = bf16[8,528,128]{2,1,0:T(8,128)(2,1)} async-done(((bf16[8,528,128]{2,1,0:T(8,128)(2,1)}), bf16[8,528,128]{2,1,0:T(8,128)(2,1)}, u32[]{:S(2)}, u32[]{:S(2)}) %all-to-all-start) | async-done | bytes 1081376 | tf_op jit(solution)/shard_map/all_to_all | solution.py:554
  37.1 4.3 %all-to-all-start.1 = ((bf16[8,128,256]{2,1,0:T(8,128)(2,1)}), bf16[8,128,256]{2,1,0:T(8,128)(2,1)}, u32[]{:S(2)}, u32[]{:S(2)}) async-start(bf16[8,128,256]{2,1,0:T(8,128)(2,1)} %copy-done.6), calls=%async_computation.1 | async-start | bytes 1048576 | tf_op jit(solution)/shard_map/all_to_all | solution.py:561
  41.5 12.1 %attend.1 = bf16[4,128,512]{2,1,0:T(8,128)(2,1)} custom-call(s32[8]{0:T(128)} %copy-done.17, s32[8]{0:T(128)} %copy-done.16, s32[1]{0:T(128)} %bitcast.group, bf16[8,128,512]{2,1,0:T(8,128)(2,1)} %copy-done.11, bf16[8,128,256]{2,1,0:T(8,128)(2,1)} %copy-done.6, bf16[8,528,128]{2,1,0:T(8,128)(2,1)} %all-to-all-done.pages, ...), custom_call_target="tpu_custom_call" | custom-call | tf_op jit(solution)/shard_map/attend/pallas_call | solution.py:244
  63.7 10.8 %collective-permute-done.3.over = bf16[128,2048]{1,0:T(8,128)(2,1)} collective-permute-done((bf16[128,2048]{1,0:T(8,128)(2,1)}, bf16[128,2048]{1,0:T(8,128)(2,1)}, u32[]{:S(2)}, u32[]{:S(2)}) %collective-permute-start.3) | collective-permute-done | bytes 524320 | tf_op jit(solution)/shard_map/ppermute | solution.py:316
  81.0 10.6 %collective-permute-done.4.refs_0_ = bf16[64,2048]{1,0:T(8,128)(2,1)S(1)} collective-permute-done((bf16[64,2048]{1,0:T(8,128)(2,1)S(1)}, bf16[64,2048]{1,0:T(8,128)(2,1)S(1)}, u32[]{:S(2)}, u32[]{:S(2)}) %collective-permute-start.4) | collective-permute-done | bytes 262176 | tf_op jit(solution)/shard_map/ppermute | solution.py:316
  96.5 2.2 %copy-done.3 = bf16[2048,1024]{1,0:T(8,128)(2,1)S(1)} copy-done((bf16[2048,1024]{1,0:T(8,128)(2,1)S(1)}, bf16[2048,1024]{1,0:T(8,128)(2,1)}, u32[]{:S(2)}) %copy-start.3) | copy-done | bytes 4194328
  98.7 3.1 %mlp_up.5 = (bf16[128,1024]{1,0:T(8,128)(2,1)S(1)}, bf16[128,1024]{1,0:T(8,128)(2,1)S(1)}) custom-call(bf16[128,2048]{1,0:T(8,128)(2,1)S(1)} %get-tuple-element.65.refs_0_, bf16[128,2048]{1,0:T(8,128)(2,1)S(1)} %collective-permute-done.6.refs_1_, bf16[2048,1024]{1,0:T(8,128)(2,1)S(1)} %copy-done.2, bf16[2048,1024]{1,0:T(8,128)(2,1)S(1)} %copy-done.3), custom_call_target="tpu_custom_call" | custom-call | tf_op jit(solution)/shard_map/mlp_up/pallas_call | solution.py:390
  101.9 4.3 %collective-permute-done.7.refs_0_ = bf16[64,2048]{1,0:T(8,128)(2,1)S(1)} collective-permute-done((bf16[64,2048]{1,0:T(8,128)(2,1)S(1)}, bf16[64,2048]{1,0:T(8,128)(2,1)S(1)}, u32[]{:S(2)}, u32[]{:S(2)}) %collective-permute-start.7) | collective-permute-done | bytes 262176 | tf_op jit(solution)/shard_map/ppermute | solution.py:316
  110.7 3.2 %mlp_up.6 = (bf16[128,1024]{1,0:T(8,128)(2,1)S(1)}, bf16[128,1024]{1,0:T(8,128)(2,1)S(1)}) custom-call(bf16[64,2048]{1,0:T(8,128)(2,1)S(1)} %collective-permute-done.4.refs_0_, bf16[64,2048]{1,0:T(8,128)(2,1)S(1)} %collective-permute-done.5.refs_1_, bf16[64,2048]{1,0:T(8,128)(2,1)S(1)} %collective-permute-done.9.refs_2_, ...), custom_call_target="tpu_custom_call" | custom-call | tf_op jit(solution)/shard_map/mlp_up/pallas_call | solution.py:390
  113.9 6.1 %collective-permute-done.12.refs_0_ = bf16[64,2048]{1,0:T(8,128)(2,1)S(1)} collective-permute-done((bf16[64,2048]{1,0:T(8,128)(2,1)S(1)}, bf16[64,2048]{1,0:T(8,128)(2,1)S(1)}, u32[]{:S(2)}, u32[]{:S(2)}) %collective-permute-start.12) | collective-permute-done | bytes 262176 | tf_op jit(solution)/shard_map/ppermute | solution.py:316
  122.2 3.2 %mlp_up.7 = (bf16[128,1024]{1,0:T(8,128)(2,1)S(1)}, bf16[128,1024]{1,0:T(8,128)(2,1)S(1)}) custom-call(bf16[64,2048]{1,0:T(8,128)(2,1)S(1)} %collective-permute-done.7.refs_0_, bf16[64,2048]{1,0:T(8,128)(2,1)S(1)} %collective-permute-done.8.refs_1_, bf16[64,2048]{1,0:T(8,128)(2,1)S(1)} %collective-permute-done.13.refs_2_, ...), custom_call_target="tpu_custom_call" | custom-call | tf_op jit(solution)/shard_map/mlp_up/pallas_call | solution.py:390
  126.7 3.8 %collective-permute-done.17.refs_1_ = bf16[64,2048]{1,0:T(8,128)(2,1)S(1)} collective-permute-done((bf16[64,2048]{1,0:T(8,128)(2,1)S(1)}, bf16[64,2048]{1,0:T(8,128)(2,1)S(1)}, u32[]{:S(2)}, u32[]{:S(2)}) %collective-permute-start.17) | collective-permute-done | bytes 262176 | tf_op jit(solution)/shard_map/ppermute | solution.py:316
  130.6 2.0 %mlp_up.8 = (bf16[64,1024]{1,0:T(8,128)(2,1)S(1)}, bf16[64,1024]{1,0:T(8,128)(2,1)S(1)}) custom-call(bf16[64,2048]{1,0:T(8,128)(2,1)S(1)} %collective-permute-done.11.refs_0_, bf16[64,2048]{1,0:T(8,128)(2,1)S(1)} %collective-permute-done.17.refs_1_, bf16[2048,1024]{1,0:T(8,128)(2,1)S(1)} %copy-done.2, bf16[2048,1024]{1,0:T(8,128)(2,1)S(1)} %copy-done.3), custom_call_target="tpu_custom_call" | custom-call | tf_op jit(solution)/shard_map/mlp_up/pallas_call | solution.py:390
  144.8 2.0 %mlp_up.9 = (bf16[64,1024]{1,0:T(8,128)(2,1)S(1)}, bf16[64,1024]{1,0:T(8,128)(2,1)S(1)}) custom-call(bf16[64,2048]{1,0:T(8,128)(2,1)S(1)} %collective-permute-done.12.refs_0_, bf16[64,2048]{1,0:T(8,128)(2,1)S(1)} %collective-permute-done.24.refs_1_, bf16[2048,1024]{1,0:T(8,128)(2,1)S(1)} %copy-done.2, bf16[2048,1024]{1,0:T(8,128)(2,1)S(1)} %copy-done.3), custom_call_target="tpu_custom_call" | custom-call | tf_op jit(solution)/shard_map/mlp_up/pallas_call | solution.py:390
  147.6 2.8 %collective-permute-done.22.refs_1_ = bf16[128,1024]{1,0:T(8,128)(2,1)S(1)} collective-permute-done((bf16[128,1024]{1,0:T(8,128)(2,1)S(1)}, bf16[128,1024]{1,0:T(8,128)(2,1)S(1)}, u32[]{:S(2)}, u32[]{:S(2)}) %collective-permute-start.22) | collective-permute-done | bytes 262176 | tf_op jit(solution)/shard_map/ppermute | solution.py:316
  161.1 4.1 %store_new.1 = (bf16[128,16,128]{2,1,0:T(8,128)(2,1)}, bf16[128,16,128]{2,1,0:T(8,128)(2,1)}) custom-call(s32[128]{0:T(128)S(1)} %bitcast.29, s32[8]{0:T(128)S(1)} %bitcast.31, s32[8]{0:T(128)S(1)} %bitcast.32, bf16[8,128,256]{2,1,0:T(8,128)(2,1)} %all-to-all-done.1.new, f32[384,128]{1,0:T(8,128)S(1)} %copy-done.10, f32[384,128]{1,0:T(8,128)S(1)} %copy-done.9, ...), custom_call_target="tpu_custom_call" | custom-call | tf_op jit(solution)/shard_map/store_new/pallas_call | solution.py:304
  167.1 4.3 %collective-permute-done.28 = bf16[64,2048]{1,0:T(8,128)(2,1)S(1)} collective-permute-done((bf16[64,2048]{1,0:T(8,128)(2,1)S(1)}, bf16[64,2048]{1,0:T(8,128)(2,1)S(1)}, u32[]{:S(2)}, u32[]{:S(2)}) %collective-permute-start.28) | collective-permute-done | bytes 262176 | tf_op jit(solution)/shard_map/ppermute | solution.py:316
  171.5 6.3 %collective-permute-done.29 = bf16[64,2048]{1,0:T(8,128)(2,1)S(1)} collective-permute-done((bf16[64,2048]{1,0:T(8,128)(2,1)S(1)}, bf16[64,2048]{1,0:T(8,128)(2,1)S(1)}, u32[]{:S(2)}, u32[]{:S(2)}) %collective-permute-start.29) | collective-permute-done | bytes 262176 | tf_op jit(solution)/shard_map/ppermute | solution.py:316
  177.7 2.0 %collective-permute-done.27 = bf16[64,2048]{1,0:T(8,128)(2,1)S(1)} collective-permute-done((bf16[64,2048]{1,0:T(8,128)(2,1)S(1)}, bf16[64,2048]{1,0:T(8,128)(2,1)S(1)}, u32[]{:S(2)}, u32[]{:S(2)}) %collective-permute-start.27) | collective-permute-done | bytes 262176 | tf_op jit(solution)/shard_map/ppermute | solution.py:316
  (115 shorter events, 63.2 us)
Async XLA Ops:
  3.1 34.0 %all-to-all-start = ((bf16[8,528,128]{2,1,0:T(8,128)(2,1)}), bf16[8,528,128]{2,1,0:T(8,128)(2,1)}, u32[]{:S(2)}, u32[]{:S(2)}) async-start(bf16[8,528,128]{2,1,0:T(8,128)(2,1)} %pack_pages.1), calls=%async_computation | async-start | bytes 2162688 | tf_op jit(solution)/shard_map/all_to_all | solution.py:554
  13.0 40.6 %collective-permute-start = (bf16[256,2048]{1,0:T(8,128)(2,1)}, bf16[256,2048]{1,0:T(8,128)(2,1)S(1)}, u32[]{:S(2)}, u32[]{:S(2)}) collective-permute-start(bf16[256,2048]{1,0:T(8,128)(2,1)} %constant_dynamic-slice_fusion), channel_id=1, source_target_pairs={{0,4},{4,0},{8,12},{12,8},{16,20},{20,16},{24,28},{28,24},{1,5},{5... | collective-permute-start | bytes 3145736 | tf_op jit(solution)/shard_map/ppermute | solution.py:316
  37.1 18.4 %all-to-all-start.1 = ((bf16[8,128,256]{2,1,0:T(8,128)(2,1)}), bf16[8,128,256]{2,1,0:T(8,128)(2,1)}, u32[]{:S(2)}, u32[]{:S(2)}) async-start(bf16[8,128,256]{2,1,0:T(8,128)(2,1)} %copy-done.6), calls=%async_computation.1 | async-start | bytes 1048576 | tf_op jit(solution)/shard_map/all_to_all | solution.py:561
  60.2 14.3 %collective-permute-start.3 = (bf16[128,2048]{1,0:T(8,128)(2,1)}, bf16[128,2048]{1,0:T(8,128)(2,1)}, u32[]{:S(2)}, u32[]{:S(2)}) collective-permute-start(bf16[128,2048]{1,0:T(8,128)(2,1)} %add_convert_fusion.1), channel_id=1, source_target_pairs={{0,2},{1,3},{2,0},{3,1},{4,6},{5,7},{6,4},{7,5},{8,10},{9,11},{10,... | collective-permute-start | bytes 1572872 | tf_op jit(solution)/shard_map/ppermute | solution.py:316
  75.9 16.0 %collective-permute-start.6 = (bf16[128,2048]{1,0:T(8,128)(2,1)S(1)}, bf16[128,2048]{1,0:T(8,128)(2,1)S(1)}, u32[]{:S(2)}, u32[]{:S(2)}) collective-permute-start(bf16[128,2048]{1,0:T(8,128)(2,1)S(1)} %get-tuple-element.65.refs_0_), channel_id=1, source_target_pairs={{0,4},{4,0},{8,12},{12,8},{16,20},{20,16},{24,28},{28,24},{1,5},{5... | collective-permute-start | bytes 1572872 | tf_op jit(solution)/shard_map/ppermute | solution.py:316
  77.4 36.5 %collective-permute-start.15 = (bf16[256,2048]{1,0:T(8,128)(2,1)S(1)}, bf16[256,2048]{1,0:T(8,128)(2,1)S(1)}, u32[]{:S(2)}, u32[]{:S(2)}) collective-permute-start(bf16[256,2048]{1,0:T(8,128)(2,1)S(1)} %collective-permute-done.refs_3_), channel_id=1, source_target_pairs={{0,2},{1,3},{2,0},{3,1},{4,6},{5,7},{6,4},{7,5},{8,10},{9,11},{10,... | collective-permute-start | bytes 3145736 | tf_op jit(solution)/shard_map/ppermute | solution.py:316
  78.9 12.8 %collective-permute-start.4 = (bf16[64,2048]{1,0:T(8,128)(2,1)S(1)}, bf16[64,2048]{1,0:T(8,128)(2,1)S(1)}, u32[]{:S(2)}, u32[]{:S(2)}) collective-permute-start(bf16[64,2048]{1,0:T(8,128)(2,1)S(1)} %get-tuple-element.66), channel_id=1, source_target_pairs={{0,16},{4,20},{8,24},{12,28},{16,0},{20,4},{24,8},{28,12},{1,17},{... | collective-permute-start | bytes 786440 | tf_op jit(solution)/shard_map/ppermute | solution.py:316
  79.6 12.3 %collective-permute-start.5 = (bf16[64,2048]{1,0:T(8,128)(2,1)S(1)}, bf16[64,2048]{1,0:T(8,128)(2,1)S(1)}, u32[]{:S(2)}, u32[]{:S(2)}) collective-permute-start(bf16[64,2048]{1,0:T(8,128)(2,1)S(1)} %get-tuple-element.66), channel_id=1, source_target_pairs={{0,8},{4,12},{8,0},{12,4},{16,24},{20,28},{24,16},{28,20},{1,9},{5... | collective-permute-start | bytes 786440 | tf_op jit(solution)/shard_map/ppermute | solution.py:316
  91.9 14.3 %collective-permute-start.7 = (bf16[64,2048]{1,0:T(8,128)(2,1)S(1)}, bf16[64,2048]{1,0:T(8,128)(2,1)S(1)}, u32[]{:S(2)}, u32[]{:S(2)}) collective-permute-start(bf16[64,2048]{1,0:T(8,128)(2,1)S(1)} %get-tuple-element.76), channel_id=1, source_target_pairs={{0,16},{4,20},{8,24},{12,28},{16,0},{20,4},{24,8},{28,12},{1,17},{... | collective-permute-start | bytes 786440 | tf_op jit(solution)/shard_map/ppermute | solution.py:316
  92.2 14.0 %collective-permute-start.10 = (bf16[64,2048]{1,0:T(8,128)(2,1)S(1)}, bf16[64,2048]{1,0:T(8,128)(2,1)S(1)}, u32[]{:S(2)}, u32[]{:S(2)}) collective-permute-start(bf16[64,2048]{1,0:T(8,128)(2,1)S(1)} %collective-permute-done.5.refs_1_), channel_id=1, source_target_pairs={{0,4},{4,0},{8,12},{12,8},{16,20},{20,16},{24,28},{28,24},{1,5},{5... | collective-permute-start | bytes 786440 | tf_op jit(solution)/shard_map/ppermute | solution.py:316
  93.7 12.9 %collective-permute-start.8 = (bf16[64,2048]{1,0:T(8,128)(2,1)S(1)}, bf16[64,2048]{1,0:T(8,128)(2,1)S(1)}, u32[]{:S(2)}, u32[]{:S(2)}) collective-permute-start(bf16[64,2048]{1,0:T(8,128)(2,1)S(1)} %collective-permute-done.4.refs_0_), channel_id=1, source_target_pairs={{0,8},{4,12},{8,0},{12,4},{16,24},{20,28},{24,16},{28,20},{1,9},{5... | collective-permute-start | bytes 786440 | tf_op jit(solution)/shard_map/ppermute | solution.py:316
  95.4 11.2 %collective-permute-start.9 = (bf16[64,2048]{1,0:T(8,128)(2,1)S(1)}, bf16[64,2048]{1,0:T(8,128)(2,1)S(1)}, u32[]{:S(2)}, u32[]{:S(2)}) collective-permute-start(bf16[64,2048]{1,0:T(8,128)(2,1)S(1)} %collective-permute-done.4.refs_0_), channel_id=1, source_target_pairs={{0,4},{4,0},{8,12},{12,8},{16,20},{20,16},{24,28},{28,24},{1,5},{5... | collective-permute-start | bytes 786440 | tf_op jit(solution)/shard_map/ppermute | solution.py:316
  106.6 13.4 %collective-permute-start.11 = (bf16[64,2048]{1,0:T(8,128)(2,1)S(1)}, bf16[64,2048]{1,0:T(8,128)(2,1)S(1)}, u32[]{:S(2)}, u32[]{:S(2)}) collective-permute-start(bf16[64,2048]{1,0:T(8,128)(2,1)S(1)} %collective-permute-done.7.refs_0_), channel_id=1, source_target_pairs={{0,8},{4,12},{8,0},{12,4},{16,24},{20,28},{24,16},{28,20},{1,9},{5... | collective-permute-start | bytes 786440 | tf_op jit(solution)/shard_map/ppermute | solution.py:316
  108.1 11.9 %collective-permute-start.12 = (bf16[64,2048]{1,0:T(8,128)(2,1)S(1)}, bf16[64,2048]{1,0:T(8,128)(2,1)S(1)}, u32[]{:S(2)}, u32[]{:S(2)}) collective-permute-start(bf16[64,2048]{1,0:T(8,128)(2,1)S(1)} %get-tuple-element.76), channel_id=1, source_target_pairs={{0,8},{4,12},{8,0},{12,4},{16,24},{20,28},{24,16},{28,20},{1,9},{5... | collective-permute-start | bytes 786440 | tf_op jit(solution)/shard_map/ppermute | solution.py:316
  108.6 11.4 %collective-permute-start.13 = (bf16[64,2048]{1,0:T(8,128)(2,1)S(1)}, bf16[64,2048]{1,0:T(8,128)(2,1)S(1)}, u32[]{:S(2)}, u32[]{:S(2)}) collective-permute-start(bf16[64,2048]{1,0:T(8,128)(2,1)S(1)} %collective-permute-done.7.refs_0_), channel_id=1, source_target_pairs={{0,4},{4,0},{8,12},{12,8},{16,20},{20,16},{24,28},{28,24},{1,5},{5... | collective-permute-start | bytes 786440 | tf_op jit(solution)/shard_map/ppermute | solution.py:316
  110.0 11.4 %collective-permute-start.14 = (bf16[64,2048]{1,0:T(8,128)(2,1)S(1)}, bf16[64,2048]{1,0:T(8,128)(2,1)S(1)}, u32[]{:S(2)}, u32[]{:S(2)}) collective-permute-start(bf16[64,2048]{1,0:T(8,128)(2,1)S(1)} %collective-permute-done.8.refs_1_), channel_id=1, source_target_pairs={{0,4},{4,0},{8,12},{12,8},{16,20},{20,16},{24,28},{28,24},{1,5},{5... | collective-permute-start | bytes 786440 | tf_op jit(solution)/shard_map/ppermute | solution.py:316
  113.9 22.3 %collective-permute-start.18 = (bf16[256,2048]{1,0:T(8,128)(2,1)S(1)}, bf16[256,2048]{1,0:T(8,128)(2,1)S(1)}, u32[]{:S(2)}, u32[]{:S(2)}) collective-permute-start(bf16[256,2048]{1,0:T(8,128)(2,1)S(1)} %collective-permute-done.refs_3_), channel_id=1, source_target_pairs={{0,1},{1,0},{2,3},{3,2},{4,5},{5,4},{6,7},{7,6},{8,9},{9,8},{10,11... | collective-permute-start | bytes 3145736 | tf_op jit(solution)/shard_map/ppermute | solution.py:316
  121.5 14.7 %collective-permute-start.19 = (bf16[256,2048]{1,0:T(8,128)(2,1)S(1)}, bf16[256,2048]{1,0:T(8,128)(2,1)S(1)}, u32[]{:S(2)}, u32[]{:S(2)}) collective-permute-start(bf16[256,2048]{1,0:T(8,128)(2,1)S(1)} %collective-permute-done.15.refs_5_), channel_id=1, source_target_pairs={{0,1},{1,0},{2,3},{3,2},{4,5},{5,4},{6,7},{7,6},{8,9},{9,8},{10,11... | collective-permute-start | bytes 3145736 | tf_op jit(solution)/shard_map/ppermute | solution.py:316
  133.4 11.3 %collective-permute-start.24 = (bf16[64,2048]{1,0:T(8,128)(2,1)S(1)}, bf16[64,2048]{1,0:T(8,128)(2,1)S(1)}, u32[]{:S(2)}, u32[]{:S(2)}) collective-permute-start(bf16[64,2048]{1,0:T(8,128)(2,1)S(1)} %collective-permute-done.12.refs_0_), channel_id=1, source_target_pairs={{0,4},{4,0},{8,12},{12,8},{16,20},{20,16},{24,28},{28,24},{1,5},{5... | collective-permute-start | bytes 786440 | tf_op jit(solution)/shard_map/ppermute | solution.py:316
  152.6 18.9 %collective-permute-start.30 = (bf16[64,2048]{1,0:T(8,128)(2,1)S(1)}, bf16[64,2048]{1,0:T(8,128)(2,1)S(1)}, u32[]{:S(2)}, u32[]{:S(2)}) collective-permute-start(bf16[64,2048]{1,0:T(8,128)(2,1)S(1)} %add_convert_fusion.2), channel_id=1, source_target_pairs={{0,16},{4,20},{8,24},{12,28},{16,0},{20,4},{24,8},{28,12},{1,17},{... | collective-permute-start | bytes 786440 | tf_op jit(solution)/shard_map/ppermute | solution.py:316
  153.7 11.5 %collective-permute-start.25 = (bf16[128,1024]{1,0:T(8,128)(2,1)S(1)}, bf16[128,1024]{1,0:T(8,128)(2,1)S(1)}, u32[]{:S(2)}, u32[]{:S(2)}) collective-permute-start(bf16[128,1024]{1,0:T(8,128)(2,1)S(1)} %get-tuple-element.105), channel_id=1, source_target_pairs={{0,4},{4,0},{8,12},{12,8},{16,20},{20,16},{24,28},{28,24},{1,5},{5... | collective-permute-start | bytes 786440 | tf_op jit(solution)/shard_map/ppermute | solution.py:316
  156.5 14.9 %collective-permute-start.28 = (bf16[64,2048]{1,0:T(8,128)(2,1)S(1)}, bf16[64,2048]{1,0:T(8,128)(2,1)S(1)}, u32[]{:S(2)}, u32[]{:S(2)}) collective-permute-start(bf16[64,2048]{1,0:T(8,128)(2,1)S(1)} %mlp_down.8), channel_id=1, source_target_pairs={{0,8},{4,12},{8,0},{12,4},{16,24},{20,28},{24,16},{28,20},{1,9},{5... | collective-permute-start | bytes 786440 | tf_op jit(solution)/shard_map/ppermute | solution.py:316
  158.2 19.5 %collective-permute-start.29 = (bf16[64,2048]{1,0:T(8,128)(2,1)S(1)}, bf16[64,2048]{1,0:T(8,128)(2,1)S(1)}, u32[]{:S(2)}, u32[]{:S(2)}) collective-permute-start(bf16[64,2048]{1,0:T(8,128)(2,1)S(1)} %add_convert_fusion.3), channel_id=1, source_target_pairs={{0,16},{4,20},{8,24},{12,28},{16,0},{20,4},{24,8},{28,12},{1,17},{... | collective-permute-start | bytes 786440 | tf_op jit(solution)/shard_map/ppermute | solution.py:316
  159.8 20.0 %collective-permute-start.27 = (bf16[64,2048]{1,0:T(8,128)(2,1)S(1)}, bf16[64,2048]{1,0:T(8,128)(2,1)S(1)}, u32[]{:S(2)}, u32[]{:S(2)}) collective-permute-start(bf16[64,2048]{1,0:T(8,128)(2,1)S(1)} %get-tuple-element.109), channel_id=1, source_target_pairs={{0,8},{4,12},{8,0},{12,4},{16,24},{20,28},{24,16},{28,20},{1,9},{5... | collective-permute-start | bytes 786440 | tf_op jit(solution)/shard_map/ppermute | solution.py:316
  (32 other events, 293.1 us)

commit v4 on v3

--- a/solution.py
+++ b/solution.py
@@ -463,23 +463,23 @@
     far_a = send(own_a, bit=4)
     near_a = send(own_a, bit=2)
     side = send(own, bit=1)
-    far_a, near_a, side = sync(far_a, near_a, side)
+    side, near_a, far_a = sync(side, near_a, far_a)
     far_b = send(after(own_b, far_a), bit=4)
     both_a = send(far_a, bit=2)
     side_far_a = send(far_a, bit=1)
     side_near_a = send(near_a, bit=1)
     over_down = over(after(side_down, own))
     hidden_own, theirs_own = up([own], [side])
-    far_b, both_a, side_far_a, side_near_a, _ = sync(
-        far_b, both_a, side_far_a, side_near_a, hidden_own
+    side_far_a, side_near_a, far_b, both_a, _ = sync(
+        side_far_a, side_near_a, far_b, both_a, hidden_own
     )
     both_b = send(far_b, bit=2)
     near_b = send(after(own_b, far_b), bit=2)
     side_far_b = send(far_b, bit=1)
     side_both_a = send(both_a, bit=1)
     hidden_a, theirs_a = up([far_a, near_a], [side_far_a, side_near_a])
-    both_b, near_b, side_far_b, side_both_a, over_down, _ = sync(
-        both_b, near_b, side_far_b, side_both_a, over_down, hidden_a
+    side_both_a, side_far_b, both_b, near_b, over_down, _ = sync(
+        side_both_a, side_far_b, both_b, near_b, over_down, hidden_a
     )
     side_both_b = send(both_b, bit=1)
     pieces = [side_down, cross(side_down), over_down, cross(over_down)]

time: 181 us -> 176 us (0.972)
  waiting for transfers between devices: 68 us -> 62.3 us
    ppermute x31, waiting for transfers between devices: 56.8 us -> 51.3 us  [swap(): return lax.ppermute(values, axis, [(at, at ^ bit) for at in range(size)])]
  transfers between devices with their start and end apart: 33 -> 33, of which waited for: 19 -> 20; matrix products, arithmetic and copies ran while one was open for 5% -> 5% of each run, Pallas kernels for 25% -> 26%
where the time goes in v4:
time: 176 us
  waiting for transfers between devices  62.3 us (35%)
  Pallas kernels  49.1 us (28%)
  starting transfers between devices  44.4 us (25%)
  local copies, waits for them, and re-layouts  10.2 us (6%)
  matrix products  5.84 us (3%)
  other arithmetic  2.91 us (2%)
    ppermute x31, waiting for transfers between devices, swap(): return lax.ppermute(values, axis, [(at, at ^ bit) for at in range(size)])  51.3 us
    ppermute x31, starting transfers between devices, swap(): return lax.ppermute(values, axis, [(at, at ^ bit) for at in range(size)])  32.7 us
    pallas_call x5, Pallas kernels, mlp_up(): pl.pallas_call(functools.partial(up_kernel, count), out_shape=[jax.ShapeD...  13.5 us
    pallas_call x1, Pallas kernels, attend(): pl.pallas_call(attention_kernel, out_shape=jax.ShapeDtypeStruct(result, B...  12.2 us
    pallas_call x5, Pallas kernels, mlp_down(): pl.pallas_call(functools.partial(down_kernel, len(pieces)), out_shape=[ja...  9.62 us
    all_to_all x1, waiting for transfers between devices, body(): lax.all_to_all(packed, 'req', split_axis=0, concat_axis=0, tiled=True)  9.13 us
    unnamed x46, local copies, waits for them, and re-layouts  7.7 us
    all_to_all x1, starting transfers between devices, body(): lax.all_to_all(packed, 'req', split_axis=0, concat_axis=0, tiled=True)  7.41 us
  transfers between devices with their start and end apart: 33, of which 20 were waited for; matrix products, arithmetic and copies ran while one was open for 5% of the time, Pallas kernels for 26%

profile of v4, /device:TPU:0, one launch (start us, length us, event | category | flops | bytes accessed | tf_op | source)
XLA Modules:
  0.0 175.7 jit_solution(3825726761645832552)
XLA Ops:
  0.6 2.5 %pack_pages.1 = bf16[8,528,128]{2,1,0:T(8,128)(2,1)} custom-call(s32[128]{0:T(128)} %bitcast.28, s32[8]{0:T(128)} %bitcast.30, bf16[128,16,128]{2,1,0:T(8,128)(2,1)} %cache_k.3, bf16[128,16,128]{2,1,0:T(8,128)(2,1)} %cache_v.3), custom_call_target="tpu_custom_call" | custom-call | tf_op jit(solution)/shard_map/pack_pages/pallas_call | solution.py:71
  3.1 7.4 %all-to-all-start = ((bf16[8,528,128]{2,1,0:T(8,128)(2,1)}), bf16[8,528,128]{2,1,0:T(8,128)(2,1)}, u32[]{:S(2)}, u32[]{:S(2)}) async-start(bf16[8,528,128]{2,1,0:T(8,128)(2,1)} %pack_pages.1), calls=%async_computation | async-start | bytes 2162688 | tf_op jit(solution)/shard_map/all_to_all | solution.py:554
  10.6 2.5 %constant_dynamic-slice_fusion = bf16[256,2048]{1,0:T(8,128)(2,1)} fusion(bf16[1024,2048]{1,0:T(8,128)(2,1)} %refs_2_.15, s32[]{:T(128)S(6)} %select_n.60), kind=kLoop, calls=%fused_computation.32 | loop fusion | bytes 2097156 | tf_op jit(solution)/shard_map/dynamic_slice | solution.py:446
  20.5 5.7 %project.1 = (bf16[8,128,512]{2,1,0:T(8,128)(2,1)S(1)}, bf16[8,128,256]{2,1,0:T(8,128)(2,1)S(1)}) custom-call(s32[8]{0:T(128)S(1)} %get-tuple-element.114.starts, s32[8]{0:T(128)S(1)} %get-tuple-element.113.counts, bf16[512,2048]{1,0:T(8,128)(2,1)S(1)} %copy-done.4, f32[1,2048]{1,0:T(1,128)S(1)} %bitcast.26, bf16[2048,512]{1,0:T(8,128)(2,1)S(1)} %copy-done.5, ...), custom_call_target="tpu_custom_call" | custom-call | tf_op jit(solution)/shard_map/project/pallas_call | solution.py:118
  28.0 9.1 %all-to-all-done.pages = bf16[8,528,128]{2,1,0:T(8,128)(2,1)} async-done(((bf16[8,528,128]{2,1,0:T(8,128)(2,1)}), bf16[8,528,128]{2,1,0:T(8,128)(2,1)}, u32[]{:S(2)}, u32[]{:S(2)}) %all-to-all-start) | async-done | bytes 1081376 | tf_op jit(solution)/shard_map/all_to_all | solution.py:554
  37.1 4.3 %all-to-all-start.1 = ((bf16[8,128,256]{2,1,0:T(8,128)(2,1)}), bf16[8,128,256]{2,1,0:T(8,128)(2,1)}, u32[]{:S(2)}, u32[]{:S(2)}) async-start(bf16[8,128,256]{2,1,0:T(8,128)(2,1)} %copy-done.6), calls=%async_computation.1 | async-start | bytes 1048576 | tf_op jit(solution)/shard_map/all_to_all | solution.py:561
  41.5 12.2 %attend.1 = bf16[4,128,512]{2,1,0:T(8,128)(2,1)} custom-call(s32[8]{0:T(128)} %copy-done.17, s32[8]{0:T(128)} %copy-done.16, s32[1]{0:T(128)} %bitcast.group, bf16[8,128,512]{2,1,0:T(8,128)(2,1)} %copy-done.11, bf16[8,128,256]{2,1,0:T(8,128)(2,1)} %copy-done.6, bf16[8,528,128]{2,1,0:T(8,128)(2,1)} %all-to-all-done.pages, ...), custom_call_target="tpu_custom_call" | custom-call | tf_op jit(solution)/shard_map/attend/pallas_call | solution.py:244
  63.7 10.8 %collective-permute-done.3.over = bf16[128,2048]{1,0:T(8,128)(2,1)} collective-permute-done((bf16[128,2048]{1,0:T(8,128)(2,1)}, bf16[128,2048]{1,0:T(8,128)(2,1)}, u32[]{:S(2)}, u32[]{:S(2)}) %collective-permute-start.3) | collective-permute-done | bytes 524320 | tf_op jit(solution)/shard_map/ppermute | solution.py:316
  78.9 2.2 %collective-permute-start.6 = (bf16[64,2048]{1,0:T(8,128)(2,1)S(1)}, bf16[64,2048]{1,0:T(8,128)(2,1)S(1)}, u32[]{:S(2)}, u32[]{:S(2)}) collective-permute-start(bf16[64,2048]{1,0:T(8,128)(2,1)S(1)} %get-tuple-element.66), channel_id=1, source_target_pairs={{0,16},{4,20},{8,24},{12,28},{16,0},{20,4},{24,8},{28,12},{1,17},{... | collective-permute-start | bytes 786440 | tf_op jit(solution)/shard_map/ppermute | solution.py:316
  81.0 9.7 %collective-permute-done.5.refs_1_ = bf16[64,2048]{1,0:T(8,128)(2,1)S(1)} collective-permute-done((bf16[64,2048]{1,0:T(8,128)(2,1)S(1)}, bf16[64,2048]{1,0:T(8,128)(2,1)S(1)}, u32[]{:S(2)}, u32[]{:S(2)}) %collective-permute-start.5) | collective-permute-done | bytes 262176 | tf_op jit(solution)/shard_map/ppermute | solution.py:316
  92.4 2.5 %collective-permute-start.9 = (bf16[64,2048]{1,0:T(8,128)(2,1)S(1)}, bf16[64,2048]{1,0:T(8,128)(2,1)S(1)}, u32[]{:S(2)}, u32[]{:S(2)}) collective-permute-start(bf16[64,2048]{1,0:T(8,128)(2,1)S(1)} %get-tuple-element.76), channel_id=1, source_target_pairs={{0,16},{4,20},{8,24},{12,28},{16,0},{20,4},{24,8},{28,12},{1,17},{... | collective-permute-start | bytes 786440 | tf_op jit(solution)/shard_map/ppermute | solution.py:316
  96.9 2.2 %copy-done.3 = bf16[2048,1024]{1,0:T(8,128)(2,1)S(1)} copy-done((bf16[2048,1024]{1,0:T(8,128)(2,1)S(1)}, bf16[2048,1024]{1,0:T(8,128)(2,1)}, u32[]{:S(2)}) %copy-start.3) | copy-done | bytes 4194328
  99.1 3.1 %mlp_up.5 = (bf16[128,1024]{1,0:T(8,128)(2,1)S(1)}, bf16[128,1024]{1,0:T(8,128)(2,1)S(1)}) custom-call(bf16[128,2048]{1,0:T(8,128)(2,1)S(1)} %get-tuple-element.65.refs_0_, bf16[128,2048]{1,0:T(8,128)(2,1)S(1)} %collective-permute-done.4.refs_1_, bf16[2048,1024]{1,0:T(8,128)(2,1)S(1)} %copy-done.2, bf16[2048,1024]{1,0:T(8,128)(2,1)S(1)} %copy-done.3), custom_call_target="tpu_custom_call" | custom-call | tf_op jit(solution)/shard_map/mlp_up/pallas_call | solution.py:390
  102.2 2.4 %collective-permute-done.9.refs_0_ = bf16[64,2048]{1,0:T(8,128)(2,1)S(1)} collective-permute-done((bf16[64,2048]{1,0:T(8,128)(2,1)S(1)}, bf16[64,2048]{1,0:T(8,128)(2,1)S(1)}, u32[]{:S(2)}, u32[]{:S(2)}) %collective-permute-start.9) | collective-permute-done | bytes 262176 | tf_op jit(solution)/shard_map/ppermute | solution.py:316
  109.2 3.2 %mlp_up.6 = (bf16[128,1024]{1,0:T(8,128)(2,1)S(1)}, bf16[128,1024]{1,0:T(8,128)(2,1)S(1)}) custom-call(bf16[64,2048]{1,0:T(8,128)(2,1)S(1)} %collective-permute-done.6.refs_0_, bf16[64,2048]{1,0:T(8,128)(2,1)S(1)} %collective-permute-done.5.refs_1_, bf16[64,2048]{1,0:T(8,128)(2,1)S(1)} %collective-permute-done.7.refs_2_, ...), custom_call_target="tpu_custom_call" | custom-call | tf_op jit(solution)/shard_map/mlp_up/pallas_call | solution.py:390
  113.4 2.8 %collective-permute-done.12.refs_2_ = bf16[64,2048]{1,0:T(8,128)(2,1)S(1)} collective-permute-done((bf16[64,2048]{1,0:T(8,128)(2,1)S(1)}, bf16[64,2048]{1,0:T(8,128)(2,1)S(1)}, u32[]{:S(2)}, u32[]{:S(2)}) %collective-permute-start.12) | collective-permute-done | bytes 262176 | tf_op jit(solution)/shard_map/ppermute | solution.py:316
  117.6 3.2 %mlp_up.7 = (bf16[128,1024]{1,0:T(8,128)(2,1)S(1)}, bf16[128,1024]{1,0:T(8,128)(2,1)S(1)}) custom-call(bf16[64,2048]{1,0:T(8,128)(2,1)S(1)} %collective-permute-done.9.refs_0_, bf16[64,2048]{1,0:T(8,128)(2,1)S(1)} %collective-permute-done.10.refs_1_, bf16[64,2048]{1,0:T(8,128)(2,1)S(1)} %collective-permute-done.12.refs_2_, ...), custom_call_target="tpu_custom_call" | custom-call | tf_op jit(solution)/shard_map/mlp_up/pallas_call | solution.py:390
  121.5 3.8 %collective-permute-done.17.refs_1_ = bf16[64,2048]{1,0:T(8,128)(2,1)S(1)} collective-permute-done((bf16[64,2048]{1,0:T(8,128)(2,1)S(1)}, bf16[64,2048]{1,0:T(8,128)(2,1)S(1)}, u32[]{:S(2)}, u32[]{:S(2)}) %collective-permute-start.17) | collective-permute-done | bytes 262176 | tf_op jit(solution)/shard_map/ppermute | solution.py:316
  125.4 2.0 %mlp_up.8 = (bf16[64,1024]{1,0:T(8,128)(2,1)S(1)}, bf16[64,1024]{1,0:T(8,128)(2,1)S(1)}) custom-call(bf16[64,2048]{1,0:T(8,128)(2,1)S(1)} %collective-permute-done.13.refs_0_, bf16[64,2048]{1,0:T(8,128)(2,1)S(1)} %collective-permute-done.17.refs_1_, bf16[2048,1024]{1,0:T(8,128)(2,1)S(1)} %copy-done.2, bf16[2048,1024]{1,0:T(8,128)(2,1)S(1)} %copy-done.3), custom_call_target="tpu_custom_call" | custom-call | tf_op jit(solution)/shard_map/mlp_up/pallas_call | solution.py:390
  143.0 2.2 %collective-permute-done.22.refs_1_ = bf16[128,1024]{1,0:T(8,128)(2,1)S(1)} collective-permute-done((bf16[128,1024]{1,0:T(8,128)(2,1)S(1)}, bf16[128,1024]{1,0:T(8,128)(2,1)S(1)}, u32[]{:S(2)}, u32[]{:S(2)}) %collective-permute-start.22) | collective-permute-done | bytes 262176 | tf_op jit(solution)/shard_map/ppermute | solution.py:316
  155.9 4.1 %store_new.1 = (bf16[128,16,128]{2,1,0:T(8,128)(2,1)}, bf16[128,16,128]{2,1,0:T(8,128)(2,1)}) custom-call(s32[128]{0:T(128)S(1)} %bitcast.29, s32[8]{0:T(128)S(1)} %bitcast.31, s32[8]{0:T(128)S(1)} %bitcast.32, bf16[8,128,256]{2,1,0:T(8,128)(2,1)} %all-to-all-done.1.new, f32[384,128]{1,0:T(8,128)S(1)} %copy-done.10, f32[384,128]{1,0:T(8,128)S(1)} %copy-done.9, ...), custom_call_target="tpu_custom_call" | custom-call | tf_op jit(solution)/shard_map/store_new/pallas_call | solution.py:304
  161.9 5.8 %collective-permute-done.28 = bf16[64,2048]{1,0:T(8,128)(2,1)S(1)} collective-permute-done((bf16[64,2048]{1,0:T(8,128)(2,1)S(1)}, bf16[64,2048]{1,0:T(8,128)(2,1)S(1)}, u32[]{:S(2)}, u32[]{:S(2)}) %collective-permute-start.28) | collective-permute-done | bytes 262176 | tf_op jit(solution)/shard_map/ppermute | solution.py:316
  167.7 4.8 %collective-permute-done.29 = bf16[64,2048]{1,0:T(8,128)(2,1)S(1)} collective-permute-done((bf16[64,2048]{1,0:T(8,128)(2,1)S(1)}, bf16[64,2048]{1,0:T(8,128)(2,1)S(1)}, u32[]{:S(2)}, u32[]{:S(2)}) %collective-permute-start.29) | collective-permute-done | bytes 262176 | tf_op jit(solution)/shard_map/ppermute | solution.py:316
  172.5 2.1 %collective-permute-done.27 = bf16[64,2048]{1,0:T(8,128)(2,1)S(1)} collective-permute-done((bf16[64,2048]{1,0:T(8,128)(2,1)S(1)}, bf16[64,2048]{1,0:T(8,128)(2,1)S(1)}, u32[]{:S(2)}, u32[]{:S(2)}) %collective-permute-start.27) | collective-permute-done | bytes 262176 | tf_op jit(solution)/shard_map/ppermute | solution.py:316
  (115 shorter events, 63.9 us)
Async XLA Ops:
  3.1 34.0 %all-to-all-start = ((bf16[8,528,128]{2,1,0:T(8,128)(2,1)}), bf16[8,528,128]{2,1,0:T(8,128)(2,1)}, u32[]{:S(2)}, u32[]{:S(2)}) async-start(bf16[8,528,128]{2,1,0:T(8,128)(2,1)} %pack_pages.1), calls=%async_computation | async-start | bytes 2162688 | tf_op jit(solution)/shard_map/all_to_all | solution.py:554
  13.0 40.7 %collective-permute-start = (bf16[256,2048]{1,0:T(8,128)(2,1)}, bf16[256,2048]{1,0:T(8,128)(2,1)S(1)}, u32[]{:S(2)}, u32[]{:S(2)}) collective-permute-start(bf16[256,2048]{1,0:T(8,128)(2,1)} %constant_dynamic-slice_fusion), channel_id=1, source_target_pairs={{0,4},{4,0},{8,12},{12,8},{16,20},{20,16},{24,28},{28,24},{1,5},{5... | collective-permute-start | bytes 3145736 | tf_op jit(solution)/shard_map/ppermute | solution.py:316
  37.1 18.4 %all-to-all-start.1 = ((bf16[8,128,256]{2,1,0:T(8,128)(2,1)}), bf16[8,128,256]{2,1,0:T(8,128)(2,1)}, u32[]{:S(2)}, u32[]{:S(2)}) async-start(bf16[8,128,256]{2,1,0:T(8,128)(2,1)} %copy-done.6), calls=%async_computation.1 | async-start | bytes 1048576 | tf_op jit(solution)/shard_map/all_to_all | solution.py:561
  60.2 14.3 %collective-permute-start.3 = (bf16[128,2048]{1,0:T(8,128)(2,1)}, bf16[128,2048]{1,0:T(8,128)(2,1)}, u32[]{:S(2)}, u32[]{:S(2)}) collective-permute-start(bf16[128,2048]{1,0:T(8,128)(2,1)} %add_convert_fusion.1), channel_id=1, source_target_pairs={{0,2},{1,3},{2,0},{3,1},{4,6},{5,7},{6,4},{7,5},{8,10},{9,11},{10,... | collective-permute-start | bytes 1572872 | tf_op jit(solution)/shard_map/ppermute | solution.py:316
  75.9 16.5 %collective-permute-start.4 = (bf16[128,2048]{1,0:T(8,128)(2,1)S(1)}, bf16[128,2048]{1,0:T(8,128)(2,1)S(1)}, u32[]{:S(2)}, u32[]{:S(2)}) collective-permute-start(bf16[128,2048]{1,0:T(8,128)(2,1)S(1)} %get-tuple-element.65.refs_0_), channel_id=1, source_target_pairs={{0,4},{4,0},{8,12},{12,8},{16,20},{20,16},{24,28},{28,24},{1,5},{5... | collective-permute-start | bytes 1572872 | tf_op jit(solution)/shard_map/ppermute | solution.py:316
  77.4 35.0 %collective-permute-start.15 = (bf16[256,2048]{1,0:T(8,128)(2,1)S(1)}, bf16[256,2048]{1,0:T(8,128)(2,1)S(1)}, u32[]{:S(2)}, u32[]{:S(2)}) collective-permute-start(bf16[256,2048]{1,0:T(8,128)(2,1)S(1)} %collective-permute-done.refs_3_), channel_id=1, source_target_pairs={{0,2},{1,3},{2,0},{3,1},{4,6},{5,7},{6,4},{7,5},{8,10},{9,11},{10,... | collective-permute-start | bytes 3145736 | tf_op jit(solution)/shard_map/ppermute | solution.py:316
  78.9 11.9 %collective-permute-start.5 = (bf16[64,2048]{1,0:T(8,128)(2,1)S(1)}, bf16[64,2048]{1,0:T(8,128)(2,1)S(1)}, u32[]{:S(2)}, u32[]{:S(2)}) collective-permute-start(bf16[64,2048]{1,0:T(8,128)(2,1)S(1)} %get-tuple-element.66), channel_id=1, source_target_pairs={{0,8},{4,12},{8,0},{12,4},{16,24},{20,28},{24,16},{28,20},{1,9},{5... | collective-permute-start | bytes 786440 | tf_op jit(solution)/shard_map/ppermute | solution.py:316
  78.9 13.5 %collective-permute-start.6 = (bf16[64,2048]{1,0:T(8,128)(2,1)S(1)}, bf16[64,2048]{1,0:T(8,128)(2,1)S(1)}, u32[]{:S(2)}, u32[]{:S(2)}) collective-permute-start(bf16[64,2048]{1,0:T(8,128)(2,1)S(1)} %get-tuple-element.66), channel_id=1, source_target_pairs={{0,16},{4,20},{8,24},{12,28},{16,0},{20,4},{24,8},{28,12},{1,17},{... | collective-permute-start | bytes 786440 | tf_op jit(solution)/shard_map/ppermute | solution.py:316
  92.4 12.3 %collective-permute-start.10 = (bf16[64,2048]{1,0:T(8,128)(2,1)S(1)}, bf16[64,2048]{1,0:T(8,128)(2,1)S(1)}, u32[]{:S(2)}, u32[]{:S(2)}) collective-permute-start(bf16[64,2048]{1,0:T(8,128)(2,1)S(1)} %collective-permute-done.6.refs_0_), channel_id=1, source_target_pairs={{0,8},{4,12},{8,0},{12,4},{16,24},{20,28},{24,16},{28,20},{1,9},{5... | collective-permute-start | bytes 786440 | tf_op jit(solution)/shard_map/ppermute | solution.py:316
  92.4 12.3 %collective-permute-start.9 = (bf16[64,2048]{1,0:T(8,128)(2,1)S(1)}, bf16[64,2048]{1,0:T(8,128)(2,1)S(1)}, u32[]{:S(2)}, u32[]{:S(2)}) collective-permute-start(bf16[64,2048]{1,0:T(8,128)(2,1)S(1)} %get-tuple-element.76), channel_id=1, source_target_pairs={{0,16},{4,20},{8,24},{12,28},{16,0},{20,4},{24,8},{28,12},{1,17},{... | collective-permute-start | bytes 786440 | tf_op jit(solution)/shard_map/ppermute | solution.py:316
  94.9 9.8 %collective-permute-start.7 = (bf16[64,2048]{1,0:T(8,128)(2,1)S(1)}, bf16[64,2048]{1,0:T(8,128)(2,1)S(1)}, u32[]{:S(2)}, u32[]{:S(2)}) collective-permute-start(bf16[64,2048]{1,0:T(8,128)(2,1)S(1)} %collective-permute-done.6.refs_0_), channel_id=1, source_target_pairs={{0,4},{4,0},{8,12},{12,8},{16,20},{20,16},{24,28},{28,24},{1,5},{5... | collective-permute-start | bytes 786440 | tf_op jit(solution)/shard_map/ppermute | solution.py:316
  95.4 9.8 %collective-permute-start.8 = (bf16[64,2048]{1,0:T(8,128)(2,1)S(1)}, bf16[64,2048]{1,0:T(8,128)(2,1)S(1)}, u32[]{:S(2)}, u32[]{:S(2)}) collective-permute-start(bf16[64,2048]{1,0:T(8,128)(2,1)S(1)} %collective-permute-done.5.refs_1_), channel_id=1, source_target_pairs={{0,4},{4,0},{8,12},{12,8},{16,20},{20,16},{24,28},{28,24},{1,5},{5... | collective-permute-start | bytes 786440 | tf_op jit(solution)/shard_map/ppermute | solution.py:316
  112.4 18.6 %collective-permute-start.18 = (bf16[256,2048]{1,0:T(8,128)(2,1)S(1)}, bf16[256,2048]{1,0:T(8,128)(2,1)S(1)}, u32[]{:S(2)}, u32[]{:S(2)}) collective-permute-start(bf16[256,2048]{1,0:T(8,128)(2,1)S(1)} %collective-permute-done.refs_3_), channel_id=1, source_target_pairs={{0,1},{1,0},{2,3},{3,2},{4,5},{5,4},{6,7},{7,6},{8,9},{9,8},{10,11... | collective-permute-start | bytes 3145736 | tf_op jit(solution)/shard_map/ppermute | solution.py:316
  116.3 14.7 %collective-permute-start.19 = (bf16[256,2048]{1,0:T(8,128)(2,1)S(1)}, bf16[256,2048]{1,0:T(8,128)(2,1)S(1)}, u32[]{:S(2)}, u32[]{:S(2)}) collective-permute-start(bf16[256,2048]{1,0:T(8,128)(2,1)S(1)} %collective-permute-done.15.refs_5_), channel_id=1, source_target_pairs={{0,1},{1,0},{2,3},{3,2},{4,5},{5,4},{6,7},{7,6},{8,9},{9,8},{10,11... | collective-permute-start | bytes 3145736 | tf_op jit(solution)/shard_map/ppermute | solution.py:316
  120.7 10.3 %collective-permute-start.16 = (bf16[128,1024]{1,0:T(8,128)(2,1)S(1)}, bf16[128,1024]{1,0:T(8,128)(2,1)S(1)}, u32[]{:S(2)}, u32[]{:S(2)}) collective-permute-start(bf16[128,1024]{1,0:T(8,128)(2,1)S(1)} %get-tuple-element.85), channel_id=1, source_target_pairs={{0,4},{4,0},{8,12},{12,8},{16,20},{20,16},{24,28},{28,24},{1,5},{5... | collective-permute-start | bytes 786440 | tf_op jit(solution)/shard_map/ppermute | solution.py:316
  128.8 10.8 %collective-permute-start.24 = (bf16[64,2048]{1,0:T(8,128)(2,1)S(1)}, bf16[64,2048]{1,0:T(8,128)(2,1)S(1)}, u32[]{:S(2)}, u32[]{:S(2)}) collective-permute-start(bf16[64,2048]{1,0:T(8,128)(2,1)S(1)} %collective-permute-done.14.refs_0_), channel_id=1, source_target_pairs={{0,4},{4,0},{8,12},{12,8},{16,20},{20,16},{24,28},{28,24},{1,5},{5... | collective-permute-start | bytes 786440 | tf_op jit(solution)/shard_map/ppermute | solution.py:316
  133.9 11.2 %collective-permute-start.22 = (bf16[128,1024]{1,0:T(8,128)(2,1)S(1)}, bf16[128,1024]{1,0:T(8,128)(2,1)S(1)}, u32[]{:S(2)}, u32[]{:S(2)}) collective-permute-start(bf16[128,1024]{1,0:T(8,128)(2,1)S(1)} %get-tuple-element.96), channel_id=1, source_target_pairs={{0,4},{4,0},{8,12},{12,8},{16,20},{20,16},{24,28},{28,24},{1,5},{5... | collective-permute-start | bytes 786440 | tf_op jit(solution)/shard_map/ppermute | solution.py:316
  135.2 9.9 %collective-permute-start.23 = (bf16[64,2048]{1,0:T(8,128)(2,1)S(1)}, bf16[64,2048]{1,0:T(8,128)(2,1)S(1)}, u32[]{:S(2)}, u32[]{:S(2)}) collective-permute-start(bf16[64,2048]{1,0:T(8,128)(2,1)S(1)} %get-tuple-element.93), channel_id=1, source_target_pairs={{0,8},{4,12},{8,0},{12,4},{16,24},{20,28},{24,16},{28,20},{1,9},{5... | collective-permute-start | bytes 786440 | tf_op jit(solution)/shard_map/ppermute | solution.py:316
  138.1 9.8 %collective-permute-start.21 = (bf16[64,2048]{1,0:T(8,128)(2,1)S(1)}, bf16[64,2048]{1,0:T(8,128)(2,1)S(1)}, u32[]{:S(2)}, u32[]{:S(2)}) collective-permute-start(bf16[64,2048]{1,0:T(8,128)(2,1)S(1)} %mlp_down.6), channel_id=1, source_target_pairs={{0,8},{4,12},{8,0},{12,4},{16,24},{20,28},{24,16},{28,20},{1,9},{5... | collective-permute-start | bytes 786440 | tf_op jit(solution)/shard_map/ppermute | solution.py:316
  147.9 19.8 %collective-permute-start.30 = (bf16[64,2048]{1,0:T(8,128)(2,1)S(1)}, bf16[64,2048]{1,0:T(8,128)(2,1)S(1)}, u32[]{:S(2)}, u32[]{:S(2)}) collective-permute-start(bf16[64,2048]{1,0:T(8,128)(2,1)S(1)} %add_convert_fusion.2), channel_id=1, source_target_pairs={{0,16},{4,20},{8,24},{12,28},{16,0},{20,4},{24,8},{28,12},{1,17},{... | collective-permute-start | bytes 786440 | tf_op jit(solution)/shard_map/ppermute | solution.py:316
  149.2 10.8 %collective-permute-start.25 = (bf16[128,1024]{1,0:T(8,128)(2,1)S(1)}, bf16[128,1024]{1,0:T(8,128)(2,1)S(1)}, u32[]{:S(2)}, u32[]{:S(2)}) collective-permute-start(bf16[128,1024]{1,0:T(8,128)(2,1)S(1)} %get-tuple-element.105), channel_id=1, source_target_pairs={{0,4},{4,0},{8,12},{12,8},{16,20},{20,16},{24,28},{28,24},{1,5},{5... | collective-permute-start | bytes 786440 | tf_op jit(solution)/shard_map/ppermute | solution.py:316
  152.8 14.9 %collective-permute-start.28 = (bf16[64,2048]{1,0:T(8,128)(2,1)S(1)}, bf16[64,2048]{1,0:T(8,128)(2,1)S(1)}, u32[]{:S(2)}, u32[]{:S(2)}) collective-permute-start(bf16[64,2048]{1,0:T(8,128)(2,1)S(1)} %mlp_down.8), channel_id=1, source_target_pairs={{0,8},{4,12},{8,0},{12,4},{16,24},{20,28},{24,16},{28,20},{1,9},{5... | collective-permute-start | bytes 786440 | tf_op jit(solution)/shard_map/ppermute | solution.py:316
  153.9 18.6 %collective-permute-start.29 = (bf16[64,2048]{1,0:T(8,128)(2,1)S(1)}, bf16[64,2048]{1,0:T(8,128)(2,1)S(1)}, u32[]{:S(2)}, u32[]{:S(2)}) collective-permute-start(bf16[64,2048]{1,0:T(8,128)(2,1)S(1)} %add_convert_fusion.3), channel_id=1, source_target_pairs={{0,16},{4,20},{8,24},{12,28},{16,0},{20,4},{24,8},{28,12},{1,17},{... | collective-permute-start | bytes 786440 | tf_op jit(solution)/shard_map/ppermute | solution.py:316
  155.0 19.6 %collective-permute-start.27 = (bf16[64,2048]{1,0:T(8,128)(2,1)S(1)}, bf16[64,2048]{1,0:T(8,128)(2,1)S(1)}, u32[]{:S(2)}, u32[]{:S(2)}) collective-permute-start(bf16[64,2048]{1,0:T(8,128)(2,1)S(1)} %get-tuple-element.109), channel_id=1, source_target_pairs={{0,8},{4,12},{8,0},{12,4},{16,24},{20,28},{24,16},{28,20},{1,9},{5... | collective-permute-start | bytes 786440 | tf_op jit(solution)/shard_map/ppermute | solution.py:316
  (32 other events, 279.2 us)

commit v5 on v4

--- a/solution.py
+++ b/solution.py
@@ -487,24 +487,25 @@
     hidden_b, theirs_b = up([far_b, both_a], [side_far_b, side_both_a])
     from_b = send(theirs_b, bit=1)
     side_both_b, _ = sync(side_both_b, hidden_b)
-    side_near_b = send(after(near_b, side_both_b), bit=1)
+    from_a = send(after(theirs_a, side_both_b), bit=1)
     hidden_c, theirs_c = up([both_b], [side_both_b])
     from_c = send(theirs_c, bit=1)
     from_b, _ = sync(from_b, hidden_c)
     sum_far_b, sum_both_a = down(hidden_b, from_b, [half, half])
     back_both_a = send(sum_both_a, bit=2)
     from_c, _ = sync(from_c, sum_both_a)
-    from_a = send(after(theirs_a, from_c), bit=1)
+    side_near_b = send(after(near_b, from_c), bit=1)
     (sum_both_b,) = down(hidden_c, from_c, [half])
     back_both_b = send(sum_both_b, bit=2)
-    side_near_b, _ = sync(side_near_b, sum_both_b)
+    from_a, _ = sync(from_a, sum_both_b)
+    sum_far_a, sum_near_a = down(hidden_a, from_a, [half, half])
+    back_near_a = send(sum_near_a, bit=2)
+    side_near_b, _ = sync(side_near_b, sum_near_a)
     hidden_d, theirs_d = up([near_b], [side_near_b])
     from_d = send(theirs_d, bit=1)
-    from_a, back_both_a, _ = sync(from_a, back_both_a, hidden_d)
-    sum_far_a, sum_near_a = down(hidden_a, from_a, [half, half])
+    back_both_a, _ = sync(back_both_a, hidden_d)
     total_a = add(sum_far_a, back_both_a).astype(BF)
     back_far_a = send(total_a, bit=4)
-    back_near_a = send(sum_near_a, bit=2)
     back_both_b, _ = sync(back_both_b, total_a)
     total_b = add(sum_far_b, back_both_b).astype(BF)
     back_far_b = send(total_b, bit=4)
@@ -567,7 +568,7 @@
     cross = out_of(mixed[3])
     later = after(mixed, cross)
     cross = to_home(cross, bit=1)
-    over = (out_of(mixed[2]).astype(F32) + cross.astype(F32)).astype(BF)
+    over = (out_of(later[2]).astype(F32) + cross.astype(F32)).astype(BF)
     over = to_home(over, bit=2)
     beside = to_home(out_of(later[1]), bit=1)
     own_rows = lax.dynamic_slice_in_dim(hidden_in, group_index * quarter, quarter, 0).astype(F32)

time: 176 us -> 176 us (level)
  transfers between devices with their start and end apart: 33 -> 33, of which waited for: 20 -> 19; matrix products, arithmetic and copies ran while one was open for 5% -> 5% of each run, Pallas kernels for 26% -> 26%
where the time goes in v5:
time: 176 us; the launch traced here: 175 us
  waiting for transfers between devices  61.8 us (35%)
  Pallas kernels  49 us (28%)
  starting transfers between devices  44.4 us (25%)
  local copies, waits for them, and re-layouts  10.2 us (6%)
  matrix products  5.84 us (3%)
  other arithmetic  2.91 us (2%)
    ppermute x31, waiting for transfers between devices, swap(): return lax.ppermute(values, axis, [(at, at ^ bit) for at in range(size)])  50.7 us
    ppermute x31, starting transfers between devices, swap(): return lax.ppermute(values, axis, [(at, at ^ bit) for at in range(size)])  32.7 us
    pallas_call x5, Pallas kernels, mlp_up(): pl.pallas_call(functools.partial(up_kernel, count), out_shape=[jax.ShapeD...  13.5 us
    pallas_call x1, Pallas kernels, attend(): pl.pallas_call(attention_kernel, out_shape=jax.ShapeDtypeStruct(result, B...  12.1 us
    pallas_call x5, Pallas kernels, mlp_down(): pl.pallas_call(functools.partial(down_kernel, len(pieces)), out_shape=[ja...  9.65 us
    all_to_all x1, waiting for transfers between devices, body(): lax.all_to_all(packed, 'req', split_axis=0, concat_axis=0, tiled=True)  9.13 us
    unnamed x46, local copies, waits for them, and re-layouts  7.71 us
    all_to_all x1, starting transfers between devices, body(): lax.all_to_all(packed, 'req', split_axis=0, concat_axis=0, tiled=True)  7.41 us
  transfers between devices with their start and end apart: 33, of which 19 were waited for; matrix products, arithmetic and copies ran while one was open for 5% of the time, Pallas kernels for 26%

profile of v5, /device:TPU:0, one launch (start us, length us, event | category | flops | bytes accessed | tf_op | source)
XLA Modules:
  0.0 175.2 jit_solution(14538941957866532486)
XLA Ops:
  0.6 2.5 %pack_pages.1 = bf16[8,528,128]{2,1,0:T(8,128)(2,1)} custom-call(s32[128]{0:T(128)} %bitcast.28, s32[8]{0:T(128)} %bitcast.30, bf16[128,16,128]{2,1,0:T(8,128)(2,1)} %cache_k.3, bf16[128,16,128]{2,1,0:T(8,128)(2,1)} %cache_v.3), custom_call_target="tpu_custom_call" | custom-call | tf_op jit(solution)/shard_map/pack_pages/pallas_call | solution.py:71
  3.1 7.4 %all-to-all-start = ((bf16[8,528,128]{2,1,0:T(8,128)(2,1)}), bf16[8,528,128]{2,1,0:T(8,128)(2,1)}, u32[]{:S(2)}, u32[]{:S(2)}) async-start(bf16[8,528,128]{2,1,0:T(8,128)(2,1)} %pack_pages.1), calls=%async_computation | async-start | bytes 2162688 | tf_op jit(solution)/shard_map/all_to_all | solution.py:555
  10.6 2.5 %constant_dynamic-slice_fusion = bf16[256,2048]{1,0:T(8,128)(2,1)} fusion(bf16[1024,2048]{1,0:T(8,128)(2,1)} %refs_2_.15, s32[]{:T(128)S(6)} %select_n.60), kind=kLoop, calls=%fused_computation.32 | loop fusion | bytes 2097156 | tf_op jit(solution)/shard_map/dynamic_slice | solution.py:446
  20.5 5.7 %project.1 = (bf16[8,128,512]{2,1,0:T(8,128)(2,1)S(1)}, bf16[8,128,256]{2,1,0:T(8,128)(2,1)S(1)}) custom-call(s32[8]{0:T(128)S(1)} %get-tuple-element.114.starts, s32[8]{0:T(128)S(1)} %get-tuple-element.113.counts, bf16[512,2048]{1,0:T(8,128)(2,1)S(1)} %copy-done.4, f32[1,2048]{1,0:T(1,128)S(1)} %bitcast.26, bf16[2048,512]{1,0:T(8,128)(2,1)S(1)} %copy-done.5, ...), custom_call_target="tpu_custom_call" | custom-call | tf_op jit(solution)/shard_map/project/pallas_call | solution.py:118
  28.0 9.1 %all-to-all-done.pages = bf16[8,528,128]{2,1,0:T(8,128)(2,1)} async-done(((bf16[8,528,128]{2,1,0:T(8,128)(2,1)}), bf16[8,528,128]{2,1,0:T(8,128)(2,1)}, u32[]{:S(2)}, u32[]{:S(2)}) %all-to-all-start) | async-done | bytes 1081376 | tf_op jit(solution)/shard_map/all_to_all | solution.py:555
  37.1 4.3 %all-to-all-start.1 = ((bf16[8,128,256]{2,1,0:T(8,128)(2,1)}), bf16[8,128,256]{2,1,0:T(8,128)(2,1)}, u32[]{:S(2)}, u32[]{:S(2)}) async-start(bf16[8,128,256]{2,1,0:T(8,128)(2,1)} %copy-done.6), calls=%async_computation.1 | async-start | bytes 1048576 | tf_op jit(solution)/shard_map/all_to_all | solution.py:562
  41.5 12.1 %attend.1 = bf16[4,128,512]{2,1,0:T(8,128)(2,1)} custom-call(s32[8]{0:T(128)} %copy-done.17, s32[8]{0:T(128)} %copy-done.16, s32[1]{0:T(128)} %bitcast.group, bf16[8,128,512]{2,1,0:T(8,128)(2,1)} %copy-done.11, bf16[8,128,256]{2,1,0:T(8,128)(2,1)} %copy-done.6, bf16[8,528,128]{2,1,0:T(8,128)(2,1)} %all-to-all-done.pages, ...), custom_call_target="tpu_custom_call" | custom-call | tf_op jit(solution)/shard_map/attend/pallas_call | solution.py:244
  63.7 10.8 %collective-permute-done.3.over = bf16[128,2048]{1,0:T(8,128)(2,1)} collective-permute-done((bf16[128,2048]{1,0:T(8,128)(2,1)}, bf16[128,2048]{1,0:T(8,128)(2,1)}, u32[]{:S(2)}, u32[]{:S(2)}) %collective-permute-start.3) | collective-permute-done | bytes 524320 | tf_op jit(solution)/shard_map/ppermute | solution.py:316
  78.9 2.2 %collective-permute-start.6 = (bf16[64,2048]{1,0:T(8,128)(2,1)S(1)}, bf16[64,2048]{1,0:T(8,128)(2,1)S(1)}, u32[]{:S(2)}, u32[]{:S(2)}) collective-permute-start(bf16[64,2048]{1,0:T(8,128)(2,1)S(1)} %get-tuple-element.66), channel_id=1, source_target_pairs={{0,16},{4,20},{8,24},{12,28},{16,0},{20,4},{24,8},{28,12},{1,17},{... | collective-permute-start | bytes 786440 | tf_op jit(solution)/shard_map/ppermute | solution.py:316
  81.0 9.7 %collective-permute-done.5.refs_1_ = bf16[64,2048]{1,0:T(8,128)(2,1)S(1)} collective-permute-done((bf16[64,2048]{1,0:T(8,128)(2,1)S(1)}, bf16[64,2048]{1,0:T(8,128)(2,1)S(1)}, u32[]{:S(2)}, u32[]{:S(2)}) %collective-permute-start.5) | collective-permute-done | bytes 262176 | tf_op jit(solution)/shard_map/ppermute | solution.py:316
  92.4 2.5 %collective-permute-start.9 = (bf16[64,2048]{1,0:T(8,128)(2,1)S(1)}, bf16[64,2048]{1,0:T(8,128)(2,1)S(1)}, u32[]{:S(2)}, u32[]{:S(2)}) collective-permute-start(bf16[64,2048]{1,0:T(8,128)(2,1)S(1)} %get-tuple-element.76), channel_id=1, source_target_pairs={{0,16},{4,20},{8,24},{12,28},{16,0},{20,4},{24,8},{28,12},{1,17},{... | collective-permute-start | bytes 786440 | tf_op jit(solution)/shard_map/ppermute | solution.py:316
  96.9 2.2 %copy-done.3 = bf16[2048,1024]{1,0:T(8,128)(2,1)S(1)} copy-done((bf16[2048,1024]{1,0:T(8,128)(2,1)S(1)}, bf16[2048,1024]{1,0:T(8,128)(2,1)}, u32[]{:S(2)}) %copy-start.3) | copy-done | bytes 4194328
  99.1 3.1 %mlp_up.5 = (bf16[128,1024]{1,0:T(8,128)(2,1)S(1)}, bf16[128,1024]{1,0:T(8,128)(2,1)S(1)}) custom-call(bf16[128,2048]{1,0:T(8,128)(2,1)S(1)} %get-tuple-element.65.refs_0_, bf16[128,2048]{1,0:T(8,128)(2,1)S(1)} %collective-permute-done.4.refs_1_, bf16[2048,1024]{1,0:T(8,128)(2,1)S(1)} %copy-done.2, bf16[2048,1024]{1,0:T(8,128)(2,1)S(1)} %copy-done.3), custom_call_target="tpu_custom_call" | custom-call | tf_op jit(solution)/shard_map/mlp_up/pallas_call | solution.py:390
  102.3 2.4 %collective-permute-done.9.refs_0_ = bf16[64,2048]{1,0:T(8,128)(2,1)S(1)} collective-permute-done((bf16[64,2048]{1,0:T(8,128)(2,1)S(1)}, bf16[64,2048]{1,0:T(8,128)(2,1)S(1)}, u32[]{:S(2)}, u32[]{:S(2)}) %collective-permute-start.9) | collective-permute-done | bytes 262176 | tf_op jit(solution)/shard_map/ppermute | solution.py:316
  109.2 3.2 %mlp_up.6 = (bf16[128,1024]{1,0:T(8,128)(2,1)S(1)}, bf16[128,1024]{1,0:T(8,128)(2,1)S(1)}) custom-call(bf16[64,2048]{1,0:T(8,128)(2,1)S(1)} %collective-permute-done.6.refs_0_, bf16[64,2048]{1,0:T(8,128)(2,1)S(1)} %collective-permute-done.5.refs_1_, bf16[64,2048]{1,0:T(8,128)(2,1)S(1)} %collective-permute-done.7.refs_2_, ...), custom_call_target="tpu_custom_call" | custom-call | tf_op jit(solution)/shard_map/mlp_up/pallas_call | solution.py:390
  113.4 2.8 %collective-permute-done.12.refs_2_ = bf16[64,2048]{1,0:T(8,128)(2,1)S(1)} collective-permute-done((bf16[64,2048]{1,0:T(8,128)(2,1)S(1)}, bf16[64,2048]{1,0:T(8,128)(2,1)S(1)}, u32[]{:S(2)}, u32[]{:S(2)}) %collective-permute-start.12) | collective-permute-done | bytes 262176 | tf_op jit(solution)/shard_map/ppermute | solution.py:316
  117.3 3.2 %mlp_up.7 = (bf16[128,1024]{1,0:T(8,128)(2,1)S(1)}, bf16[128,1024]{1,0:T(8,128)(2,1)S(1)}) custom-call(bf16[64,2048]{1,0:T(8,128)(2,1)S(1)} %collective-permute-done.9.refs_0_, bf16[64,2048]{1,0:T(8,128)(2,1)S(1)} %collective-permute-done.10.refs_1_, bf16[64,2048]{1,0:T(8,128)(2,1)S(1)} %collective-permute-done.12.refs_2_, ...), custom_call_target="tpu_custom_call" | custom-call | tf_op jit(solution)/shard_map/mlp_up/pallas_call | solution.py:390
  121.5 3.8 %collective-permute-done.17.refs_1_ = bf16[64,2048]{1,0:T(8,128)(2,1)S(1)} collective-permute-done((bf16[64,2048]{1,0:T(8,128)(2,1)S(1)}, bf16[64,2048]{1,0:T(8,128)(2,1)S(1)}, u32[]{:S(2)}, u32[]{:S(2)}) %collective-permute-start.17) | collective-permute-done | bytes 262176 | tf_op jit(solution)/shard_map/ppermute | solution.py:316
  125.3 2.0 %mlp_up.8 = (bf16[64,1024]{1,0:T(8,128)(2,1)S(1)}, bf16[64,1024]{1,0:T(8,128)(2,1)S(1)}) custom-call(bf16[64,2048]{1,0:T(8,128)(2,1)S(1)} %collective-permute-done.13.refs_0_, bf16[64,2048]{1,0:T(8,128)(2,1)S(1)} %collective-permute-done.17.refs_1_, bf16[2048,1024]{1,0:T(8,128)(2,1)S(1)} %copy-done.2, bf16[2048,1024]{1,0:T(8,128)(2,1)S(1)} %copy-done.3), custom_call_target="tpu_custom_call" | custom-call | tf_op jit(solution)/shard_map/mlp_up/pallas_call | solution.py:390
  144.6 2.0 %mlp_up.9 = (bf16[64,1024]{1,0:T(8,128)(2,1)S(1)}, bf16[64,1024]{1,0:T(8,128)(2,1)S(1)}) custom-call(bf16[64,2048]{1,0:T(8,128)(2,1)S(1)} %collective-permute-done.14.refs_0_, bf16[64,2048]{1,0:T(8,128)(2,1)S(1)} %collective-permute-done.24.refs_1_, bf16[2048,1024]{1,0:T(8,128)(2,1)S(1)} %copy-done.2, bf16[2048,1024]{1,0:T(8,128)(2,1)S(1)} %copy-done.3), custom_call_target="tpu_custom_call" | custom-call | tf_op jit(solution)/shard_map/mlp_up/pallas_call | solution.py:390
  146.7 3.1 %collective-permute-done.21 = bf16[64,2048]{1,0:T(8,128)(2,1)S(1)} collective-permute-done((bf16[64,2048]{1,0:T(8,128)(2,1)S(1)}, bf16[64,2048]{1,0:T(8,128)(2,1)S(1)}, u32[]{:S(2)}, u32[]{:S(2)}) %collective-permute-start.21) | collective-permute-done | bytes 262176 | tf_op jit(solution)/shard_map/ppermute | solution.py:316
  158.2 4.1 %store_new.1 = (bf16[128,16,128]{2,1,0:T(8,128)(2,1)}, bf16[128,16,128]{2,1,0:T(8,128)(2,1)}) custom-call(s32[128]{0:T(128)S(1)} %bitcast.29, s32[8]{0:T(128)S(1)} %bitcast.31, s32[8]{0:T(128)S(1)} %bitcast.32, bf16[8,128,256]{2,1,0:T(8,128)(2,1)} %all-to-all-done.1.new, f32[384,128]{1,0:T(8,128)S(1)} %copy-done.10, f32[384,128]{1,0:T(8,128)S(1)} %copy-done.9, ...), custom_call_target="tpu_custom_call" | custom-call | tf_op jit(solution)/shard_map/store_new/pallas_call | solution.py:304
  164.2 6.6 %collective-permute-done.30 = bf16[64,2048]{1,0:T(8,128)(2,1)S(1)} collective-permute-done((bf16[64,2048]{1,0:T(8,128)(2,1)S(1)}, bf16[64,2048]{1,0:T(8,128)(2,1)S(1)}, u32[]{:S(2)}, u32[]{:S(2)}) %collective-permute-start.30) | collective-permute-done | bytes 262176 | tf_op jit(solution)/shard_map/ppermute | solution.py:316
  170.8 3.2 %collective-permute-done.29 = bf16[64,2048]{1,0:T(8,128)(2,1)S(1)} collective-permute-done((bf16[64,2048]{1,0:T(8,128)(2,1)S(1)}, bf16[64,2048]{1,0:T(8,128)(2,1)S(1)}, u32[]{:S(2)}, u32[]{:S(2)}) %collective-permute-start.29) | collective-permute-done | bytes 262176 | tf_op jit(solution)/shard_map/ppermute | solution.py:316
  (115 shorter events, 63.4 us)
Async XLA Ops:
  3.1 34.0 %all-to-all-start = ((bf16[8,528,128]{2,1,0:T(8,128)(2,1)}), bf16[8,528,128]{2,1,0:T(8,128)(2,1)}, u32[]{:S(2)}, u32[]{:S(2)}) async-start(bf16[8,528,128]{2,1,0:T(8,128)(2,1)} %pack_pages.1), calls=%async_computation | async-start | bytes 2162688 | tf_op jit(solution)/shard_map/all_to_all | solution.py:555
  13.0 40.6 %collective-permute-start = (bf16[256,2048]{1,0:T(8,128)(2,1)}, bf16[256,2048]{1,0:T(8,128)(2,1)S(1)}, u32[]{:S(2)}, u32[]{:S(2)}) collective-permute-start(bf16[256,2048]{1,0:T(8,128)(2,1)} %constant_dynamic-slice_fusion), channel_id=1, source_target_pairs={{0,4},{4,0},{8,12},{12,8},{16,20},{20,16},{24,28},{28,24},{1,5},{5... | collective-permute-start | bytes 3145736 | tf_op jit(solution)/shard_map/ppermute | solution.py:316
  37.1 18.4 %all-to-all-start.1 = ((bf16[8,128,256]{2,1,0:T(8,128)(2,1)}), bf16[8,128,256]{2,1,0:T(8,128)(2,1)}, u32[]{:S(2)}, u32[]{:S(2)}) async-start(bf16[8,128,256]{2,1,0:T(8,128)(2,1)} %copy-done.6), calls=%async_computation.1 | async-start | bytes 1048576 | tf_op jit(solution)/shard_map/all_to_all | solution.py:562
  60.2 14.3 %collective-permute-start.3 = (bf16[128,2048]{1,0:T(8,128)(2,1)}, bf16[128,2048]{1,0:T(8,128)(2,1)}, u32[]{:S(2)}, u32[]{:S(2)}) collective-permute-start(bf16[128,2048]{1,0:T(8,128)(2,1)} %add_convert_fusion.1), channel_id=1, source_target_pairs={{0,2},{1,3},{2,0},{3,1},{4,6},{5,7},{6,4},{7,5},{8,10},{9,11},{10,... | collective-permute-start | bytes 1572872 | tf_op jit(solution)/shard_map/ppermute | solution.py:316
  75.9 16.5 %collective-permute-start.4 = (bf16[128,2048]{1,0:T(8,128)(2,1)S(1)}, bf16[128,2048]{1,0:T(8,128)(2,1)S(1)}, u32[]{:S(2)}, u32[]{:S(2)}) collective-permute-start(bf16[128,2048]{1,0:T(8,128)(2,1)S(1)} %get-tuple-element.65.refs_0_), channel_id=1, source_target_pairs={{0,4},{4,0},{8,12},{12,8},{16,20},{20,16},{24,28},{28,24},{1,5},{5... | collective-permute-start | bytes 1572872 | tf_op jit(solution)/shard_map/ppermute | solution.py:316
  77.4 35.0 %collective-permute-start.15 = (bf16[256,2048]{1,0:T(8,128)(2,1)S(1)}, bf16[256,2048]{1,0:T(8,128)(2,1)S(1)}, u32[]{:S(2)}, u32[]{:S(2)}) collective-permute-start(bf16[256,2048]{1,0:T(8,128)(2,1)S(1)} %collective-permute-done.refs_3_), channel_id=1, source_target_pairs={{0,2},{1,3},{2,0},{3,1},{4,6},{5,7},{6,4},{7,5},{8,10},{9,11},{10,... | collective-permute-start | bytes 3145736 | tf_op jit(solution)/shard_map/ppermute | solution.py:316
  78.9 11.9 %collective-permute-start.5 = (bf16[64,2048]{1,0:T(8,128)(2,1)S(1)}, bf16[64,2048]{1,0:T(8,128)(2,1)S(1)}, u32[]{:S(2)}, u32[]{:S(2)}) collective-permute-start(bf16[64,2048]{1,0:T(8,128)(2,1)S(1)} %get-tuple-element.66), channel_id=1, source_target_pairs={{0,8},{4,12},{8,0},{12,4},{16,24},{20,28},{24,16},{28,20},{1,9},{5... | collective-permute-start | bytes 786440 | tf_op jit(solution)/shard_map/ppermute | solution.py:316
  78.9 13.5 %collective-permute-start.6 = (bf16[64,2048]{1,0:T(8,128)(2,1)S(1)}, bf16[64,2048]{1,0:T(8,128)(2,1)S(1)}, u32[]{:S(2)}, u32[]{:S(2)}) collective-permute-start(bf16[64,2048]{1,0:T(8,128)(2,1)S(1)} %get-tuple-element.66), channel_id=1, source_target_pairs={{0,16},{4,20},{8,24},{12,28},{16,0},{20,4},{24,8},{28,12},{1,17},{... | collective-permute-start | bytes 786440 | tf_op jit(solution)/shard_map/ppermute | solution.py:316
  92.4 12.3 %collective-permute-start.10 = (bf16[64,2048]{1,0:T(8,128)(2,1)S(1)}, bf16[64,2048]{1,0:T(8,128)(2,1)S(1)}, u32[]{:S(2)}, u32[]{:S(2)}) collective-permute-start(bf16[64,2048]{1,0:T(8,128)(2,1)S(1)} %collective-permute-done.6.refs_0_), channel_id=1, source_target_pairs={{0,8},{4,12},{8,0},{12,4},{16,24},{20,28},{24,16},{28,20},{1,9},{5... | collective-permute-start | bytes 786440 | tf_op jit(solution)/shard_map/ppermute | solution.py:316
  92.4 12.3 %collective-permute-start.9 = (bf16[64,2048]{1,0:T(8,128)(2,1)S(1)}, bf16[64,2048]{1,0:T(8,128)(2,1)S(1)}, u32[]{:S(2)}, u32[]{:S(2)}) collective-permute-start(bf16[64,2048]{1,0:T(8,128)(2,1)S(1)} %get-tuple-element.76), channel_id=1, source_target_pairs={{0,16},{4,20},{8,24},{12,28},{16,0},{20,4},{24,8},{28,12},{1,17},{... | collective-permute-start | bytes 786440 | tf_op jit(solution)/shard_map/ppermute | solution.py:316
  94.9 9.8 %collective-permute-start.7 = (bf16[64,2048]{1,0:T(8,128)(2,1)S(1)}, bf16[64,2048]{1,0:T(8,128)(2,1)S(1)}, u32[]{:S(2)}, u32[]{:S(2)}) collective-permute-start(bf16[64,2048]{1,0:T(8,128)(2,1)S(1)} %collective-permute-done.6.refs_0_), channel_id=1, source_target_pairs={{0,4},{4,0},{8,12},{12,8},{16,20},{20,16},{24,28},{28,24},{1,5},{5... | collective-permute-start | bytes 786440 | tf_op jit(solution)/shard_map/ppermute | solution.py:316
  95.4 9.7 %collective-permute-start.8 = (bf16[64,2048]{1,0:T(8,128)(2,1)S(1)}, bf16[64,2048]{1,0:T(8,128)(2,1)S(1)}, u32[]{:S(2)}, u32[]{:S(2)}) collective-permute-start(bf16[64,2048]{1,0:T(8,128)(2,1)S(1)} %collective-permute-done.5.refs_1_), channel_id=1, source_target_pairs={{0,4},{4,0},{8,12},{12,8},{16,20},{20,16},{24,28},{28,24},{1,5},{5... | collective-permute-start | bytes 786440 | tf_op jit(solution)/shard_map/ppermute | solution.py:316
  112.4 18.6 %collective-permute-start.18 = (bf16[256,2048]{1,0:T(8,128)(2,1)S(1)}, bf16[256,2048]{1,0:T(8,128)(2,1)S(1)}, u32[]{:S(2)}, u32[]{:S(2)}) collective-permute-start(bf16[256,2048]{1,0:T(8,128)(2,1)S(1)} %collective-permute-done.refs_3_), channel_id=1, source_target_pairs={{0,1},{1,0},{2,3},{3,2},{4,5},{5,4},{6,7},{7,6},{8,9},{9,8},{10,11... | collective-permute-start | bytes 3145736 | tf_op jit(solution)/shard_map/ppermute | solution.py:316
  116.2 14.7 %collective-permute-start.19 = (bf16[256,2048]{1,0:T(8,128)(2,1)S(1)}, bf16[256,2048]{1,0:T(8,128)(2,1)S(1)}, u32[]{:S(2)}, u32[]{:S(2)}) collective-permute-start(bf16[256,2048]{1,0:T(8,128)(2,1)S(1)} %collective-permute-done.15.refs_5_), channel_id=1, source_target_pairs={{0,1},{1,0},{2,3},{3,2},{4,5},{5,4},{6,7},{7,6},{8,9},{9,8},{10,11... | collective-permute-start | bytes 3145736 | tf_op jit(solution)/shard_map/ppermute | solution.py:316
  120.5 10.5 %collective-permute-start.16 = (bf16[128,1024]{1,0:T(8,128)(2,1)S(1)}, bf16[128,1024]{1,0:T(8,128)(2,1)S(1)}, u32[]{:S(2)}, u32[]{:S(2)}) collective-permute-start(bf16[128,1024]{1,0:T(8,128)(2,1)S(1)} %get-tuple-element.85), channel_id=1, source_target_pairs={{0,4},{4,0},{8,12},{12,8},{16,20},{20,16},{24,28},{28,24},{1,5},{5... | collective-permute-start | bytes 786440 | tf_op jit(solution)/shard_map/ppermute | solution.py:316
  128.5 11.0 %collective-permute-start.22 = (bf16[128,1024]{1,0:T(8,128)(2,1)S(1)}, bf16[128,1024]{1,0:T(8,128)(2,1)S(1)}, u32[]{:S(2)}, u32[]{:S(2)}) collective-permute-start(bf16[128,1024]{1,0:T(8,128)(2,1)S(1)} %get-tuple-element.96), channel_id=1, source_target_pairs={{0,4},{4,0},{8,12},{12,8},{16,20},{20,16},{24,28},{28,24},{1,5},{5... | collective-permute-start | bytes 786440 | tf_op jit(solution)/shard_map/ppermute | solution.py:316
  133.9 10.7 %collective-permute-start.24 = (bf16[64,2048]{1,0:T(8,128)(2,1)S(1)}, bf16[64,2048]{1,0:T(8,128)(2,1)S(1)}, u32[]{:S(2)}, u32[]{:S(2)}) collective-permute-start(bf16[64,2048]{1,0:T(8,128)(2,1)S(1)} %collective-permute-done.14.refs_0_), channel_id=1, source_target_pairs={{0,4},{4,0},{8,12},{12,8},{16,20},{20,16},{24,28},{28,24},{1,5},{5... | collective-permute-start | bytes 786440 | tf_op jit(solution)/shard_map/ppermute | solution.py:316
  134.9 11.7 %collective-permute-start.23 = (bf16[64,2048]{1,0:T(8,128)(2,1)S(1)}, bf16[64,2048]{1,0:T(8,128)(2,1)S(1)}, u32[]{:S(2)}, u32[]{:S(2)}) collective-permute-start(bf16[64,2048]{1,0:T(8,128)(2,1)S(1)} %get-tuple-element.93), channel_id=1, source_target_pairs={{0,8},{4,12},{8,0},{12,4},{16,24},{20,28},{24,16},{28,20},{1,9},{5... | collective-permute-start | bytes 786440 | tf_op jit(solution)/shard_map/ppermute | solution.py:316
  138.1 11.7 %collective-permute-start.21 = (bf16[64,2048]{1,0:T(8,128)(2,1)S(1)}, bf16[64,2048]{1,0:T(8,128)(2,1)S(1)}, u32[]{:S(2)}, u32[]{:S(2)}) collective-permute-start(bf16[64,2048]{1,0:T(8,128)(2,1)S(1)} %mlp_down.6), channel_id=1, source_target_pairs={{0,8},{4,12},{8,0},{12,4},{16,24},{20,28},{24,16},{28,20},{1,9},{5... | collective-permute-start | bytes 786440 | tf_op jit(solution)/shard_map/ppermute | solution.py:316
  141.4 22.8 %collective-permute-start.27 = (bf16[64,2048]{1,0:T(8,128)(2,1)S(1)}, bf16[64,2048]{1,0:T(8,128)(2,1)S(1)}, u32[]{:S(2)}, u32[]{:S(2)}) collective-permute-start(bf16[64,2048]{1,0:T(8,128)(2,1)S(1)} %get-tuple-element.101), channel_id=1, source_target_pairs={{0,8},{4,12},{8,0},{12,4},{16,24},{20,28},{24,16},{28,20},{1,9},{5... | collective-permute-start | bytes 786440 | tf_op jit(solution)/shard_map/ppermute | solution.py:316
  150.9 11.4 %collective-permute-start.25 = (bf16[128,1024]{1,0:T(8,128)(2,1)S(1)}, bf16[128,1024]{1,0:T(8,128)(2,1)S(1)}, u32[]{:S(2)}, u32[]{:S(2)}) collective-permute-start(bf16[128,1024]{1,0:T(8,128)(2,1)S(1)} %get-tuple-element.106), channel_id=1, source_target_pairs={{0,4},{4,0},{8,12},{12,8},{16,20},{20,16},{24,28},{28,24},{1,5},{5... | collective-permute-start | bytes 786440 | tf_op jit(solution)/shard_map/ppermute | solution.py:316
  152.0 18.8 %collective-permute-start.30 = (bf16[64,2048]{1,0:T(8,128)(2,1)S(1)}, bf16[64,2048]{1,0:T(8,128)(2,1)S(1)}, u32[]{:S(2)}, u32[]{:S(2)}) collective-permute-start(bf16[64,2048]{1,0:T(8,128)(2,1)S(1)} %add_convert_fusion.2), channel_id=1, source_target_pairs={{0,16},{4,20},{8,24},{12,28},{16,0},{20,4},{24,8},{28,12},{1,17},{... | collective-permute-start | bytes 786440 | tf_op jit(solution)/shard_map/ppermute | solution.py:316
  153.2 20.8 %collective-permute-start.29 = (bf16[64,2048]{1,0:T(8,128)(2,1)S(1)}, bf16[64,2048]{1,0:T(8,128)(2,1)S(1)}, u32[]{:S(2)}, u32[]{:S(2)}) collective-permute-start(bf16[64,2048]{1,0:T(8,128)(2,1)S(1)} %add_convert_fusion.3), channel_id=1, source_target_pairs={{0,16},{4,20},{8,24},{12,28},{16,0},{20,4},{24,8},{28,12},{1,17},{... | collective-permute-start | bytes 786440 | tf_op jit(solution)/shard_map/ppermute | solution.py:316
  157.0 17.1 %collective-permute-start.28 = (bf16[64,2048]{1,0:T(8,128)(2,1)S(1)}, bf16[64,2048]{1,0:T(8,128)(2,1)S(1)}, u32[]{:S(2)}, u32[]{:S(2)}) collective-permute-start(bf16[64,2048]{1,0:T(8,128)(2,1)S(1)} %mlp_down.8), channel_id=1, source_target_pairs={{0,8},{4,12},{8,0},{12,4},{16,24},{20,28},{24,16},{28,20},{1,9},{5... | collective-permute-start | bytes 786440 | tf_op jit(solution)/shard_map/ppermute | solution.py:316
  (32 other events, 280.1 us)

commit v6 on v5

--- a/solution.py
+++ b/solution.py
@@ -468,7 +468,7 @@
     both_a = send(far_a, bit=2)
     side_far_a = send(far_a, bit=1)
     side_near_a = send(near_a, bit=1)
-    over_down = over(after(side_down, own))
+    over_down = over(after(side_down, far_a))
     hidden_own, theirs_own = up([own], [side])
     side_far_a, side_near_a, far_b, both_a, _ = sync(
         side_far_a, side_near_a, far_b, both_a, hidden_own

time: 176 us -> 176 us (level)
  no operation moved by 1% of the time
where the time goes in v6:
time: 176 us; the launch traced here: 175 us
  waiting for transfers between devices  62.4 us (35%)
  Pallas kernels  49 us (28%)
  starting transfers between devices  44 us (25%)
  local copies, waits for them, and re-layouts  10.2 us (6%)
  matrix products  5.84 us (3%)
  other arithmetic  2.91 us (2%)
    ppermute x31, waiting for transfers between devices, swap(): return lax.ppermute(values, axis, [(at, at ^ bit) for at in range(size)])  51.3 us
    ppermute x31, starting transfers between devices, swap(): return lax.ppermute(values, axis, [(at, at ^ bit) for at in range(size)])  32.3 us
    pallas_call x5, Pallas kernels, mlp_up(): pl.pallas_call(functools.partial(up_kernel, count), out_shape=[jax.ShapeD...  13.5 us
    pallas_call x1, Pallas kernels, attend(): pl.pallas_call(attention_kernel, out_shape=jax.ShapeDtypeStruct(result, B...  12.1 us
    pallas_call x5, Pallas kernels, mlp_down(): pl.pallas_call(functools.partial(down_kernel, len(pieces)), out_shape=[ja...  9.63 us
    all_to_all x1, waiting for transfers between devices, body(): lax.all_to_all(packed, 'req', split_axis=0, concat_axis=0, tiled=True)  9.13 us
    unnamed x46, local copies, waits for them, and re-layouts  7.71 us
    all_to_all x1, starting transfers between devices, body(): lax.all_to_all(packed, 'req', split_axis=0, concat_axis=0, tiled=True)  7.41 us
  transfers between devices with their start and end apart: 33, of which 19 were waited for; matrix products, arithmetic and copies ran while one was open for 5% of the time, Pallas kernels for 26%

profile of v6, /device:TPU:0, one launch (start us, length us, event | category | flops | bytes accessed | tf_op | source)
XLA Modules:
  0.0 175.3 jit_solution(2159582811339185125)
XLA Ops:
  0.6 2.5 %pack_pages.1 = bf16[8,528,128]{2,1,0:T(8,128)(2,1)} custom-call(s32[128]{0:T(128)} %bitcast.28, s32[8]{0:T(128)} %bitcast.30, bf16[128,16,128]{2,1,0:T(8,128)(2,1)} %cache_k.3, bf16[128,16,128]{2,1,0:T(8,128)(2,1)} %cache_v.3), custom_call_target="tpu_custom_call" | custom-call | tf_op jit(solution)/shard_map/pack_pages/pallas_call | solution.py:71
  3.1 7.4 %all-to-all-start = ((bf16[8,528,128]{2,1,0:T(8,128)(2,1)}), bf16[8,528,128]{2,1,0:T(8,128)(2,1)}, u32[]{:S(2)}, u32[]{:S(2)}) async-start(bf16[8,528,128]{2,1,0:T(8,128)(2,1)} %pack_pages.1), calls=%async_computation | async-start | bytes 2162688 | tf_op jit(solution)/shard_map/all_to_all | solution.py:555
  10.6 2.5 %constant_dynamic-slice_fusion = bf16[256,2048]{1,0:T(8,128)(2,1)} fusion(bf16[1024,2048]{1,0:T(8,128)(2,1)} %refs_2_.15, s32[]{:T(128)S(6)} %select_n.60), kind=kLoop, calls=%fused_computation.32 | loop fusion | bytes 2097156 | tf_op jit(solution)/shard_map/dynamic_slice | solution.py:446
  20.5 5.7 %project.1 = (bf16[8,128,512]{2,1,0:T(8,128)(2,1)S(1)}, bf16[8,128,256]{2,1,0:T(8,128)(2,1)S(1)}) custom-call(s32[8]{0:T(128)S(1)} %get-tuple-element.114.starts, s32[8]{0:T(128)S(1)} %get-tuple-element.113.counts, bf16[512,2048]{1,0:T(8,128)(2,1)S(1)} %copy-done.4, f32[1,2048]{1,0:T(1,128)S(1)} %bitcast.26, bf16[2048,512]{1,0:T(8,128)(2,1)S(1)} %copy-done.5, ...), custom_call_target="tpu_custom_call" | custom-call | tf_op jit(solution)/shard_map/project/pallas_call | solution.py:118
  28.0 9.1 %all-to-all-done.pages = bf16[8,528,128]{2,1,0:T(8,128)(2,1)} async-done(((bf16[8,528,128]{2,1,0:T(8,128)(2,1)}), bf16[8,528,128]{2,1,0:T(8,128)(2,1)}, u32[]{:S(2)}, u32[]{:S(2)}) %all-to-all-start) | async-done | bytes 1081376 | tf_op jit(solution)/shard_map/all_to_all | solution.py:555
  37.1 4.3 %all-to-all-start.1 = ((bf16[8,128,256]{2,1,0:T(8,128)(2,1)}), bf16[8,128,256]{2,1,0:T(8,128)(2,1)}, u32[]{:S(2)}, u32[]{:S(2)}) async-start(bf16[8,128,256]{2,1,0:T(8,128)(2,1)} %copy-done.6), calls=%async_computation.1 | async-start | bytes 1048576 | tf_op jit(solution)/shard_map/all_to_all | solution.py:562
  41.5 12.1 %attend.1 = bf16[4,128,512]{2,1,0:T(8,128)(2,1)} custom-call(s32[8]{0:T(128)} %copy-done.17, s32[8]{0:T(128)} %copy-done.16, s32[1]{0:T(128)} %bitcast.group, bf16[8,128,512]{2,1,0:T(8,128)(2,1)} %copy-done.11, bf16[8,128,256]{2,1,0:T(8,128)(2,1)} %copy-done.6, bf16[8,528,128]{2,1,0:T(8,128)(2,1)} %all-to-all-done.pages, ...), custom_call_target="tpu_custom_call" | custom-call | tf_op jit(solution)/shard_map/attend/pallas_call | solution.py:244
  63.7 10.8 %collective-permute-done.3.over = bf16[128,2048]{1,0:T(8,128)(2,1)} collective-permute-done((bf16[128,2048]{1,0:T(8,128)(2,1)}, bf16[128,2048]{1,0:T(8,128)(2,1)}, u32[]{:S(2)}, u32[]{:S(2)}) %collective-permute-start.3) | collective-permute-done | bytes 524320 | tf_op jit(solution)/shard_map/ppermute | solution.py:316
  77.4 2.3 %collective-permute-start.6 = (bf16[64,2048]{1,0:T(8,128)(2,1)S(1)}, bf16[64,2048]{1,0:T(8,128)(2,1)S(1)}, u32[]{:S(2)}, u32[]{:S(2)}) collective-permute-start(bf16[64,2048]{1,0:T(8,128)(2,1)S(1)} %get-tuple-element.66), channel_id=1, source_target_pairs={{0,16},{4,20},{8,24},{12,28},{16,0},{20,4},{24,8},{28,12},{1,17},{... | collective-permute-start | bytes 786440 | tf_op jit(solution)/shard_map/ppermute | solution.py:316
  79.7 9.8 %collective-permute-done.5.refs_1_ = bf16[64,2048]{1,0:T(8,128)(2,1)S(1)} collective-permute-done((bf16[64,2048]{1,0:T(8,128)(2,1)S(1)}, bf16[64,2048]{1,0:T(8,128)(2,1)S(1)}, u32[]{:S(2)}, u32[]{:S(2)}) %collective-permute-start.5) | collective-permute-done | bytes 262176 | tf_op jit(solution)/shard_map/ppermute | solution.py:316
  92.7 2.5 %collective-permute-start.9 = (bf16[64,2048]{1,0:T(8,128)(2,1)S(1)}, bf16[64,2048]{1,0:T(8,128)(2,1)S(1)}, u32[]{:S(2)}, u32[]{:S(2)}) collective-permute-start(bf16[64,2048]{1,0:T(8,128)(2,1)S(1)} %get-tuple-element.76), channel_id=1, source_target_pairs={{0,16},{4,20},{8,24},{12,28},{16,0},{20,4},{24,8},{28,12},{1,17},{... | collective-permute-start | bytes 786440 | tf_op jit(solution)/shard_map/ppermute | solution.py:316
  97.2 2.2 %copy-done.3 = bf16[2048,1024]{1,0:T(8,128)(2,1)S(1)} copy-done((bf16[2048,1024]{1,0:T(8,128)(2,1)S(1)}, bf16[2048,1024]{1,0:T(8,128)(2,1)}, u32[]{:S(2)}) %copy-start.3) | copy-done | bytes 4194328
  99.3 3.1 %mlp_up.5 = (bf16[128,1024]{1,0:T(8,128)(2,1)S(1)}, bf16[128,1024]{1,0:T(8,128)(2,1)S(1)}) custom-call(bf16[128,2048]{1,0:T(8,128)(2,1)S(1)} %get-tuple-element.65.refs_0_, bf16[128,2048]{1,0:T(8,128)(2,1)S(1)} %collective-permute-done.4.refs_1_, bf16[2048,1024]{1,0:T(8,128)(2,1)S(1)} %copy-done.2, bf16[2048,1024]{1,0:T(8,128)(2,1)S(1)} %copy-done.3), custom_call_target="tpu_custom_call" | custom-call | tf_op jit(solution)/shard_map/mlp_up/pallas_call | solution.py:390
  102.5 2.3 %collective-permute-done.9.refs_0_ = bf16[64,2048]{1,0:T(8,128)(2,1)S(1)} collective-permute-done((bf16[64,2048]{1,0:T(8,128)(2,1)S(1)}, bf16[64,2048]{1,0:T(8,128)(2,1)S(1)}, u32[]{:S(2)}, u32[]{:S(2)}) %collective-permute-start.9) | collective-permute-done | bytes 262176 | tf_op jit(solution)/shard_map/ppermute | solution.py:316
  109.4 3.2 %mlp_up.6 = (bf16[128,1024]{1,0:T(8,128)(2,1)S(1)}, bf16[128,1024]{1,0:T(8,128)(2,1)S(1)}) custom-call(bf16[64,2048]{1,0:T(8,128)(2,1)S(1)} %collective-permute-done.6.refs_0_, bf16[64,2048]{1,0:T(8,128)(2,1)S(1)} %collective-permute-done.5.refs_1_, bf16[64,2048]{1,0:T(8,128)(2,1)S(1)} %collective-permute-done.7.refs_2_, ...), custom_call_target="tpu_custom_call" | custom-call | tf_op jit(solution)/shard_map/mlp_up/pallas_call | solution.py:390
  113.7 2.8 %collective-permute-done.12.refs_2_ = bf16[64,2048]{1,0:T(8,128)(2,1)S(1)} collective-permute-done((bf16[64,2048]{1,0:T(8,128)(2,1)S(1)}, bf16[64,2048]{1,0:T(8,128)(2,1)S(1)}, u32[]{:S(2)}, u32[]{:S(2)}) %collective-permute-start.12) | collective-permute-done | bytes 262176 | tf_op jit(solution)/shard_map/ppermute | solution.py:316
  117.4 3.2 %mlp_up.7 = (bf16[128,1024]{1,0:T(8,128)(2,1)S(1)}, bf16[128,1024]{1,0:T(8,128)(2,1)S(1)}) custom-call(bf16[64,2048]{1,0:T(8,128)(2,1)S(1)} %collective-permute-done.9.refs_0_, bf16[64,2048]{1,0:T(8,128)(2,1)S(1)} %collective-permute-done.10.refs_1_, bf16[64,2048]{1,0:T(8,128)(2,1)S(1)} %collective-permute-done.12.refs_2_, ...), custom_call_target="tpu_custom_call" | custom-call | tf_op jit(solution)/shard_map/mlp_up/pallas_call | solution.py:390
  121.8 3.9 %collective-permute-done.17.refs_1_ = bf16[64,2048]{1,0:T(8,128)(2,1)S(1)} collective-permute-done((bf16[64,2048]{1,0:T(8,128)(2,1)S(1)}, bf16[64,2048]{1,0:T(8,128)(2,1)S(1)}, u32[]{:S(2)}, u32[]{:S(2)}) %collective-permute-start.17) | collective-permute-done | bytes 262176 | tf_op jit(solution)/shard_map/ppermute | solution.py:316
  125.7 2.0 %mlp_up.8 = (bf16[64,1024]{1,0:T(8,128)(2,1)S(1)}, bf16[64,1024]{1,0:T(8,128)(2,1)S(1)}) custom-call(bf16[64,2048]{1,0:T(8,128)(2,1)S(1)} %collective-permute-done.13.refs_0_, bf16[64,2048]{1,0:T(8,128)(2,1)S(1)} %collective-permute-done.17.refs_1_, bf16[2048,1024]{1,0:T(8,128)(2,1)S(1)} %copy-done.2, bf16[2048,1024]{1,0:T(8,128)(2,1)S(1)} %copy-done.3), custom_call_target="tpu_custom_call" | custom-call | tf_op jit(solution)/shard_map/mlp_up/pallas_call | solution.py:390
  144.9 2.0 %mlp_up.9 = (bf16[64,1024]{1,0:T(8,128)(2,1)S(1)}, bf16[64,1024]{1,0:T(8,128)(2,1)S(1)}) custom-call(bf16[64,2048]{1,0:T(8,128)(2,1)S(1)} %collective-permute-done.14.refs_0_, bf16[64,2048]{1,0:T(8,128)(2,1)S(1)} %collective-permute-done.24.refs_1_, bf16[2048,1024]{1,0:T(8,128)(2,1)S(1)} %copy-done.2, bf16[2048,1024]{1,0:T(8,128)(2,1)S(1)} %copy-done.3), custom_call_target="tpu_custom_call" | custom-call | tf_op jit(solution)/shard_map/mlp_up/pallas_call | solution.py:390
  147.0 2.9 %collective-permute-done.21 = bf16[64,2048]{1,0:T(8,128)(2,1)S(1)} collective-permute-done((bf16[64,2048]{1,0:T(8,128)(2,1)S(1)}, bf16[64,2048]{1,0:T(8,128)(2,1)S(1)}, u32[]{:S(2)}, u32[]{:S(2)}) %collective-permute-start.21) | collective-permute-done | bytes 262176 | tf_op jit(solution)/shard_map/ppermute | solution.py:316
  158.2 4.1 %store_new.1 = (bf16[128,16,128]{2,1,0:T(8,128)(2,1)}, bf16[128,16,128]{2,1,0:T(8,128)(2,1)}) custom-call(s32[128]{0:T(128)S(1)} %bitcast.29, s32[8]{0:T(128)S(1)} %bitcast.31, s32[8]{0:T(128)S(1)} %bitcast.32, bf16[8,128,256]{2,1,0:T(8,128)(2,1)} %all-to-all-done.1.new, f32[384,128]{1,0:T(8,128)S(1)} %copy-done.10, f32[384,128]{1,0:T(8,128)S(1)} %copy-done.9, ...), custom_call_target="tpu_custom_call" | custom-call | tf_op jit(solution)/shard_map/store_new/pallas_call | solution.py:304
  164.2 6.5 %collective-permute-done.30 = bf16[64,2048]{1,0:T(8,128)(2,1)S(1)} collective-permute-done((bf16[64,2048]{1,0:T(8,128)(2,1)S(1)}, bf16[64,2048]{1,0:T(8,128)(2,1)S(1)}, u32[]{:S(2)}, u32[]{:S(2)}) %collective-permute-start.30) | collective-permute-done | bytes 262176 | tf_op jit(solution)/shard_map/ppermute | solution.py:316
  170.8 3.5 %collective-permute-done.29 = bf16[64,2048]{1,0:T(8,128)(2,1)S(1)} collective-permute-done((bf16[64,2048]{1,0:T(8,128)(2,1)S(1)}, bf16[64,2048]{1,0:T(8,128)(2,1)S(1)}, u32[]{:S(2)}, u32[]{:S(2)}) %collective-permute-start.29) | collective-permute-done | bytes 262176 | tf_op jit(solution)/shard_map/ppermute | solution.py:316
  (115 shorter events, 63.4 us)
Async XLA Ops:
  3.1 34.0 %all-to-all-start = ((bf16[8,528,128]{2,1,0:T(8,128)(2,1)}), bf16[8,528,128]{2,1,0:T(8,128)(2,1)}, u32[]{:S(2)}, u32[]{:S(2)}) async-start(bf16[8,528,128]{2,1,0:T(8,128)(2,1)} %pack_pages.1), calls=%async_computation | async-start | bytes 2162688 | tf_op jit(solution)/shard_map/all_to_all | solution.py:555
  13.0 40.6 %collective-permute-start = (bf16[256,2048]{1,0:T(8,128)(2,1)}, bf16[256,2048]{1,0:T(8,128)(2,1)S(1)}, u32[]{:S(2)}, u32[]{:S(2)}) collective-permute-start(bf16[256,2048]{1,0:T(8,128)(2,1)} %constant_dynamic-slice_fusion), channel_id=1, source_target_pairs={{0,4},{4,0},{8,12},{12,8},{16,20},{20,16},{24,28},{28,24},{1,5},{5... | collective-permute-start | bytes 3145736 | tf_op jit(solution)/shard_map/ppermute | solution.py:316
  37.1 18.4 %all-to-all-start.1 = ((bf16[8,128,256]{2,1,0:T(8,128)(2,1)}), bf16[8,128,256]{2,1,0:T(8,128)(2,1)}, u32[]{:S(2)}, u32[]{:S(2)}) async-start(bf16[8,128,256]{2,1,0:T(8,128)(2,1)} %copy-done.6), calls=%async_computation.1 | async-start | bytes 1048576 | tf_op jit(solution)/shard_map/all_to_all | solution.py:562
  60.2 14.3 %collective-permute-start.3 = (bf16[128,2048]{1,0:T(8,128)(2,1)}, bf16[128,2048]{1,0:T(8,128)(2,1)}, u32[]{:S(2)}, u32[]{:S(2)}) collective-permute-start(bf16[128,2048]{1,0:T(8,128)(2,1)} %add_convert_fusion.1), channel_id=1, source_target_pairs={{0,2},{1,3},{2,0},{3,1},{4,6},{5,7},{6,4},{7,5},{8,10},{9,11},{10,... | collective-permute-start | bytes 1572872 | tf_op jit(solution)/shard_map/ppermute | solution.py:316
  75.9 15.3 %collective-permute-start.4 = (bf16[128,2048]{1,0:T(8,128)(2,1)S(1)}, bf16[128,2048]{1,0:T(8,128)(2,1)S(1)}, u32[]{:S(2)}, u32[]{:S(2)}) collective-permute-start(bf16[128,2048]{1,0:T(8,128)(2,1)S(1)} %get-tuple-element.65.refs_0_), channel_id=1, source_target_pairs={{0,4},{4,0},{8,12},{12,8},{16,20},{20,16},{24,28},{28,24},{1,5},{5... | collective-permute-start | bytes 1572872 | tf_op jit(solution)/shard_map/ppermute | solution.py:316
  77.4 12.1 %collective-permute-start.5 = (bf16[64,2048]{1,0:T(8,128)(2,1)S(1)}, bf16[64,2048]{1,0:T(8,128)(2,1)S(1)}, u32[]{:S(2)}, u32[]{:S(2)}) collective-permute-start(bf16[64,2048]{1,0:T(8,128)(2,1)S(1)} %get-tuple-element.66), channel_id=1, source_target_pairs={{0,8},{4,12},{8,0},{12,4},{16,24},{20,28},{24,16},{28,20},{1,9},{5... | collective-permute-start | bytes 786440 | tf_op jit(solution)/shard_map/ppermute | solution.py:316
  77.4 13.8 %collective-permute-start.6 = (bf16[64,2048]{1,0:T(8,128)(2,1)S(1)}, bf16[64,2048]{1,0:T(8,128)(2,1)S(1)}, u32[]{:S(2)}, u32[]{:S(2)}) collective-permute-start(bf16[64,2048]{1,0:T(8,128)(2,1)S(1)} %get-tuple-element.66), channel_id=1, source_target_pairs={{0,16},{4,20},{8,24},{12,28},{16,0},{20,4},{24,8},{28,12},{1,17},{... | collective-permute-start | bytes 786440 | tf_op jit(solution)/shard_map/ppermute | solution.py:316
  91.2 25.3 %collective-permute-start.15 = (bf16[256,2048]{1,0:T(8,128)(2,1)S(1)}, bf16[256,2048]{1,0:T(8,128)(2,1)S(1)}, u32[]{:S(2)}, u32[]{:S(2)}) collective-permute-start(bf16[256,2048]{1,0:T(8,128)(2,1)S(1)} %collective-permute-done.refs_3_), channel_id=1, source_target_pairs={{0,2},{1,3},{2,0},{3,1},{4,6},{5,7},{6,4},{7,5},{8,10},{9,11},{10,... | collective-permute-start | bytes 3145736 | tf_op jit(solution)/shard_map/ppermute | solution.py:316
  92.7 12.2 %collective-permute-start.10 = (bf16[64,2048]{1,0:T(8,128)(2,1)S(1)}, bf16[64,2048]{1,0:T(8,128)(2,1)S(1)}, u32[]{:S(2)}, u32[]{:S(2)}) collective-permute-start(bf16[64,2048]{1,0:T(8,128)(2,1)S(1)} %collective-permute-done.6.refs_0_), channel_id=1, source_target_pairs={{0,8},{4,12},{8,0},{12,4},{16,24},{20,28},{24,16},{28,20},{1,9},{5... | collective-permute-start | bytes 786440 | tf_op jit(solution)/shard_map/ppermute | solution.py:316
  92.7 12.2 %collective-permute-start.9 = (bf16[64,2048]{1,0:T(8,128)(2,1)S(1)}, bf16[64,2048]{1,0:T(8,128)(2,1)S(1)}, u32[]{:S(2)}, u32[]{:S(2)}) collective-permute-start(bf16[64,2048]{1,0:T(8,128)(2,1)S(1)} %get-tuple-element.76), channel_id=1, source_target_pairs={{0,16},{4,20},{8,24},{12,28},{16,0},{20,4},{24,8},{28,12},{1,17},{... | collective-permute-start | bytes 786440 | tf_op jit(solution)/shard_map/ppermute | solution.py:316
  95.1 9.7 %collective-permute-start.7 = (bf16[64,2048]{1,0:T(8,128)(2,1)S(1)}, bf16[64,2048]{1,0:T(8,128)(2,1)S(1)}, u32[]{:S(2)}, u32[]{:S(2)}) collective-permute-start(bf16[64,2048]{1,0:T(8,128)(2,1)S(1)} %collective-permute-done.6.refs_0_), channel_id=1, source_target_pairs={{0,4},{4,0},{8,12},{12,8},{16,20},{20,16},{24,28},{28,24},{1,5},{5... | collective-permute-start | bytes 786440 | tf_op jit(solution)/shard_map/ppermute | solution.py:316
  95.7 9.7 %collective-permute-start.8 = (bf16[64,2048]{1,0:T(8,128)(2,1)S(1)}, bf16[64,2048]{1,0:T(8,128)(2,1)S(1)}, u32[]{:S(2)}, u32[]{:S(2)}) collective-permute-start(bf16[64,2048]{1,0:T(8,128)(2,1)S(1)} %collective-permute-done.5.refs_1_), channel_id=1, source_target_pairs={{0,4},{4,0},{8,12},{12,8},{16,20},{20,16},{24,28},{28,24},{1,5},{5... | collective-permute-start | bytes 786440 | tf_op jit(solution)/shard_map/ppermute | solution.py:316
  113.2 18.1 %collective-permute-start.18 = (bf16[256,2048]{1,0:T(8,128)(2,1)S(1)}, bf16[256,2048]{1,0:T(8,128)(2,1)S(1)}, u32[]{:S(2)}, u32[]{:S(2)}) collective-permute-start(bf16[256,2048]{1,0:T(8,128)(2,1)S(1)} %collective-permute-done.refs_3_), channel_id=1, source_target_pairs={{0,1},{1,0},{2,3},{3,2},{4,5},{5,4},{6,7},{7,6},{8,9},{9,8},{10,11... | collective-permute-start | bytes 3145736 | tf_op jit(solution)/shard_map/ppermute | solution.py:316
  116.5 14.8 %collective-permute-start.19 = (bf16[256,2048]{1,0:T(8,128)(2,1)S(1)}, bf16[256,2048]{1,0:T(8,128)(2,1)S(1)}, u32[]{:S(2)}, u32[]{:S(2)}) collective-permute-start(bf16[256,2048]{1,0:T(8,128)(2,1)S(1)} %collective-permute-done.15.refs_5_), channel_id=1, source_target_pairs={{0,1},{1,0},{2,3},{3,2},{4,5},{5,4},{6,7},{7,6},{8,9},{9,8},{10,11... | collective-permute-start | bytes 3145736 | tf_op jit(solution)/shard_map/ppermute | solution.py:316
  120.5 10.8 %collective-permute-start.16 = (bf16[128,1024]{1,0:T(8,128)(2,1)S(1)}, bf16[128,1024]{1,0:T(8,128)(2,1)S(1)}, u32[]{:S(2)}, u32[]{:S(2)}) collective-permute-start(bf16[128,1024]{1,0:T(8,128)(2,1)S(1)} %get-tuple-element.85), channel_id=1, source_target_pairs={{0,4},{4,0},{8,12},{12,8},{16,20},{20,16},{24,28},{28,24},{1,5},{5... | collective-permute-start | bytes 786440 | tf_op jit(solution)/shard_map/ppermute | solution.py:316
  128.6 11.2 %collective-permute-start.22 = (bf16[128,1024]{1,0:T(8,128)(2,1)S(1)}, bf16[128,1024]{1,0:T(8,128)(2,1)S(1)}, u32[]{:S(2)}, u32[]{:S(2)}) collective-permute-start(bf16[128,1024]{1,0:T(8,128)(2,1)S(1)} %get-tuple-element.96), channel_id=1, source_target_pairs={{0,4},{4,0},{8,12},{12,8},{16,20},{20,16},{24,28},{28,24},{1,5},{5... | collective-permute-start | bytes 786440 | tf_op jit(solution)/shard_map/ppermute | solution.py:316
  134.2 10.7 %collective-permute-start.24 = (bf16[64,2048]{1,0:T(8,128)(2,1)S(1)}, bf16[64,2048]{1,0:T(8,128)(2,1)S(1)}, u32[]{:S(2)}, u32[]{:S(2)}) collective-permute-start(bf16[64,2048]{1,0:T(8,128)(2,1)S(1)} %collective-permute-done.14.refs_0_), channel_id=1, source_target_pairs={{0,4},{4,0},{8,12},{12,8},{16,20},{20,16},{24,28},{28,24},{1,5},{5... | collective-permute-start | bytes 786440 | tf_op jit(solution)/shard_map/ppermute | solution.py:316
  135.0 11.9 %collective-permute-start.23 = (bf16[64,2048]{1,0:T(8,128)(2,1)S(1)}, bf16[64,2048]{1,0:T(8,128)(2,1)S(1)}, u32[]{:S(2)}, u32[]{:S(2)}) collective-permute-start(bf16[64,2048]{1,0:T(8,128)(2,1)S(1)} %get-tuple-element.93), channel_id=1, source_target_pairs={{0,8},{4,12},{8,0},{12,4},{16,24},{20,28},{24,16},{28,20},{1,9},{5... | collective-permute-start | bytes 786440 | tf_op jit(solution)/shard_map/ppermute | solution.py:316
  138.1 11.8 %collective-permute-start.21 = (bf16[64,2048]{1,0:T(8,128)(2,1)S(1)}, bf16[64,2048]{1,0:T(8,128)(2,1)S(1)}, u32[]{:S(2)}, u32[]{:S(2)}) collective-permute-start(bf16[64,2048]{1,0:T(8,128)(2,1)S(1)} %mlp_down.6), channel_id=1, source_target_pairs={{0,8},{4,12},{8,0},{12,4},{16,24},{20,28},{24,16},{28,20},{1,9},{5... | collective-permute-start | bytes 786440 | tf_op jit(solution)/shard_map/ppermute | solution.py:316
  141.8 22.5 %collective-permute-start.27 = (bf16[64,2048]{1,0:T(8,128)(2,1)S(1)}, bf16[64,2048]{1,0:T(8,128)(2,1)S(1)}, u32[]{:S(2)}, u32[]{:S(2)}) collective-permute-start(bf16[64,2048]{1,0:T(8,128)(2,1)S(1)} %get-tuple-element.101), channel_id=1, source_target_pairs={{0,8},{4,12},{8,0},{12,4},{16,24},{20,28},{24,16},{28,20},{1,9},{5... | collective-permute-start | bytes 786440 | tf_op jit(solution)/shard_map/ppermute | solution.py:316
  151.3 11.1 %collective-permute-start.25 = (bf16[128,1024]{1,0:T(8,128)(2,1)S(1)}, bf16[128,1024]{1,0:T(8,128)(2,1)S(1)}, u32[]{:S(2)}, u32[]{:S(2)}) collective-permute-start(bf16[128,1024]{1,0:T(8,128)(2,1)S(1)} %get-tuple-element.106), channel_id=1, source_target_pairs={{0,4},{4,0},{8,12},{12,8},{16,20},{20,16},{24,28},{28,24},{1,5},{5... | collective-permute-start | bytes 786440 | tf_op jit(solution)/shard_map/ppermute | solution.py:316
  152.1 18.6 %collective-permute-start.30 = (bf16[64,2048]{1,0:T(8,128)(2,1)S(1)}, bf16[64,2048]{1,0:T(8,128)(2,1)S(1)}, u32[]{:S(2)}, u32[]{:S(2)}) collective-permute-start(bf16[64,2048]{1,0:T(8,128)(2,1)S(1)} %add_convert_fusion.2), channel_id=1, source_target_pairs={{0,16},{4,20},{8,24},{12,28},{16,0},{20,4},{24,8},{28,12},{1,17},{... | collective-permute-start | bytes 786440 | tf_op jit(solution)/shard_map/ppermute | solution.py:316
  153.3 20.9 %collective-permute-start.29 = (bf16[64,2048]{1,0:T(8,128)(2,1)S(1)}, bf16[64,2048]{1,0:T(8,128)(2,1)S(1)}, u32[]{:S(2)}, u32[]{:S(2)}) collective-permute-start(bf16[64,2048]{1,0:T(8,128)(2,1)S(1)} %add_convert_fusion.3), channel_id=1, source_target_pairs={{0,16},{4,20},{8,24},{12,28},{16,0},{20,4},{24,8},{28,12},{1,17},{... | collective-permute-start | bytes 786440 | tf_op jit(solution)/shard_map/ppermute | solution.py:316
  157.1 17.2 %collective-permute-start.28 = (bf16[64,2048]{1,0:T(8,128)(2,1)S(1)}, bf16[64,2048]{1,0:T(8,128)(2,1)S(1)}, u32[]{:S(2)}, u32[]{:S(2)}) collective-permute-start(bf16[64,2048]{1,0:T(8,128)(2,1)S(1)} %mlp_down.8), channel_id=1, source_target_pairs={{0,8},{4,12},{8,0},{12,4},{16,24},{20,28},{24,16},{28,20},{1,9},{5... | collective-permute-start | bytes 786440 | tf_op jit(solution)/shard_map/ppermute | solution.py:316
  (32 other events, 276.8 us)
